TPU v7x, 128 devices: a whole 4x4x4 slice. The times are simulated.
128 devices in a mesh: seq: 16 (over y, z), expert: 8 (over x, core).
Axes of the slice: x: 4, y: 4, z: 4, core: 2. Of those that a mesh axis runs over, the one named last changes fastest.
Arguments:
- tokens: bfloat16 [8, 4096, 1152], P('expert', 'seq'), may hold values from -6 to 6
- expert_index: int32 [8, 4096, 1], P('expert', 'seq'), may hold values from 0 to 7; in each aligned block of 256 rows (0 to 255, 256 to 511, ..., all dimensions but the last counted through in order) at most 64 rows name the same one
- cotangent: bfloat16 [8, 4096, 1152], P('expert', 'seq'), may hold values from -6 to 6
- first_gain: float32 [1152], replicated, may hold values from 0.5 to 1.5
- in_weight: bfloat16 [1152, 4608], replicated, may hold values from -0.1875 to 0.1875
- conv_weight: float32 [4, 2304], replicated, may hold values from -3 to 3
- conv_bias: float32 [2304], replicated, may hold values from -3 to 3
- select_weight: bfloat16 [2304, 104], replicated, may hold values from -0.125 to 0.125
- step_weight: bfloat16 [72, 2304], replicated, may hold values from -0.75 to 0.75
- step_bias: float32 [2304], replicated, may hold values from -4 to -2.5
- decay_log: float32 [16, 2304], replicated, may hold values from -9 to 1
- skip_gain: float32 [2304], replicated, may hold values from 0.5 to 1.5
- out_weight: bfloat16 [2304, 1152], replicated, may hold values from -0.125 to 0.125
- second_gain: float32 [1152], replicated, may hold values from 0.5 to 1.5
- router_weight: bfloat16 [1152, 8], replicated, may hold values from -0.125 to 0.125
- expert_first: bfloat16 [8, 1152, 3072], P('expert'), may hold values from -0.1875 to 0.1875
- expert_second: bfloat16 [8, 3072, 1152], P('expert'), may hold values from -0.875 to 0.875
Outputs:
- mixed: bfloat16 [8, 4096, 1152], P('expert', 'seq')
- grad_tokens: float32 [8, 4096, 1152], P('expert', 'seq')
- grad_first_gain: float32 [1152], P(('seq', 'expert'))
- grad_in_weight: float32 [1152, 4608], P(None, ('seq', 'expert'))
- grad_conv_weight: float32 [4, 2304], P(None, ('seq', 'expert'))
- grad_conv_bias: float32 [2304], P(('seq', 'expert'))
- grad_select_weight: float32 [2304, 104], P(('seq', 'expert'))
- grad_step_weight: float32 [72, 2304], P(None, ('seq', 'expert'))
- grad_step_bias: float32 [2304], P(('seq', 'expert'))
- grad_decay_log: float32 [16, 2304], P(None, ('seq', 'expert'))
- grad_skip_gain: float32 [2304], P(('seq', 'expert'))
- grad_out_weight: float32 [2304, 1152], P(('seq', 'expert'))
- grad_second_gain: float32 [1152], P(('seq', 'expert'))
- grad_router_weight: float32 [1152, 8], P(('seq', 'expert'))
- grad_expert_first: float32 [8, 1152, 3072], P('expert', None, 'seq')
- grad_expert_second: float32 [8, 3072, 1152], P('expert', 'seq')
Inputs may be any that keep to these rules, and one draw needn't show every extreme that they name: `expert_index`: in each aligned block of 256 tokens of a sequence no expert is named more than 64 times, a bound that some block reaches.
All inputs are finite; a program needn't handle non-finite values.
Results may differ from a plain program's by a relative error of at most 0.038.
Values may be sent and summed in bfloat16 or wider, within the bound.
A program may use at most 256 MiB of HBM per device.

v0:
```python
import math

import jax
import jax.numpy as jnp
from jax import lax
from jax.sharding import PartitionSpec as P


def from_behind(block, axis, distance):
    devices = range(lax.axis_size(axis))
    route = [(i - distance, i) for i in devices if i - distance in devices]
    return lax.ppermute(block, axis, route)


def rms_norm(stream, norm_gain):
    return stream * lax.rsqrt(jnp.mean(stream * stream, axis=-1, keepdims=True) + 1e-05) * norm_gain


def conv_silu(padded, conv_weight, conv_bias):
    tap_count = conv_weight.shape[0]
    out_rows = padded.shape[0] - tap_count + 1
    summed = conv_bias[None, :]
    for offset in range(tap_count):
        summed = summed + conv_weight[offset][None, :] * padded[offset : offset + out_rows]
    return jax.nn.silu(summed)


def soft_step(step_raw, step_bias):
    return jax.nn.softplus(step_raw + step_bias)


def gate_mix(mixer_out, gate_input):
    return mixer_out * jax.nn.silu(gate_input)


def run_scan(step_size, input_map, output_map, conv_out, decay_log, carried):
    decay_rate = -jnp.exp(decay_log)
    row_count = step_size.shape[0]
    block_rows = math.gcd(row_count, 32)

    def advance(memory, item_now):
        step_now, input_now, output_now, value_now = item_now
        memory = (
            jnp.exp(step_now[None, :] * decay_rate) * memory
            + input_now[:, None] * (step_now * value_now)[None, :]
        )
        return (memory, jnp.sum(output_now[:, None] * memory, axis=0))

    def sweep(memory, block_items):
        return lax.scan(advance, memory, block_items, unroll=True)

    shaped = tuple(
        (
            array_now.reshape(row_count // block_rows, block_rows, array_now.shape[1])
            for array_now in (step_size, input_map, output_map, conv_out)
        )
    )
    last_state, outputs = lax.scan(jax.checkpoint(sweep), carried, shaped)
    return (outputs.reshape(row_count, outputs.shape[2]), last_state)


def decay_total(exponent, left_rows, right_rows, decay_rate):
    row_count = exponent.shape[0]
    block_rows = math.gcd(row_count, 32)

    def accumulate(summed, pieces):
        expo_block, left_block, right_block = pieces
        weights_block = jnp.exp(decay_rate[None, :, :] * expo_block[:, None, :])
        return (
            summed
            + jnp.sum(weights_block * left_block[:, :, None] * right_block[:, None, :], axis=0),
            None,
        )

    shaped = tuple(
        (
            array_now.reshape(row_count // block_rows, block_rows, array_now.shape[1])
            for array_now in (exponent, left_rows, right_rows)
        )
    )
    summed, unused = lax.scan(
        accumulate, jnp.zeros((left_rows.shape[1], exponent.shape[1]), jnp.float32), shaped
    )
    return summed


def local(
    tokens,
    expert_index,
    cotangent,
    first_gain,
    in_weight,
    conv_weight,
    conv_bias,
    select_weight,
    step_weight,
    step_bias,
    decay_log,
    skip_gain,
    out_weight,
    second_gain,
    router_weight,
    expert_first,
    expert_second,
):
    stream = tokens[0].astype(jnp.float32)
    routes = expert_index[0, :, 0]
    upstream = cotangent[0].astype(jnp.float32)
    row_count = stream.shape[0]
    model_width = stream.shape[1]
    inner_width = conv_bias.shape[0]
    rank_width = step_weight.shape[0]
    state_width = decay_log.shape[0]
    tap_count = conv_weight.shape[0]
    expert_count = router_weight.shape[1]
    capacity = 2 * row_count // expert_count
    chain_length = lax.axis_size("seq")
    normed_first, first_back = jax.vjp(rms_norm, stream, first_gain)
    normed_in = normed_first.astype(jnp.bfloat16)
    projected = jnp.dot(normed_in, in_weight, preferred_element_type=jnp.float32)
    conv_input = projected[:, :inner_width]
    gate_input = projected[:, inner_width:]
    tail_rows = from_behind(conv_input[row_count - tap_count + 1 :], "seq", 1)
    padded = jnp.concatenate([tail_rows, conv_input], axis=0)
    conv_out, conv_pullback = jax.vjp(conv_silu, padded, conv_weight, conv_bias)
    conv_low = conv_out.astype(jnp.bfloat16)
    selection = jnp.dot(conv_low, select_weight, preferred_element_type=jnp.float32)
    step_low = selection[:, :rank_width].astype(jnp.bfloat16)
    input_map = selection[:, rank_width : rank_width + state_width]
    output_map = selection[:, rank_width + state_width :]
    step_raw = jnp.dot(step_low, step_weight, preferred_element_type=jnp.float32)
    step_size, step_pullback = jax.vjp(soft_step, step_raw, step_bias)
    decay_rate = -jnp.exp(decay_log)
    elapsed = jnp.cumsum(step_size, axis=0)
    span_total = elapsed[row_count - 1]
    through = jnp.exp(decay_rate * span_total[None, :])
    fresh = decay_total(span_total[None, :] - elapsed, input_map, step_size * conv_out, decay_rate)

    def pass_forward(turn, carried):
        return from_behind((through * carried + fresh).astype(jnp.bfloat16), "seq", 1).astype(
            jnp.float32
        )

    entering = lax.fori_loop(0, chain_length - 1, pass_forward, jnp.zeros_like(fresh))
    (scanned, leaving), scan_pullback = jax.vjp(
        run_scan, step_size, input_map, output_map, conv_out, decay_log, entering
    )
    mixer_out = scanned + skip_gain * conv_out
    gated_full, gated_pullback = jax.vjp(gate_mix, mixer_out, gate_input)
    gated = gated_full.astype(jnp.bfloat16)
    middle = stream + jnp.dot(gated, out_weight, preferred_element_type=jnp.float32)
    normed_second, second_back = jax.vjp(rms_norm, middle, second_gain)
    normed_mid = normed_second.astype(jnp.bfloat16)
    logits = jnp.dot(normed_mid, router_weight, preferred_element_type=jnp.float32)
    router_probs = jax.nn.softmax(logits, axis=-1)
    picks = (routes[:, None] == jnp.arange(expert_count, dtype=jnp.int32)[None, :]).astype(
        jnp.int32
    )
    chosen = picks.astype(jnp.float32)
    gate_value = jnp.sum(router_probs * chosen, axis=1)
    slot_rank = jnp.sum((jnp.cumsum(picks, axis=0) - 1) * picks, axis=1)
    slot_index = routes * capacity + slot_rank
    outgoing = (
        jnp.zeros((expert_count * capacity, model_width), jnp.bfloat16)
        .at[slot_index]
        .set(normed_mid)
    )
    outgoing = outgoing.reshape(expert_count, capacity, model_width)
    first_matrix = expert_first[0]
    second_matrix = expert_second[0]
    received = lax.all_to_all(outgoing, "expert", split_axis=0, concat_axis=0, tiled=True)
    hidden_pre = jnp.einsum(
        "scd,df->scf", received, first_matrix, preferred_element_type=jnp.float32
    )
    activated = jax.nn.gelu(hidden_pre).astype(jnp.bfloat16)
    result = jnp.einsum(
        "scf,fd->scd", activated, second_matrix, preferred_element_type=jnp.float32
    ).astype(jnp.bfloat16)
    back_home = lax.all_to_all(result, "expert", split_axis=0, concat_axis=0, tiled=True)
    returned, received, hidden_pre, activated = (back_home, received, hidden_pre, activated)
    expert_value = returned.reshape(expert_count * capacity, model_width)[slot_index].astype(
        jnp.float32
    )
    mixed = middle + gate_value[:, None] * expert_value
    grad_gate = jnp.sum(upstream * expert_value, axis=1)
    grad_value = (gate_value[:, None] * upstream).astype(jnp.bfloat16)
    grad_outgoing = (
        jnp.zeros((expert_count * capacity, model_width), jnp.bfloat16)
        .at[slot_index]
        .set(grad_value)
    )
    grad_outgoing = grad_outgoing.reshape(expert_count, capacity, model_width)
    grad_received = lax.all_to_all(grad_outgoing, "expert", split_axis=0, concat_axis=0, tiled=True)
    grad_act = jnp.einsum(
        "scd,fd->scf", grad_received, second_matrix, preferred_element_type=jnp.float32
    )
    grad_hidden = jax.vjp(jax.nn.gelu, hidden_pre)[1](grad_act)[0].astype(jnp.bfloat16)
    grad_first_expert = jnp.einsum(
        "scd,scf->df", received, grad_hidden, preferred_element_type=jnp.float32
    )
    grad_second_expert = jnp.einsum(
        "scf,scd->fd", activated, grad_received, preferred_element_type=jnp.float32
    )
    grad_sent = jnp.einsum(
        "scf,df->scd", grad_hidden, first_matrix, preferred_element_type=jnp.float32
    ).astype(jnp.bfloat16)
    grad_back_home = lax.all_to_all(grad_sent, "expert", split_axis=0, concat_axis=0, tiled=True)
    grad_mid_expert = grad_back_home.reshape(expert_count * capacity, model_width)[
        slot_index
    ].astype(jnp.float32)
    grad_logits = (grad_gate[:, None] * gate_value[:, None] * (chosen - router_probs)).astype(
        jnp.bfloat16
    )
    grad_router = jnp.einsum(
        "td,tx->dx", normed_mid, grad_logits, preferred_element_type=jnp.float32
    )
    grad_mid = (
        jnp.einsum("tx,dx->td", grad_logits, router_weight, preferred_element_type=jnp.float32)
        + grad_mid_expert
    )
    grad_middle_norm, grad_second_gain = second_back(grad_mid)
    grad_middle = upstream + grad_middle_norm
    middle_low = grad_middle.astype(jnp.bfloat16)
    grad_out_weight = jnp.einsum("te,td->ed", gated, middle_low, preferred_element_type=jnp.float32)
    grad_gated = jnp.einsum("td,ed->te", middle_low, out_weight, preferred_element_type=jnp.float32)
    grad_mixer, grad_gate_input = gated_pullback(grad_gated)
    grad_skip = jnp.sum(grad_mixer * conv_out, axis=0)
    local_back = decay_total(elapsed, output_map, grad_mixer, decay_rate)

    def pass_backward(turn, carried):
        return from_behind((through * carried + local_back).astype(jnp.bfloat16), "seq", -1).astype(
            jnp.float32
        )

    leaving_grad = lax.fori_loop(0, chain_length - 1, pass_backward, jnp.zeros_like(local_back))
    grad_step, grad_input_map, grad_output_map, grad_conv_scan, grad_decay_log, unused_entry = (
        scan_pullback((grad_mixer, leaving_grad))
    )
    grad_step_raw, grad_step_bias = step_pullback(grad_step)
    step_raw_low = grad_step_raw.astype(jnp.bfloat16)
    grad_step_weight = jnp.einsum(
        "tr,te->re", step_low, step_raw_low, preferred_element_type=jnp.float32
    )
    grad_step_low = jnp.einsum(
        "te,re->tr", step_raw_low, step_weight, preferred_element_type=jnp.float32
    )
    grad_selection = jnp.concatenate(
        [grad_step_low, grad_input_map, grad_output_map], axis=1
    ).astype(jnp.bfloat16)
    grad_select_weight = jnp.einsum(
        "te,tk->ek", conv_low, grad_selection, preferred_element_type=jnp.float32
    )
    grad_conv_out = (
        jnp.einsum("tk,ek->te", grad_selection, select_weight, preferred_element_type=jnp.float32)
        + grad_conv_scan
        + skip_gain * grad_mixer
    )
    grad_padded, grad_conv_weight, grad_conv_bias = conv_pullback(grad_conv_out)
    spill = from_behind(grad_padded[: tap_count - 1], "seq", -1)
    grad_conv_input = grad_padded[tap_count - 1 :] + jnp.concatenate(
        [jnp.zeros((row_count - tap_count + 1, inner_width), jnp.float32), spill], axis=0
    )
    grad_projected = jnp.concatenate([grad_conv_input, grad_gate_input], axis=1).astype(
        jnp.bfloat16
    )
    grad_in_weight = jnp.einsum(
        "td,tk->dk", normed_in, grad_projected, preferred_element_type=jnp.float32
    )
    grad_normed = jnp.einsum(
        "tk,dk->td", grad_projected, in_weight, preferred_element_type=jnp.float32
    )
    grad_stream_norm, grad_first_gain = first_back(grad_normed)
    grad_tokens = grad_middle + grad_stream_norm
    shares = (
        lax.psum_scatter(grad_first_gain, ("seq", "expert"), scatter_dimension=0, tiled=True),
        lax.psum_scatter(grad_in_weight, ("seq", "expert"), scatter_dimension=1, tiled=True),
        lax.psum_scatter(grad_conv_weight, ("seq", "expert"), scatter_dimension=1, tiled=True),
        lax.psum_scatter(grad_conv_bias, ("seq", "expert"), scatter_dimension=0, tiled=True),
        lax.psum_scatter(grad_select_weight, ("seq", "expert"), scatter_dimension=0, tiled=True),
        lax.psum_scatter(grad_step_weight, ("seq", "expert"), scatter_dimension=1, tiled=True),
        lax.psum_scatter(grad_step_bias, ("seq", "expert"), scatter_dimension=0, tiled=True),
        lax.psum_scatter(grad_decay_log, ("seq", "expert"), scatter_dimension=1, tiled=True),
        lax.psum_scatter(grad_skip, ("seq", "expert"), scatter_dimension=0, tiled=True),
        lax.psum_scatter(grad_out_weight, ("seq", "expert"), scatter_dimension=0, tiled=True),
        lax.psum_scatter(grad_second_gain, ("seq", "expert"), scatter_dimension=0, tiled=True),
        lax.psum_scatter(grad_router, ("seq", "expert"), scatter_dimension=0, tiled=True),
    )
    expert_shares = (
        lax.psum_scatter(
            grad_first_expert[None].astype(jnp.bfloat16), "seq", scatter_dimension=2, tiled=True
        ).astype(jnp.float32),
        lax.psum_scatter(
            grad_second_expert[None].astype(jnp.bfloat16), "seq", scatter_dimension=1, tiled=True
        ).astype(jnp.float32),
    )
    return (
        mixed.astype(jnp.bfloat16)[None],
        grad_tokens[None],
        shares[0],
        shares[1],
        shares[2],
        shares[3],
        shares[4],
        shares[5],
        shares[6],
        shares[7],
        shares[8],
        shares[9],
        shares[10],
        shares[11],
        expert_shares[0],
        expert_shares[1],
    )


def solution(mesh):
    return jax.shard_map(
        local,
        mesh=mesh,
        in_specs=(
            P("expert", "seq", None),
            P("expert", "seq", None),
            P("expert", "seq", None),
            P(),
            P(),
            P(),
            P(),
            P(),
            P(),
            P(),
            P(),
            P(),
            P(),
            P(),
            P(),
            P("expert", None, None),
            P("expert", None, None),
        ),
        out_specs=(
            P("expert", "seq", None),
            P("expert", "seq", None),
            P(("seq", "expert")),
            P(None, ("seq", "expert")),
            P(None, ("seq", "expert")),
            P(("seq", "expert")),
            P(("seq", "expert"), None),
            P(None, ("seq", "expert")),
            P(("seq", "expert")),
            P(None, ("seq", "expert")),
            P(("seq", "expert")),
            P(("seq", "expert"), None),
            P(("seq", "expert")),
            P(("seq", "expert"), None),
            P("expert", None, "seq"),
            P("expert", "seq", None),
        ),
        check_vma=False,
    )
```

profile of v0, /device:TPU:1, one launch (start us, length us, event | category | flops | bytes accessed | tf_op | source)
XLA Modules:
  0.0 2157.8 jit_solution(13245825787652827784)
XLA Ops:
  50.9 45.5 %while.84 = (s32[]{:T(128)}, f32[16,2304]{1,0:T(8,128)S(1)}, f32[16,2304]{1,0:T(8,128)S(1)}, f32[8,32,2304]{2,1,0:T(8,128)}, f32[8,32,16]{1,0,2:T(8,128)S(1)}, /*index=5*/f32[8,32,2304]{2,1,0:T(8,128)}, s32[]{:T(128)}, s32[]{:T(128)}) while((s32[]{:T(128)}, f32[16,2304]{1,0:T(8,128)S(1)}, f32[16,2304]{1,0:T(8,128)S(1)}, ...), condition=%wide.region_5.6_spmd.clone, body=%wide.region_3.5_spmd.clone.sunk | while | flops 4755459 | bytes 2517103 | solution.py:81
  97.2 113.5 %while.85 = (s32[]{:T(128)}, f32[16,2304]{1,0:T(8,128)S(1)}, f32[16,2304]{1,0:T(8,128)S(1)}, f32[16,2304]{1,0:T(8,128)S(1)}, s32[]{:T(128)}, /*index=5*/s32[]{:T(128)}) while((s32[]{:T(128)}, f32[16,2304]{1,0:T(8,128)S(1)}, f32[16,2304]{1,0:T(8,128)S(1)}, f32[16,2304]{1,0:T(8,128)S(1)}, s32[]{:T(128)}, /*index=5*/s32[]{:T(128)}) %tuple.803), condition=%wide.region_7.8_spmd.clone, body=%wide.region_6.7_spmd.clone.sunk | while | flops 184323 | bytes 1032311 | solution.py:144
  212.3 291.6 %while.83 = (s32[]{:T(128)}, f32[16,2304]{1,0:T(8,128)S(1)}, f32[8,32,2304]{2,1,0:T(8,128)}, f32[8,16,2304]{2,1,0:T(8,128)}, f32[8,32,2304]{2,1,0:T(8,128)}, /*i...) while((s32[]{:T(128)}, f32[16,2304]{1,0:T(8,128)S(1)}, ...), condition=%wide.region_41.42_spmd, body=%wide.region_8.41_spmd.sunk | while | flops 10616865 | bytes 9902137 | solution.py:58
  514.4 21.6 %all-to-all-start = ((bf16[8,64,1152]{2,1,0:T(8,128)(2,1)}), bf16[8,64,1152]{2,1,0:T(8,128)(2,1)}, u32[]{:S(2)}, u32[]{:S(2)}) async-start(bf16[8,64,1152]{2,1,0:T(8,128)(2,1)} %bitcast.695), calls=%async_computation | async-start | bytes 2359296 | tf_op jit(solution)/shard_map/all_to_all | solution.py:171
  542.0 10.6 all-to-all-done
  557.6 10.2 fusion.142
  574.2 10.7 fusion.150
  586.5 8.3 fusion.154
  600.1 11.2 fusion.157
  625.6 12.7 all-to-all-done.1
  656.4 40.0 %while.86 = (s32[]{:T(128)}, f32[16,2304]{1,0:T(8,128)S(1)}, f32[16,2304]{1,0:T(8,128)S(1)}, f32[8,32,2304]{2,1,0:T(8,128)}, f32[8,32,16]{1,0,2:T(8,128)}, /*index=5*/f32[8,32,2304]{2,1,0:T(8,128)}, s32[]{:T(128)}, s32[]{:T(128)}) while((s32[]{:T(128)}, f32[16,2304]{1,0:T(8,128)S(1)}, f32[16,2304]{1,0:T(8,128)S(1)}, ...), condition=%wide.region_55.56_spmd.clone, body=%wide.region_53.55_spmd.clone.sunk | while | flops 4755459 | bytes 2517103 | solution.py:81
  696.4 135.3 %while.87 = (s32[]{:T(128)}, f32[16,2304]{1,0:T(8,128)}, f32[16,2304]{1,0:T(8,128)S(1)}, f32[16,2304]{1,0:T(8,128)S(1)}, s32[]{:T(128)}, /*index=5*/s32[]{:T(128)}) while((s32[]{:T(128)}, f32[16,2304]{1,0:T(8,128)}, f32[16,2304]{1,0:T(8,128)S(1)}, f32[16,2304]{1,0:T(8,128)S(1)}, s32[]{:T(128)}, /*index=5*/s32[]{:T(128)}) %tuple.833), condition=%wide.region_57.58_spmd.clone, body=%wide.region_56.57_spmd.clone.sunk | while | flops 184323 | bytes 1032311 | solution.py:235
  836.3 587.5 %while.88 = (s32[]{:T(128)}, f32[16,2304]{1,0:T(8,128)}, f32[16,2304]{1,0:T(8,128)}, f32[8,32,2304]{2,1,0:T(8,128)}, bf16[8,32,16]{2,1,0:T(8,128)(2,1)}, /*index...) while((s32[]{:T(128)}, f32[16,2304]{1,0:T(8,128)}, ...), condition=%wide.region_187.188_spmd.clone, body=%wide.region_58.187_spmd.clone.sunk | while | flops 38226948 | bytes 34291968 | solution.py:58
  1461.5 8.9 fusion.134
  1470.4 30.2 %copy.90 = bf16[1,1152,3072]{1,0,2:T(2,128)(2,1)} copy(bf16[1,1152,3072]{2,1,0:T(8,128)(2,1)} %fusion.134) | data formatting | bytes 14155776
  1500.7 9.1 copy.98
  1509.8 10.8 fusion.135
  1521.9 9.1 fusion.179
  1531.0 388.9 %fusion = f32[1152,48]{0,1:T(8,128)S(1)} fusion(f32[1152,4608]{0,1:T(8,128)} %fusion.179), kind=kCustom, calls=%all-reduce-scatter | all-reduce-scatter fusion | flops 7077889 | bytes 21454848
  1927.1 12.2 collective-permute-done.35
  1968.3 12.7 collective-permute-start.22
  1981.0 8.6 collective-permute-start.21
  2028.4 16.4 collective-permute-start.12
  2083.2 54.1 %concatenate.61 = f32[1152,1572]{0,1:T(8,128)} concatenate(f32[1152,36]{0,1:T(8,128)} %collective-permute-done.35, f32[1152,48]{0,1:T(8,128)S(1)} %collective-permute-done.34, f32[1152,48]{0,1:T(8,128)S(1)} %collective-permute-done.33, f32[1152,48]{0,1:T(8,128)S(1)} %collective-permute-done.32, f32[1152,48]{0,1:T(8,128)S(1)} %collective-permute-done.31, f32[1152,48]{0,1:T(8,128)} %copy-done.152, ...), dimensions={1} | concatenate | bytes 14487552
  (3909 shorter events, 1476.7 us)
Async XLA Ops:
  514.4 38.2 %all-to-all-start = ((bf16[8,64,1152]{2,1,0:T(8,128)(2,1)}), bf16[8,64,1152]{2,1,0:T(8,128)(2,1)}, u32[]{:S(2)}, u32[]{:S(2)}) async-start(bf16[8,64,1152]{2,1,0:T(8,128)(2,1)} %bitcast.695), calls=%async_computation | async-start | bytes 2359296 | tf_op jit(solution)/shard_map/all_to_all | solution.py:171
  594.9 21.8 %all-to-all-start.3 = ((bf16[8,64,1152]{2,1,0:T(8,128)(2,1)}), bf16[8,64,1152]{2,1,0:T(8,128)(2,1)}, u32[]{:S(2)}, u32[]{:S(2)}) async-start(bf16[8,64,1152]{2,1,0:T(8,128)(2,1)} %fusion.154), calls=%async_computation.3 | async-start | bytes 2359296 | tf_op jit(solution)/shard_map/all_to_all | solution.py:207
  621.7 1431.8 %all-reduce.27.cloned.1.call-start = ((), (), s32[]{:S(2)}) async-start(), calls=%async_computation.8 | async-start | bytes 253952
  1459.5 679.4 %all-reduce.29.cloned.1.call-start = ((), (), s32[]{:S(2)}) async-start(), calls=%async_computation.9 | async-start | bytes 26247168
  1461.2 683.3 %reduce-scatter.12.cloned.1.call-start = ((), (), s32[]{:S(2)}) async-start(), calls=%async_computation.7 | async-start | bytes 7520256
  1509.8 638.1 %reduce-scatter.10.cloned.1.call-start = ((), (), s32[]{:S(2)}) async-start(), calls=%async_computation.6 | async-start | bytes 7520256 | tf_op jit(solution)/shard_map/reduce_scatter | solution.py:292
  1924.5 23.6 %collective-permute-start.32 = (f32[1152,48]{0,1:T(8,128)S(1)}, f32[1152,48]{0,1:T(8,128)S(1)}, u32[]{:S(2)}, u32[]{:S(2)}) collective-permute-start(f32[1152,48]{0,1:T(8,128)S(1)} %fusion), channel_id=1, source_target_pairs={{0,29},{1,30},{2,31},{3,32},{4,33},{5,34},{6,35},{7,36},{8,37},{9,... | collective-permute-start | bytes 663560
  1925.8 23.5 %collective-permute-start.31 = (f32[1152,48]{0,1:T(8,128)S(1)}, f32[1152,48]{0,1:T(8,128)S(1)}, u32[]{:S(2)}, u32[]{:S(2)}) collective-permute-start(f32[1152,48]{0,1:T(8,128)S(1)} %fusion), channel_id=1, source_target_pairs={{0,28},{1,29},{2,30},{3,31},{4,32},{5,33},{6,34},{7,35},{8,36},{9,... | collective-permute-start | bytes 663560
  1941.9 23.5 %collective-permute-start.28 = (f32[1152,48]{0,1:T(8,128)S(1)}, f32[1152,48]{0,1:T(8,128)S(1)}, u32[]{:S(2)}, u32[]{:S(2)}) collective-permute-start(f32[1152,48]{0,1:T(8,128)S(1)} %fusion), channel_id=1, source_target_pairs={{0,25},{1,26},{2,27},{3,28},{4,29},{5,30},{6,31},{7,32},{8,33},{9,... | collective-permute-start | bytes 663560
  1949.4 31.6 %collective-permute-start.26 = (f32[1152,48]{0,1:T(8,128)S(1)}, f32[1152,48]{0,1:T(8,128)S(1)}, u32[]{:S(2)}, u32[]{:S(2)}) collective-permute-start(f32[1152,48]{0,1:T(8,128)S(1)} %fusion), channel_id=1, source_target_pairs={{0,23},{1,24},{2,25},{3,26},{4,27},{5,28},{6,29},{7,30},{8,31},{9,... | collective-permute-start | bytes 663560
  1954.3 35.3 %collective-permute-start.25 = (f32[1152,48]{0,1:T(8,128)S(1)}, f32[1152,48]{0,1:T(8,128)S(1)}, u32[]{:S(2)}, u32[]{:S(2)}) collective-permute-start(f32[1152,48]{0,1:T(8,128)S(1)} %fusion), channel_id=1, source_target_pairs={{0,22},{1,23},{2,24},{3,25},{4,26},{5,27},{6,28},{7,29},{8,30},{9,... | collective-permute-start | bytes 663560
  1961.9 32.8 %collective-permute-start.24 = (f32[1152,48]{0,1:T(8,128)S(1)}, f32[1152,48]{0,1:T(8,128)S(1)}, u32[]{:S(2)}, u32[]{:S(2)}) collective-permute-start(f32[1152,48]{0,1:T(8,128)S(1)} %fusion), channel_id=1, source_target_pairs={{0,21},{1,22},{2,23},{3,24},{4,25},{5,26},{6,27},{7,28},{8,29},{9,... | collective-permute-start | bytes 663560
  1965.4 34.7 %collective-permute-start.23 = (f32[1152,48]{0,1:T(8,128)S(1)}, f32[1152,48]{0,1:T(8,128)}, u32[]{:S(2)}, u32[]{:S(2)}) collective-permute-start(f32[1152,48]{0,1:T(8,128)S(1)} %fusion), channel_id=1, source_target_pairs={{0,20},{1,21},{2,22},{3,23},{4,24},{5,25},{6,26},{7,27},{8,28},{9,... | collective-permute-start | bytes 663560
  1968.3 34.7 %collective-permute-start.22 = (f32[1152,48]{0,1:T(8,128)S(1)}, f32[1152,48]{0,1:T(8,128)}, u32[]{:S(2)}, u32[]{:S(2)}) collective-permute-start(f32[1152,48]{0,1:T(8,128)S(1)} %fusion), channel_id=1, source_target_pairs={{0,19},{1,20},{2,21},{3,22},{4,23},{5,24},{6,25},{7,26},{8,27},{9,... | collective-permute-start | bytes 663560
  1981.0 23.3 %collective-permute-start.21 = (f32[1152,48]{0,1:T(8,128)S(1)}, f32[1152,48]{0,1:T(8,128)}, u32[]{:S(2)}, u32[]{:S(2)}) collective-permute-start(f32[1152,48]{0,1:T(8,128)S(1)} %fusion), channel_id=1, source_target_pairs={{0,18},{1,19},{2,20},{3,21},{4,22},{5,23},{6,24},{7,25},{8,26},{9,... | collective-permute-start | bytes 663560
  1989.6 22.7 %collective-permute-start.20 = (f32[1152,48]{0,1:T(8,128)S(1)}, f32[1152,48]{0,1:T(8,128)}, u32[]{:S(2)}, u32[]{:S(2)}) collective-permute-start(f32[1152,48]{0,1:T(8,128)S(1)} %fusion), channel_id=1, source_target_pairs={{0,17},{1,18},{2,19},{3,20},{4,21},{5,22},{6,23},{7,24},{8,25},{9,... | collective-permute-start | bytes 663560
  2000.1 24.4 %collective-permute-start.18 = (f32[1152,48]{0,1:T(8,128)S(1)}, f32[1152,48]{0,1:T(8,128)S(1)}, u32[]{:S(2)}, u32[]{:S(2)}) collective-permute-start(f32[1152,48]{0,1:T(8,128)S(1)} %fusion), channel_id=1, source_target_pairs={{0,15},{1,16},{2,17},{3,18},{4,19},{5,20},{6,21},{7,22},{8,23},{9,... | collective-permute-start | bytes 663560
  2003.0 25.3 %collective-permute-start.17 = (f32[1152,48]{0,1:T(8,128)S(1)}, f32[1152,48]{0,1:T(8,128)S(1)}, u32[]{:S(2)}, u32[]{:S(2)}) collective-permute-start(f32[1152,48]{0,1:T(8,128)S(1)} %fusion), channel_id=1, source_target_pairs={{0,14},{1,15},{2,16},{3,17},{4,18},{5,19},{6,20},{7,21},{8,22},{9,... | collective-permute-start | bytes 663560
  2004.4 40.5 %collective-permute-start.16 = (f32[1152,48]{0,1:T(8,128)S(1)}, f32[1152,48]{0,1:T(8,128)S(1)}, u32[]{:S(2)}, u32[]{:S(2)}) collective-permute-start(f32[1152,48]{0,1:T(8,128)S(1)} %fusion), channel_id=1, source_target_pairs={{0,13},{1,14},{2,15},{3,16},{4,17},{5,18},{6,19},{7,20},{8,21},{9,... | collective-permute-start | bytes 663560
  2012.3 34.5 %collective-permute-start.15 = (f32[1152,48]{0,1:T(8,128)S(1)}, f32[1152,48]{0,1:T(8,128)S(1)}, u32[]{:S(2)}, u32[]{:S(2)}) collective-permute-start(f32[1152,48]{0,1:T(8,128)S(1)} %fusion), channel_id=1, source_target_pairs={{0,12},{1,13},{2,14},{3,15},{4,16},{5,17},{6,18},{7,19},{8,20},{9,... | collective-permute-start | bytes 663560
  2014.9 34.0 %collective-permute-start.14 = (f32[1152,48]{0,1:T(8,128)S(1)}, f32[1152,48]{0,1:T(8,128)S(1)}, u32[]{:S(2)}, u32[]{:S(2)}) collective-permute-start(f32[1152,48]{0,1:T(8,128)S(1)} %fusion), channel_id=1, source_target_pairs={{0,11},{1,12},{2,13},{3,14},{4,15},{5,16},{6,17},{7,18},{8,19},{9,... | collective-permute-start | bytes 663560
  2024.5 35.3 %collective-permute-start.13 = (f32[1152,48]{0,1:T(8,128)S(1)}, f32[1152,48]{0,1:T(8,128)}, u32[]{:S(2)}, u32[]{:S(2)}) collective-permute-start(f32[1152,48]{0,1:T(8,128)S(1)} %fusion), channel_id=1, source_target_pairs={{0,10},{1,11},{2,12},{3,13},{4,14},{5,15},{6,16},{7,17},{8,18},{9,... | collective-permute-start | bytes 663560
  2028.4 33.8 %collective-permute-start.12 = (f32[1152,48]{0,1:T(8,128)S(1)}, f32[1152,48]{0,1:T(8,128)}, u32[]{:S(2)}, u32[]{:S(2)}) collective-permute-start(f32[1152,48]{0,1:T(8,128)S(1)} %fusion), channel_id=1, source_target_pairs={{0,9},{1,10},{2,11},{3,12},{4,13},{5,14},{6,15},{7,16},{8,17},{9,1... | collective-permute-start | bytes 663560
  2046.8 21.9 %collective-permute-start.10 = (f32[1152,48]{0,1:T(8,128)S(1)}, f32[1152,48]{0,1:T(8,128)}, u32[]{:S(2)}, u32[]{:S(2)}) collective-permute-start(f32[1152,48]{0,1:T(8,128)S(1)} %fusion), channel_id=1, source_target_pairs={{0,7},{1,8},{2,9},{3,10},{4,11},{5,12},{6,13},{7,14},{8,15},{9,16}... | collective-permute-start | bytes 663560
  (1276 other events, 13463.5 us)
Sparse Core Ops, SparseCore 0:
  1459.7 192.2 all-reduce.26
  1658.6 250.4 all-reduce.28
Sparse Core Ops, SparseCore 1:
  1509.9 135.9 reduce-scatter.11
  1649.2 147.8 reduce-scatter.9
where the time goes:
time: 2200 us; the launch traced here: 2160 us
  local copies, waits for them, and re-layouts  677 us (31%)
  other arithmetic  500 us (23%)
  blocking collectives  389 us (18%)
  starting transfers between devices  268 us (12%)
  waiting for transfers between devices  175 us (8%)
  matrix products  114 us (5%)
    unnamed x1, blocking collectives  389 us
    concatenate x40, local copies, waits for them, and re-layouts, sweep(): return lax.scan(advance, memory, block_items, unroll=True)  145 us
    broadcast_in_dim x256, local copies, waits for them, and re-layouts, sweep(): return lax.scan(advance, memory, block_items, unroll=True)  130 us
    unnamed x188, local copies, waits for them, and re-layouts  125 us
    reduce_sum x136, other arithmetic, advance(): return (memory, jnp.sum(output_now[:, None] * memory, axis=0))  120 us
    unnamed x35, starting transfers between devices  119 us
    ppermute x32, starting transfers between devices, from_behind(): return lax.ppermute(block, axis, route)  112 us
    ppermute x32, waiting for transfers between devices, from_behind(): return lax.ppermute(block, axis, route)  107 us
  transfers between devices with their start and end apart: 72, of which 40 were waited for; matrix products, arithmetic and copies ran while one was open for 27% of the time, Pallas kernels for 0%

commit v1 on v0

v1 whole, which is shorter than its diff:
```python
import functools
import math

import jax
import jax.numpy as jnp
from jax import lax
from jax.experimental import pallas as pl
from jax.experimental.pallas import tpu as pltpu
from jax.sharding import PartitionSpec as P

LANES = 128
SEGS = 8
LOG2E = math.log2(math.e)


def fill_maps(sel_ref, wide_ref, steps, column, states):
    def fill(j, unused):
        rows = sel_ref[pl.ds(pl.multiple_of(j * SEGS, SEGS), SEGS), :]
        for n in range(states):
            wide_ref[j * states + n] = jnp.broadcast_to(
                rows[:, column + n : column + n + 1], (SEGS, LANES)
            )
        return unused

    lax.fori_loop(0, steps, fill, 0)


def segment_prefix(value, span, rate, later):
    place = lax.broadcasted_iota(jnp.int32, (SEGS, LANES), 0)
    hop = 1
    while hop < SEGS:
        turn = SEGS - hop if later else hop
        has = (place < SEGS - hop) if later else (place >= hop)
        before = jnp.where(has, pltpu.roll(value, turn, 0), 0.0)
        value = value + jnp.exp2(rate * span) * before
        span = span + jnp.where(has, pltpu.roll(span, turn, 0), 0.0)
        hop *= 2
    return value


def span_prefix(span, later):
    place = lax.broadcasted_iota(jnp.int32, (SEGS, LANES), 0)
    hop = 1
    while hop < SEGS:
        turn = SEGS - hop if later else hop
        has = (place < SEGS - hop) if later else (place >= hop)
        span = span + jnp.where(has, pltpu.roll(span, turn, 0), 0.0)
        hop *= 2
    return span


def rates_of(log_ref, lanes, states):
    return [
        jnp.broadcast_to(-LOG2E * jnp.exp(log_ref[n : n + 1, lanes]), (SEGS, LANES))
        for n in range(states)
    ]


def summary_kernel(later, column, step_ref, other_ref, sel_ref, log_ref, part_ref, span_ref, msg_ref, wide):
    rows, width = step_ref.shape
    steps, states = rows // SEGS, log_ref.shape[0]
    fill_maps(sel_ref, wide, steps, column, states)

    def block(eb, unused):
        lanes = pl.ds(pl.multiple_of(eb * LANES, LANES), LANES)
        rate = rates_of(log_ref, lanes, states)

        def advance(i, carry):
            span, memory = carry
            j = steps - 1 - i if later else i
            here = pl.ds(pl.multiple_of(j * SEGS, SEGS), SEGS)
            step = step_ref[here, lanes]
            other = other_ref[here, lanes]
            if not later:
                other = step * other
            new = []
            for n in range(states):
                decay = jnp.exp2(step * rate[n])
                fresh = wide[j * states + n] * other
                if later:
                    new.append(decay * (memory[n] + fresh))
                else:
                    new.append(decay * memory[n] + fresh)
            return span + step, tuple(new)

        zero = jnp.zeros((SEGS, LANES), jnp.float32)
        span, memory = lax.fori_loop(0, steps, advance, (zero, (zero,) * states), unroll=2)
        total = span_prefix(span, later)
        span_ref[:, lanes] = total
        end = 0 if later else SEGS - 1
        for n in range(states):
            value = segment_prefix(memory[n], span, rate[n], later)
            part_ref[n, :, lanes] = value
            msg_ref[n, pl.ds(eb, 1), :] = value[end : end + 1]
            msg_ref[n, pl.ds(24 + eb, 1), :] = total[end : end + 1]
        return unused

    lax.fori_loop(0, width // LANES, block, 0)


def entering(part, span_total, rate, carried, later):
    place = lax.broadcasted_iota(jnp.int32, (SEGS, LANES), 0)
    ends = part + jnp.exp2(rate * span_total) * carried
    if later:
        return jnp.where(place == SEGS - 1, carried, pltpu.roll(ends, SEGS - 1, 0))
    return jnp.where(place == 0, carried, pltpu.roll(ends, 1, 0))


def forward_kernel(column, step_ref, conv_ref, sel_ref, log_ref, part_ref, span_ref, in_ref, y_ref, entry_ref, wide_in, wide_out):
    rows, width = step_ref.shape
    steps, states = rows // SEGS, log_ref.shape[0]
    fill_maps(sel_ref, wide_in, steps, column, states)
    fill_maps(sel_ref, wide_out, steps, column + states, states)

    def block(eb, unused):
        lanes = pl.ds(pl.multiple_of(eb * LANES, LANES), LANES)
        rate = rates_of(log_ref, lanes, states)
        first = []
        for n in range(states):
            carried = jnp.broadcast_to(in_ref[n, pl.ds(eb, 1), :], (SEGS, LANES))
            first.append(entering(part_ref[n, :, lanes], span_ref[:, lanes], rate[n], carried, False))
            entry_ref[n, :, lanes] = first[n]

        def advance(j, memory):
            here = pl.ds(pl.multiple_of(j * SEGS, SEGS), SEGS)
            step = step_ref[here, lanes]
            fresh = step * conv_ref[here, lanes]
            new, terms = [], []
            for n in range(states):
                value = jnp.exp2(step * rate[n]) * memory[n] + wide_in[j * states + n] * fresh
                new.append(value)
                terms.append(wide_out[j * states + n] * value)
            while len(terms) > 1:
                terms = [a + b for a, b in zip(terms[::2], terms[1::2])]
            y_ref[here, lanes] = terms[0]
            return tuple(new)

        lax.fori_loop(0, steps, advance, tuple(first), unroll=2)
        return unused

    lax.fori_loop(0, width // LANES, block, 0)


def backward_kernel(column, step_ref, conv_ref, grad_ref, sel_ref, log_ref, entry_ref, part_ref, span_ref, in_ref,
                    gstep_ref, gconv_ref, gmaps_ref, glog_ref, wide_in, wide_out, sum_in, sum_out, states_ref, decays_ref):
    rows, width = step_ref.shape
    steps, states = rows // SEGS, log_ref.shape[0]
    fill_maps(sel_ref, wide_in, steps, column, states)
    fill_maps(sel_ref, wide_out, steps, column + states, states)
    sum_in[...] = jnp.zeros_like(sum_in)
    sum_out[...] = jnp.zeros_like(sum_out)

    def block(eb, unused):
        lanes = pl.ds(pl.multiple_of(eb * LANES, LANES), LANES)
        rate = rates_of(log_ref, lanes, states)

        def advance(j, memory):
            here = pl.ds(pl.multiple_of(j * SEGS, SEGS), SEGS)
            step = step_ref[here, lanes]
            fresh = step * conv_ref[here, lanes]
            new = []
            for n in range(states):
                decay = jnp.exp2(step * rate[n])
                value = decay * memory[n] + wide_in[j * states + n] * fresh
                decays_ref[j * states + n] = decay
                states_ref[(j + 1) * states + n] = value
                new.append(value)
            return tuple(new)

        first = []
        for n in range(states):
            first.append(entry_ref[n, :, lanes])
            states_ref[n] = first[n]
        lax.fori_loop(0, steps, advance, tuple(first), unroll=2)

        def retreat(i, carry):
            j = steps - 1 - i
            mu, slow = carry
            here = pl.ds(pl.multiple_of(j * SEGS, SEGS), SEGS)
            step = step_ref[here, lanes]
            conv = conv_ref[here, lanes]
            grad = grad_ref[here, lanes]
            fresh = step * conv
            new_mu, new_slow, by_in, by_rate = [], [], [], []
            for n in range(states):
                k = j * states + n
                lam = wide_out[k] * grad + mu[n]
                sum_out[k] += grad * states_ref[k + states]
                sum_in[k] += lam * fresh
                by_in.append(lam * wide_in[k])
                turned = lam * decays_ref[k]
                new_mu.append(turned)
                kept = turned * states_ref[k]
                by_rate.append(kept * rate[n])
                new_slow.append(slow[n] + kept * step)
            while len(by_in) > 1:
                by_in = [a + b for a, b in zip(by_in[::2], by_in[1::2])]
                by_rate = [a + b for a, b in zip(by_rate[::2], by_rate[1::2])]
            gstep_ref[here, lanes] = by_in[0] * conv + (1.0 / LOG2E) * by_rate[0]
            gconv_ref[here, lanes] = by_in[0] * step
            return tuple(new_mu), tuple(new_slow)

        last = []
        for n in range(states):
            carried = jnp.broadcast_to(in_ref[n, pl.ds(eb, 1), :], (SEGS, LANES))
            last.append(entering(part_ref[n, :, lanes], span_ref[:, lanes], rate[n], carried, True))
        zero = jnp.zeros((SEGS, LANES), jnp.float32)
        unused_mu, slow = lax.fori_loop(0, steps, retreat, (tuple(last), (zero,) * states))
        for n in range(states):
            glog_ref[n : n + 1, lanes] = (1.0 / LOG2E) * jnp.sum(slow[n] * rate[n], axis=0, keepdims=True)
        return unused

    lax.fori_loop(0, width // LANES, block, 0)

    def collect(j, unused):
        spot = lax.broadcasted_iota(jnp.int32, (SEGS, LANES), 1)
        row = jnp.zeros((SEGS, LANES), jnp.float32)
        for n in range(states):
            row = jnp.where(spot == column + n, jnp.sum(sum_in[j * states + n], axis=1, keepdims=True), row)
            row = jnp.where(spot == column + states + n, jnp.sum(sum_out[j * states + n], axis=1, keepdims=True), row)
        gmaps_ref[pl.ds(pl.multiple_of(j * SEGS, SEGS), SEGS), :] = row
        return unused

    lax.fori_loop(0, steps, collect, 0)


def exchange_kernel(later, size, msg_ref, log_ref, in_ref, taken, made, send_first, recv_first, send_second, recv_second):
    me = lax.axis_index("seq")
    barrier = pltpu.get_barrier_semaphore()
    for k in range(1, size):
        pl.semaphore_signal(
            barrier, inc=1, device_id={"seq": lax.rem(me + k, size)}, device_id_type=pl.DeviceIdType.MESH
        )
    pl.semaphore_wait(barrier, size - 1)

    def first(k):
        peer = lax.rem(me + k, size)
        return pltpu.make_async_remote_copy(
            src_ref=msg_ref.at[peer], dst_ref=taken.at[k], send_sem=send_first.at[k], recv_sem=recv_first.at[k],
            device_id={"seq": peer}, device_id_type=pl.DeviceIdType.MESH,
        )

    def second(k):
        peer = lax.rem(me + k, size)
        return pltpu.make_async_remote_copy(
            src_ref=made.at[peer], dst_ref=in_ref.at[me], send_sem=send_second.at[k], recv_sem=recv_second.at[k],
            device_id={"seq": peer}, device_id_type=pl.DeviceIdType.MESH,
        )

    outward = [first(k) for k in range(1, size)]
    for copy in outward:
        copy.start()
    taken[0] = msg_ref[me]
    rate = -LOG2E * jnp.exp(log_ref[me])
    for copy in outward:
        copy.wait()
    state = jnp.zeros(rate.shape, jnp.float32)
    for turn in range(size):
        d = size - 1 - turn if later else turn
        made[d] = state
        slot = lax.rem(me - d + size, size)
        state = jnp.exp2(rate * taken[slot, 24:48, :]) * state + taken[slot, 0:24, :]
    homeward = [second(k) for k in range(1, size)]
    for copy in homeward:
        copy.start()
    in_ref[me] = made[me]
    for copy in homeward:
        copy.wait()


WHOLE = pl.BlockSpec(memory_space=pltpu.VMEM)


def shaped(*dims, dtype=jnp.float32):
    return jax.ShapeDtypeStruct(dims, dtype)


def roomy(mebibytes, **more):
    return pltpu.CompilerParams(vmem_limit_bytes=mebibytes << 20, **more)


def summarize(step, other, selection, decay_log, later, column):
    rows, width = step.shape
    states, steps = decay_log.shape[0], rows // SEGS
    return pl.pallas_call(
        functools.partial(summary_kernel, later, column),
        out_shape=(shaped(states, SEGS, width), shaped(SEGS, width), shaped(states, 48, LANES)),
        in_specs=[WHOLE] * 4,
        out_specs=(WHOLE,) * 3,
        scratch_shapes=[pltpu.VMEM((steps * states, SEGS, LANES), jnp.float32)],
        compiler_params=roomy(24),
        name="summary_later" if later else "summary_earlier",
    )(step, other, selection, decay_log)


def exchange(message, log_rows, later):
    states = message.shape[0]
    return pl.pallas_call(
        functools.partial(exchange_kernel, later, states),
        out_shape=shaped(states, 24, LANES),
        in_specs=[WHOLE] * 2,
        out_specs=WHOLE,
        scratch_shapes=[
            pltpu.VMEM((states, 48, LANES), jnp.float32),
            pltpu.VMEM((states, 24, LANES), jnp.float32),
        ]
        + [pltpu.SemaphoreType.DMA((states,))] * 4,
        compiler_params=roomy(16, collective_id=1 if later else 0, has_side_effects=True),
        name="exchange_later" if later else "exchange_earlier",
    )(message, log_rows)


def scan_forward(step, conv, selection, decay_log, part, span, entry, column):
    rows, width = step.shape
    states, steps = decay_log.shape[0], rows // SEGS
    wide = pltpu.VMEM((steps * states, SEGS, LANES), jnp.float32)
    return pl.pallas_call(
        functools.partial(forward_kernel, column),
        out_shape=(shaped(rows, width), shaped(states, SEGS, width)),
        in_specs=[WHOLE] * 7,
        out_specs=(WHOLE,) * 2,
        scratch_shapes=[wide] * 2,
        compiler_params=roomy(28),
        name="scan_forward",
    )(step, conv, selection, decay_log, part, span, entry)


def scan_backward(step, conv, grad, selection, decay_log, first, part, span, entry, column):
    rows, width = step.shape
    states, steps = decay_log.shape[0], rows // SEGS
    wide = pltpu.VMEM((steps * states, SEGS, LANES), jnp.float32)
    longer = pltpu.VMEM(((steps + 1) * states, SEGS, LANES), jnp.float32)
    return pl.pallas_call(
        functools.partial(backward_kernel, column),
        out_shape=(shaped(rows, width), shaped(rows, width), shaped(rows, LANES), shaped(states, width)),
        in_specs=[WHOLE] * 9,
        out_specs=(WHOLE,) * 4,
        scratch_shapes=[wide] * 4 + [longer, wide],
        compiler_params=roomy(44),
        name="scan_backward",
    )(step, conv, grad, selection, decay_log, first, part, span, entry)


def segmented(block):
    rows = block.shape[0]
    return block.reshape(SEGS, rows // SEGS, -1).transpose(1, 0, 2).reshape(rows, -1)


def in_order(block):
    rows = block.shape[0]
    return block.reshape(rows // SEGS, SEGS, -1).transpose(1, 0, 2).reshape(rows, -1)


def rms_scale(stream):
    return lax.rsqrt(jnp.mean(stream * stream, axis=-1, keepdims=True) + 1e-05)


def rms_back(stream, scale, gain, grad):
    grown = grad * gain
    along = jnp.mean(stream * grown, axis=-1, keepdims=True)
    return scale * grown - stream * (scale * scale * scale * along), jnp.sum(grad * stream * scale, axis=0)


def silu_slope(value):
    gate = jax.nn.sigmoid(value)
    return gate * (1.0 + value * (1.0 - gate))


def product(left, right):
    return jnp.dot(left, right, preferred_element_type=jnp.float32)


def across(left, right):
    return jnp.einsum("tk,dk->td", left, right, preferred_element_type=jnp.float32)


def summed_rows(left, right):
    return jnp.einsum("tk,td->kd", left, right, preferred_element_type=jnp.float32)


def expert_sums_kernel(hidden_ref, received_ref, active_ref, grad_ref, out_ref):
    pair = out_ref.shape[0]
    half = out_ref.shape[2]

    def emit(left_ref, right_ref, which):
        total = lax.dot_general(
            left_ref[...], right_ref[...], (((0,), (0,)), ((), ())), preferred_element_type=jnp.float32
        ).astype(jnp.bfloat16)
        for i in range(pair):
            out_ref[i, which] = total[i * half : (i + 1) * half]

    emit(hidden_ref, received_ref, 0)
    emit(active_ref, grad_ref, 1)


def expert_sums(grad_hidden, received, activated, grad_received, owners):
    rows, hidden = grad_hidden.shape
    width = received.shape[1]
    pair = 2
    cols = pair * hidden // owners
    chunk = pl.BlockSpec((rows, cols), lambda i: (0, i))
    fixed = pl.BlockSpec((rows, width), lambda i: (0, 0))
    return pl.pallas_call(
        expert_sums_kernel,
        grid=(owners // pair,),
        out_shape=shaped(owners, 2, hidden // owners, width, dtype=jnp.bfloat16),
        in_specs=[chunk, fixed, chunk, fixed],
        out_specs=pl.BlockSpec((pair, 2, hidden // owners, width), lambda i: (i, 0, 0, 0)),
        compiler_params=roomy(32),
        name="expert_sums",
    )(grad_hidden, received, activated, grad_received)


def total_over(block, seqs, experts):
    rows, width = block.shape
    mine = lax.psum_scatter(block.astype(jnp.bfloat16), "seq", scatter_dimension=0, tiled=True)
    parts = mine.reshape(experts, rows // (seqs * experts), width)
    parts = lax.all_to_all(parts, "expert", split_axis=0, concat_axis=0, tiled=True)
    return jnp.sum(parts.astype(jnp.float32), axis=0)


def local(
    tokens,
    expert_index,
    cotangent,
    first_gain,
    in_weight,
    conv_weight,
    conv_bias,
    select_weight,
    step_weight,
    step_bias,
    decay_log,
    skip_gain,
    out_weight,
    second_gain,
    router_weight,
    expert_first,
    expert_second,
):
    bf16, f32 = jnp.bfloat16, jnp.float32
    stream = segmented(tokens[0]).astype(f32)
    routes = segmented(expert_index[0])[:, 0]
    upstream = segmented(cotangent[0]).astype(f32)
    row_count, model_width = stream.shape
    inner = conv_bias.shape[0]
    rank = step_weight.shape[0]
    states = decay_log.shape[0]
    taps = conv_weight.shape[0]
    expert_count = router_weight.shape[1]
    capacity = 2 * row_count // expert_count
    seqs, experts = lax.axis_size("seq"), lax.axis_size("expert")
    reach = (taps - 1) * SEGS
    onward = [(i, i + 1) for i in range(seqs - 1)]
    backward = [(i + 1, i) for i in range(seqs - 1)]

    first_scale = rms_scale(stream)
    normed_in = (stream * first_scale * first_gain).astype(bf16)
    projected = product(normed_in, in_weight)
    conv_input = projected[:, :inner]
    gate_input = projected[:, inner:]

    ends = conv_input[row_count - reach :].reshape(taps - 1, SEGS, inner)
    arrived = lax.ppermute(ends[:, SEGS - 1], "seq", onward)
    front = jnp.concatenate([arrived[:, None], ends[:, : SEGS - 1]], axis=1).reshape(reach, inner)
    padded = jnp.concatenate([front, conv_input], axis=0)
    preact = conv_bias[None, :]
    for k in range(taps):
        preact = preact + conv_weight[k][None, :] * padded[k * SEGS : k * SEGS + row_count]
    conv_out = jax.nn.silu(preact)
    conv_low = conv_out.astype(bf16)
    selection = product(conv_low, jnp.pad(select_weight, ((0, 0), (0, LANES - select_weight.shape[1]))))
    step_low = selection[:, :rank].astype(bf16)
    step_raw = product(step_low, step_weight) + step_bias
    step_size = jax.nn.softplus(step_raw)

    log_rows = jnp.pad(decay_log.reshape(states, inner // LANES, LANES), ((0, 0), (0, 24 - inner // LANES), (0, 0)))
    part, span, message = summarize(step_size, conv_out, selection, decay_log, False, rank)
    entry = exchange(message, log_rows, False)
    scanned, first = scan_forward(step_size, conv_out, selection, decay_log, part, span, entry, rank)

    mixer_out = scanned + skip_gain * conv_out
    gated = (mixer_out * jax.nn.silu(gate_input)).astype(bf16)
    middle = stream + product(gated, out_weight)
    second_scale = rms_scale(middle)
    normed_mid = (middle * second_scale * second_gain).astype(bf16)
    router_probs = jax.nn.softmax(product(normed_mid, router_weight), axis=-1)
    picks = (routes[:, None] == jnp.arange(expert_count, dtype=jnp.int32)[None, :]).astype(jnp.int32)
    chosen = picks.astype(f32)
    gate_value = jnp.sum(router_probs * chosen, axis=1)
    slot_rank = jnp.sum((jnp.cumsum(picks, axis=0) - 1) * picks, axis=1)
    slot_index = routes * capacity + slot_rank

    def dispatch(rows):
        blank = jnp.zeros((expert_count * capacity, model_width), bf16)
        placed = blank.at[slot_index].set(rows).reshape(expert_count, capacity, model_width)
        return lax.all_to_all(placed, "expert", split_axis=0, concat_axis=0, tiled=True).reshape(-1, model_width)

    def combine(rows):
        home = lax.all_to_all(
            rows.reshape(expert_count, capacity, model_width), "expert", split_axis=0, concat_axis=0, tiled=True
        )
        return home.reshape(-1, model_width)[slot_index].astype(f32)

    first_matrix, second_matrix = expert_first[0], expert_second[0]
    received = dispatch(normed_mid)
    grad_value = (gate_value[:, None] * upstream).astype(bf16)
    grad_received = dispatch(grad_value)
    hidden_pre = product(received, first_matrix)
    activated = jax.nn.gelu(hidden_pre).astype(bf16)
    result = product(activated, second_matrix).astype(bf16)
    grad_act = across(grad_received, second_matrix)
    grad_hidden = jax.vjp(jax.nn.gelu, hidden_pre)[1](grad_act)[0].astype(bf16)
    grad_sent = across(grad_hidden, first_matrix).astype(bf16)
    expert_value = combine(result)
    grad_mid_expert = combine(grad_sent)
    expert_grads = expert_sums(grad_hidden, received, activated, grad_received, seqs)

    mixed = middle + gate_value[:, None] * expert_value
    grad_gate = jnp.sum(upstream * expert_value, axis=1)
    grad_logits = (grad_gate[:, None] * gate_value[:, None] * (chosen - router_probs)).astype(bf16)
    grad_router = summed_rows(normed_mid, grad_logits)
    grad_mid = across(grad_logits, router_weight) + grad_mid_expert
    grad_middle_norm, grad_second_gain = rms_back(middle, second_scale, second_gain, grad_mid)
    grad_middle = upstream + grad_middle_norm
    middle_low = grad_middle.astype(bf16)
    grad_out_weight = summed_rows(gated, middle_low)
    grad_gated = across(middle_low, out_weight)
    grad_mixer = grad_gated * jax.nn.silu(gate_input)
    grad_gate_input = grad_gated * mixer_out * silu_slope(gate_input)
    grad_skip = jnp.sum(grad_mixer * conv_out, axis=0)

    expert_grads, out_low, grad_mixer = lax.optimization_barrier(
        (expert_grads, grad_out_weight.astype(bf16), grad_mixer)
    )
    expert_share = lax.psum_scatter(
        expert_grads.reshape(-1, model_width), "seq", scatter_dimension=0, tiled=True
    ).reshape(2, -1, model_width)
    out_share = total_over(out_low, seqs, experts)

    part, span, message = summarize(step_size, grad_mixer, selection, decay_log, True, rank + states)
    entry = exchange(message, log_rows, True)
    grad_step, grad_conv_scan, grad_maps, grad_decay_log = scan_backward(
        step_size, conv_out, grad_mixer, selection, decay_log, first, part, span, entry, rank
    )

    grad_step_raw = grad_step * jax.nn.sigmoid(step_raw)
    grad_step_bias = jnp.sum(grad_step_raw, axis=0)
    step_raw_low = grad_step_raw.astype(bf16)
    grad_step_weight = summed_rows(step_raw_low, step_low)
    grad_step_low = across(step_raw_low, step_weight)
    grad_selection = jnp.concatenate([grad_step_low, grad_maps[:, rank : rank + 2 * states]], axis=1).astype(bf16)
    grad_select_weight = summed_rows(conv_low, grad_selection)
    grad_conv_out = across(grad_selection, select_weight) + grad_conv_scan + skip_gain * grad_mixer
    grad_preact = grad_conv_out * silu_slope(preact)
    grad_conv_bias = jnp.sum(grad_preact, axis=0)
    grad_conv_weight = jnp.stack(
        [jnp.sum(grad_preact * padded[k * SEGS : k * SEGS + row_count], axis=0) for k in range(taps)], axis=1
    )
    heads = grad_preact[:reach].reshape(taps - 1, SEGS, inner)
    arrived = lax.ppermute(heads[:, 0], "seq", backward)
    back = jnp.concatenate([heads[:, 1:], arrived[:, None]], axis=1).reshape(reach, inner)
    trailing = jnp.concatenate([grad_preact, back], axis=0)
    grad_conv_input = jnp.zeros((), f32)
    for k in range(taps):
        shift = (taps - 1 - k) * SEGS
        grad_conv_input = grad_conv_input + conv_weight[k][None, :] * trailing[shift : shift + row_count]
    grad_projected = jnp.concatenate([grad_conv_input, grad_gate_input], axis=1).astype(bf16)
    grad_in_weight = summed_rows(grad_projected, normed_in)
    grad_normed = across(grad_projected, in_weight)
    grad_stream_norm, grad_first_gain = rms_back(stream, first_scale, first_gain, grad_normed)
    grad_tokens = grad_middle + grad_stream_norm

    devices = seqs * experts
    each, fewer = inner // devices, model_width // devices
    narrow = jnp.concatenate([grad_first_gain[:, None], grad_second_gain[:, None], grad_router], axis=1)
    narrow = jnp.pad(narrow.reshape(devices, fewer, -1), ((0, 0), (0, each - fewer), (0, 0))).reshape(inner, -1)
    columns = (
        grad_select_weight,
        grad_step_weight,
        grad_decay_log.T,
        grad_conv_weight,
        grad_conv_bias[:, None],
        grad_step_bias[:, None],
        grad_skip[:, None],
        narrow,
    )
    small = jnp.concatenate(columns, axis=1)
    small = jnp.pad(small, ((0, 0), (0, -small.shape[1] % LANES)))
    in_share = total_over(grad_in_weight, seqs, experts)
    small_share = total_over(small, seqs, experts)
    starts, pieces = 0, []
    for column in columns:
        pieces.append(small_share[:, starts : starts + column.shape[1]])
        starts += column.shape[1]
    narrow_share = pieces[7][:fewer]
    return (
        in_order(mixed.astype(bf16))[None],
        in_order(grad_tokens)[None],
        narrow_share[:, 0],
        in_share.T,
        pieces[3].T,
        pieces[4][:, 0],
        pieces[0],
        pieces[1].T,
        pieces[5][:, 0],
        pieces[2].T,
        pieces[6][:, 0],
        out_share,
        narrow_share[:, 1],
        narrow_share[:, 2:],
        expert_share[0].T.astype(f32)[None],
        expert_share[1].astype(f32)[None],
    )


def solution(mesh):
    return jax.shard_map(
        local,
        mesh=mesh,
        in_specs=(
            P("expert", "seq", None),
            P("expert", "seq", None),
            P("expert", "seq", None),
            P(),
            P(),
            P(),
            P(),
            P(),
            P(),
            P(),
            P(),
            P(),
            P(),
            P(),
            P(),
            P("expert", None, None),
            P("expert", None, None),
        ),
        out_specs=(
            P("expert", "seq", None),
            P("expert", "seq", None),
            P(("seq", "expert")),
            P(None, ("seq", "expert")),
            P(None, ("seq", "expert")),
            P(("seq", "expert")),
            P(("seq", "expert"), None),
            P(None, ("seq", "expert")),
            P(("seq", "expert")),
            P(None, ("seq", "expert")),
            P(("seq", "expert")),
            P(("seq", "expert"), None),
            P(("seq", "expert")),
            P(("seq", "expert"), None),
            P("expert", None, "seq"),
            P("expert", "seq", None),
        ),
        check_vma=False,
    )
```

time: 2200 us -> 747 us (0.34); the launches traced: 2160 us -> 737 us
  local copies, waits for them, and re-layouts: 677 us -> 51.3 us
  other arithmetic: 500 us -> 42.9 us
  blocking collectives: 389 us -> 0 us
  starting transfers between devices: 268 us -> 56.9 us
  waiting for transfers between devices: 175 us -> 333 us
  Pallas kernels: 0 us -> 143 us
    unnamed x1 -> x0, blocking collectives: 389 us -> none
    reduce_sum x219 -> x7, other arithmetic: 248 us -> 9.1 us  [the longest x1 5.62 us: local(): grad_conv_bias = jnp.sum(grad_preact, axis=0)]
    reduce_scatter x1 -> x3, waiting for transfers between devices: 0.01 us -> 229 us  [the longest x2 147 us: total_over(): lax.psum_scatter(block.astype(jnp.bfloat16), 'seq', scatter_dimension=0,...]
    concatenate x40 -> x7, local copies, waits for them, and re-layouts: 145 us -> 2.03 us  [the longest x6 1.17 us: local(): jnp.concatenate([grad_first_gain[:, None], grad_second_gain[:, None], gra...]
    pallas_call x0 -> x7, Pallas kernels: none -> 143 us  [the longest x1 50.8 us: scan_backward(): pl.pallas_call(functools.partial(backward_kernel, column), out_shape=(sha...]
    broadcast_in_dim x256 -> x5, local copies, waits for them, and re-layouts: 130 us -> 0.07 us  [the longest x2 0.05 us: local(): arrived[:, None]]
    unnamed x35 -> x1, starting transfers between devices: 119 us -> 0.04 us
    add_any x58 -> x0, other arithmetic: 110 us -> none  [the longest x48 82.3 us: advance(): step_now[None, :] * decay_rate]
  transfers between devices with their start and end apart: 72 -> 13, of which waited for: 40 -> 10; matrix products, arithmetic and copies ran while one was open for 27% -> 9% of each run, Pallas kernels for 0% -> 2%
where the time goes in v1:
time: 747 us; the launch traced here: 737 us
  waiting for transfers between devices  333 us (45%)
  Pallas kernels  143 us (19%)
  matrix products  95.6 us (13%)
  starting transfers between devices  56.9 us (8%)
  local copies, waits for them, and re-layouts  51.3 us (7%)
  other arithmetic  42.9 us (6%)
  between operations  15.4 us (2%)
    reduce_scatter x2, waiting for transfers between devices, total_over(): lax.psum_scatter(block.astype(jnp.bfloat16), 'seq', scatter_dimension=0,...  147 us
    reduce_scatter x1, waiting for transfers between devices, local(): lax.psum_scatter(expert_grads.reshape(-1, model_width), 'seq', scatter_di...  82.8 us
    unnamed x5, waiting for transfers between devices  71.7 us
    pallas_call x1, Pallas kernels, scan_backward(): pl.pallas_call(functools.partial(backward_kernel, column), out_shape=(sha...  50.8 us
    dot_general x7, matrix products, across(): jnp.einsum('tk,dk->td', left, right, preferred_element_type=jnp.float32)  44.6 us
    dot_general x7, matrix products, product(): return jnp.dot(left, right, preferred_element_type=jnp.float32)  35.6 us
    pallas_call x2, Pallas kernels, exchange(): pl.pallas_call(functools.partial(exchange_kernel, later, states), out_sha...  32.7 us
    pallas_call x2, Pallas kernels, summarize(): pl.pallas_call(functools.partial(summary_kernel, later, column), out_shap...  28.2 us
  transfers between devices with their start and end apart: 13, of which 10 were waited for; matrix products, arithmetic and copies ran while one was open for 9% of the time, Pallas kernels for 2%

profile of v1, /device:TPU:1, one launch (start us, length us, event | category | flops | bytes accessed | tf_op | source)
XLA Modules:
  0.0 737.4 jit_solution(3368144753046612621)
XLA Ops:
  10.6 7.1 fusion.82
  40.2 14.2 %summary_earlier.1 = (f32[16,8,2304]{2,1,0:T(8,128)S(1)}, f32[8,2304]{1,0:T(8,128)S(1)}, f32[16,48,128]{2,1,0:T(8,128)S(1)}) custom-call(f32[256,2304]{1,0:T(8,128)S(1)} %get-tuple-element.159.step_ref, f32[256,2304]{1,0:T(8,128)S(1)} %get-tuple-element.151.other_ref.conv_ref, f32[256,128]{1,0:T(8,128)S(1)} %copy.102.sel_ref, f32[16,2304]{1,0:T(8,128)S(1)} %copy-done.8), custom_call_target="tpu_custom_call" | custom-call | tf_op jit(solution)/shard_map/summary_earlier/pallas_call | solution.py:285
  54.4 17.9 %exchange_earlier.1.in_ref = f32[16,24,128]{2,1,0:T(8,128)S(1)} custom-call(f32[16,48,128]{2,1,0:T(8,128)S(1)} %get-tuple-element.33.msg_ref, f32[16,24,128]{2,1,0:T(8,128)S(1)} %pad.19.log_ref), custom_call_target="tpu_custom_call" | custom-call | tf_op jit(solution)/shard_map/exchange_earlier/pallas_call | solution.py:298
  72.4 19.1 %scan_forward.1 = (f32[256,2304]{1,0:T(8,128)S(1)}, f32[16,8,2304]{2,1,0:T(8,128)S(1)}) custom-call(f32[256,2304]{1,0:T(8,128)S(1)} %get-tuple-element.159.step_ref, f32[256,2304]{1,0:T(8,128)S(1)} %get-tuple-element.151.other_ref.conv_ref, f32[256,128]{1,0:T(8,128)S(1)} %copy.102.sel_ref, f32[16,2304]{1,0:T(8,128)S(1)} %copy-done.8, ...), custom_call_target="tpu_custom_call" | custom-call | tf_op jit(solution)/shard_map/scan_forward/pallas_call | solution.py:317
  100.5 7.0 all-to-all-start
  116.4 7.7 %all-to-all-done = bf16[8,64,1152]{2,1,0:T(8,128)(2,1)} async-done(((bf16[8,64,1152]{2,1,0:T(8,128)(2,1)}), bf16[8,64,1152]{2,1,0:T(8,128)(2,1)}, u32[]{:S(2)}, u32[]{:S(2)}) %all-to-all-start) | async-done | bytes 1179680 | tf_op jit(solution)/shard_map/all_to_all | solution.py:497
  129.1 12.3 %multiply_convert_fusion = (bf16[512,3072]{1,0:T(8,128)(2,1)}, f32[512,3072]{1,0:T(8,128)}) fusion(bf16[512,1152]{1,0:T(8,128)(2,1)} %bitcast.14.received_ref, bf16[1,1152,3072]{2,1,0:T(8,128)(2,1)} %param.32), kind=kOutput, calls=%fused_computation.24 | convolution fusion | flops 3638034432 | bytes 17694720 | tf_op jit(solution)/shard_map/dot_general | solution.py:370
  145.8 10.7 %fusion.14.hidden_ref = bf16[512,3072]{1,0:T(8,128)(2,1)S(1)} fusion(f32[512,3072]{1,0:T(8,128)} %get-tuple-element.166, bf16[512,1152]{1,0:T(8,128)(2,1)} %bitcast.28.grad_ref, bf16[1,3072,1152]{2,1,0:T(8,128)(2,1)} %param.33), kind=kOutput, calls=%fused_computation.23 | convolution fusion | flops 3655335936 | bytes 17694720 | tf_op jit(solution)/shard_map/tk,dk->td/dot_general | solution.py:374
  156.5 9.4 %fusion.19 = bf16[512,1152]{1,0:T(8,128)(2,1)} fusion(bf16[512,3072]{1,0:T(8,128)(2,1)S(1)} %fusion.14.hidden_ref, bf16[1,1152,3072]{2,1,0:T(8,128)(2,1)} %param.32), kind=kOutput, calls=%fused_computation.35 | convolution fusion | flops 3624468480 | bytes 11403264 | tf_op jit(solution)/shard_map/tk,dk->td/dot_general | solution.py:374
  165.9 15.0 %all-to-all-start.3 = ((bf16[8,64,1152]{2,1,0:T(8,128)(2,1)}), bf16[8,64,1152]{2,1,0:T(8,128)(2,1)}, u32[]{:S(2)}, u32[]{:S(2)}) async-start(bf16[8,64,1152]{2,1,0:T(8,128)(2,1)} %bitcast.167), calls=%async_computation.3 | async-start | bytes 2359296 | tf_op jit(solution)/shard_map/all_to_all | solution.py:500
  180.9 9.2 %fusion.22 = bf16[512,1152]{1,0:T(8,128)(2,1)} fusion(bf16[512,3072]{1,0:T(8,128)(2,1)} %get-tuple-element.165.active_ref, bf16[1,3072,1152]{2,1,0:T(8,128)(2,1)} %param.33), kind=kOutput, calls=%fused_computation.36 | convolution fusion | flops 3624468480 | bytes 11403264 | tf_op jit(solution)/shard_map/dot_general | solution.py:370
  190.1 7.4 all-to-all-done.3
  207.5 12.0 %expert_sums.1 = bf16[16,2,192,1152]{3,2,1,0:T(8,128)(2,1)S(1)} custom-call(bf16[512,3072]{1,0:T(8,128)(2,1)S(1)} %copy-done.11, bf16[512,1152]{1,0:T(8,128)(2,1)} %bitcast.14.received_ref, bf16[512,3072]{1,0:T(8,128)(2,1)S(1)} %copy-done.9, bf16[512,1152]{1,0:T(8,128)(2,1)} %bitcast.28.grad_ref), custom_call_target="tpu_custom_call" | custom-call | tf_op jit(solution)/shard_map/expert_sums/pallas_call | solution.py:403
  243.7 8.4 %multiply_reduce_fusion = (bf16[2304]{0:T(1024)(128)(2,1)}, f32[256,2304]{1,0:T(8,128)}, bf16[256,2304]{1,0:T(8,128)(2,1)}) fusion(f32[256,2304]{1,0:T(8,128)S(1)} %get-tuple-element.151.other_ref.conv_ref, f32[256,4608]{1,0:T(8,128)} %copy-done.21, f32[256,2304]{1,0:T(8,128)S(1)} %copy-done.13, f32[2304]{0:T(1024)S(1)} %copy-done.58, ...), kind=kOutput, calls=%fused_computation.57 | convolution fusion | flops 1368684288 | bytes 17118720 | tf_op jit(solution)/shard_map/tk,dk->td/dot_general | solution.py:374
  257.9 13.9 %summary_later.1 = (f32[16,8,2304]{2,1,0:T(8,128)S(1)}, f32[8,2304]{1,0:T(8,128)S(1)}, f32[16,48,128]{2,1,0:T(8,128)S(1)}) custom-call(f32[256,2304]{1,0:T(8,128)S(1)} %copy-done.5, f32[256,2304]{1,0:T(8,128)S(1)} %copy-done.6, f32[256,128]{1,0:T(8,128)S(1)} %copy.102.sel_ref, f32[16,2304]{1,0:T(8,128)S(1)} %copy-done.8), custom_call_target="tpu_custom_call" | custom-call | tf_op jit(solution)/shard_map/summary_later/pallas_call | solution.py:285
  271.9 14.8 %exchange_later.1.in_ref = f32[16,24,128]{2,1,0:T(8,128)S(1)} custom-call(f32[16,48,128]{2,1,0:T(8,128)S(1)} %get-tuple-element.39.msg_ref, f32[16,24,128]{2,1,0:T(8,128)S(1)} %pad.19.log_ref), custom_call_target="tpu_custom_call" | custom-call | tf_op jit(solution)/shard_map/exchange_later/pallas_call | solution.py:298
  286.7 50.8 %scan_backward.1 = (f32[256,2304]{1,0:T(8,128)S(1)}, f32[256,2304]{1,0:T(8,128)S(1)}, f32[256,128]{1,0:T(8,128)S(1)}, f32[16,2304]{1,0:T(8,128)S(1)}) custom-call(f32[256,2304]{1,0:T(8,128)S(1)} %copy-done.5, f32[256,2304]{1,0:T(8,128)} %copy-done.1, f32[256,2304]{1,0:T(8,128)} %get-tuple-element.35.other_ref.grad_ref, f32[256,128]{1,0:T(8,128)S(1)} %copy.102.sel_ref, ...), custom_call_target="tpu_custom_call" | custom-call | tf_op jit(solution)/shard_map/scan_backward/pallas_call | solution.py:333
  358.4 9.1 %fusion.51 = (bf16[1152]{0:T(1024)(128)(2,1)S(1)}, f32[256]{0:T(256)S(1)}, f32[256,1152]{1,0:T(8,128)}) fusion(f32[8,32,1152]{2,1,0:T(8,128)S(1)} %copy-done.31, f32[256]{0:T(256)S(1)} %copy-done.63, f32[1152]{0:T(1024)S(1)} %copy-done.65, bf16[1152,4608]{1,0:T(8,128)(2,1)} %param.21, bf16[256,2304]{1,0:T(8,128)(2,1)S(1)} %copy-done.71, ...), kind=kOutput, calls=%fused_computation.94 | convolution fusion | flops 2724395776 | bytes 15344384 | tf_op jit(solution)/shard_map/tk,dk->td/dot_general | solution.py:374
  373.0 8.9 %convolution_convert_fusion = bf16[4608,1152]{1,0:T(8,128)(2,1)} fusion(bf16[256,2304]{1,0:T(8,128)(2,1)} %get-tuple-element.153, bf16[256,2304]{1,0:T(8,128)(2,1)S(1)} %copy-done.39, f32[8,32,1152]{2,1,0:T(8,128)S(1)} %copy-done.32, f32[1152]{0:T(1024)S(1)} %copy-done.65, f32[256]{0:T(256)S(1)} %copy-done.63), kind=kOutput, calls=%fused_computation.4 | convolution fusion | flops 2728820736 | bytes 14161408 | tf_op jit(solution)/shard_map/tk,td->kd/dot_general | solution.py:378
  383.9 63.3 %reduce-scatter.13.cloned.1.call-done = bf16[144,256]{1,0:T(8,128)(2,1)} async-done(((bf16[2304,256]{1,0:T(8,128)(2,1)}), bf16[144,256]{1,0:T(8,128)(2,1)}) %reduce-scatter.13.cloned.1.call-update) | async-done | bytes 73744 | tf_op jit(solution)/shard_map/reduce_scatter | solution.py:416
  460.3 70.5 %reduce-scatter.15.cloned.1.call-done = bf16[144,1152]{1,0:T(8,128)(2,1)} async-done(((bf16[2304,1152]{1,0:T(8,128)(2,1)}), bf16[144,1152]{1,0:T(8,128)(2,1)}) %reduce-scatter.15.cloned.1.call-update) | async-done | bytes 331792
  541.9 83.3 %reduce-scatter.9.cloned.1.call-done = bf16[288,1152]{1,0:T(8,128)(2,1)} async-done(((bf16[4608,1152]{1,0:T(8,128)(2,1)}), bf16[288,1152]{1,0:T(8,128)(2,1)}) %reduce-scatter.9.cloned.1.call-update) | async-done | bytes 663568 | tf_op jit(solution)/shard_map/reduce_scatter | solution.py:416
  635.5 9.0 %all-to-all-done.5 = bf16[8,36,1152]{2,1,0:T(8,128)(2,1)S(1)} async-done(((bf16[8,36,1152]{2,1,0:T(8,128)(2,1)}), bf16[8,36,1152]{2,1,0:T(8,128)(2,1)S(1)}, u32[]{:S(2)}, u32[]{:S(2)}) %all-to-all-start.5) | async-done | bytes 663584 | tf_op jit(solution)/shard_map/all_to_all | solution.py:418
  645.2 82.8 %reduce-scatter.11.cloned.1.call-done = bf16[384,1152]{1,0:T(8,128)(2,1)} async-done(((bf16[6144,1152]{1,0:T(8,128)(2,1)}), bf16[384,1152]{1,0:T(8,128)(2,1)}) %reduce-scatter.11.cloned.1.call-update) | async-done | bytes 884752 | tf_op jit(solution)/shard_map/reduce_scatter | solution.py:536
  (286 shorter events, 158.2 us)
Async XLA Ops:
  7.2 30.0 %copy-start = (bf16[72,2304]{1,0:T(8,128)(2,1)S(1)}, bf16[72,2304]{1,0:T(8,128)(2,1)}, u32[]{:S(2)}) copy-start(bf16[72,2304]{1,0:T(8,128)(2,1)} %param.25) | copy-start | bytes 995332
  20.0 10.5 %collective-permute-start = (f32[3,2304]{1,0:T(4,128)S(1)}, f32[3,2304]{1,0:T(4,128)S(1)}, u32[]{:S(2)}, u32[]{:S(2)}) collective-permute-start(f32[3,2304]{1,0:T(4,128)S(1)} %bitcast.174), channel_id=1, source_target_pairs={{0,8},{8,16},{16,24},{24,32},{32,40},{40,48},{48,56},{56,64},{64,7... | collective-permute-start | bytes 82952 | tf_op jit(solution)/shard_map/ppermute | solution.py:464
  26.9 70.0 %copy-start.67 = (s32[256,1]{0,1:T(1,128)}, s32[256,1]{0,1:T(1,128)S(1)}, u32[]{:S(2)}) copy-start(s32[256,1]{0,1:T(1,128)S(1)} %compare_select_fusion.1) | copy-start | bytes 3076
  36.5 207.1 %copy-start.1 = (f32[256,2304]{1,0:T(8,128)}, f32[256,2304]{1,0:T(8,128)S(1)}, u32[]{:S(2)}) copy-start(f32[256,2304]{1,0:T(8,128)S(1)} %get-tuple-element.151.other_ref.conv_ref) | copy-start | bytes 7077892
  37.2 54.3 %slice-start = ((s8[4718592]{0:T(1024)(128)(4,1)}), s8[4194304]{0:T(1024)(128)(4,1)S(1)}, s32[]{:S(2)}) async-start(s8[4718592]{0:T(1024)(128)(4,1)} %bitcast.160), calls=%async_computation.15 | async-start | bytes 8388608
  40.2 32.2 %copy-start.4 = (f32[256,2304]{1,0:T(8,128)}, f32[256,2304]{1,0:T(8,128)S(1)}, u32[]{:S(2)}) copy-start(f32[256,2304]{1,0:T(8,128)S(1)} %get-tuple-element.159.step_ref) | copy-start | bytes 7077892
  40.2 51.4 %slice-start.1 = ((s8[4718592]{0:T(1024)(128)(4,1)}), s8[524288]{0:T(1024)(128)(4,1)S(1)}, s32[]{:S(2)}) async-start(s8[4718592]{0:T(1024)(128)(4,1)} %bitcast.160), calls=%async_computation.16 | async-start | bytes 1048576
  40.2 53.2 %slice-start.2 = ((s8[5308416]{0:T(1024)(128)(4,1)}), s8[4194304]{0:T(1024)(128)(4,1)S(1)}, s32[]{:S(2)}) async-start(s8[5308416]{0:T(1024)(128)(4,1)} %bitcast.182), calls=%async_computation.17 | async-start | bytes 8388608
  72.3 21.0 %slice-start.3 = ((s8[5308416]{0:T(1024)(128)(4,1)}), s8[1114112]{0:T(1024)(128)(4,1)S(1)}, s32[]{:S(2)}) async-start(s8[5308416]{0:T(1024)(128)(4,1)} %bitcast.182), calls=%async_computation.18 | async-start | bytes 2228224
  100.5 23.6 %all-to-all-start = ((bf16[8,64,1152]{2,1,0:T(8,128)(2,1)}), bf16[8,64,1152]{2,1,0:T(8,128)(2,1)}, u32[]{:S(2)}, u32[]{:S(2)}) async-start(bf16[8,64,1152]{2,1,0:T(8,128)(2,1)} %bitcast.162), calls=%async_computation | async-start | bytes 2359296 | tf_op jit(solution)/shard_map/all_to_all | solution.py:497
  124.1 21.7 %all-to-all-start.2 = ((bf16[8,64,1152]{2,1,0:T(8,128)(2,1)}), bf16[8,64,1152]{2,1,0:T(8,128)(2,1)}, u32[]{:S(2)}, u32[]{:S(2)}) async-start(bf16[8,64,1152]{2,1,0:T(8,128)(2,1)} %bitcast.163), calls=%async_computation.2 | async-start | bytes 2359296 | tf_op jit(solution)/shard_map/all_to_all | solution.py:497
  165.9 31.6 %all-to-all-start.3 = ((bf16[8,64,1152]{2,1,0:T(8,128)(2,1)}), bf16[8,64,1152]{2,1,0:T(8,128)(2,1)}, u32[]{:S(2)}, u32[]{:S(2)}) async-start(bf16[8,64,1152]{2,1,0:T(8,128)(2,1)} %bitcast.167), calls=%async_computation.3 | async-start | bytes 2359296 | tf_op jit(solution)/shard_map/all_to_all | solution.py:500
  197.5 31.1 %all-to-all-start.1 = ((bf16[8,64,1152]{2,1,0:T(8,128)(2,1)}), bf16[8,64,1152]{2,1,0:T(8,128)(2,1)}, u32[]{:S(2)}, u32[]{:S(2)}) async-start(bf16[8,64,1152]{2,1,0:T(8,128)(2,1)} %bitcast.166), calls=%async_computation.1 | async-start | bytes 2359296 | tf_op jit(solution)/shard_map/all_to_all | solution.py:500
  202.5 244.7 %reduce-scatter.13.cloned.1.call-start = ((), (), s32[]{:S(2)}) async-start(), calls=%async_computation.13 | async-start | bytes 1253376 | tf_op jit(solution)/shard_map/reduce_scatter | solution.py:416
  257.9 28.8 %copy-start.15 = (f32[16,8,2304]{2,1,0:T(8,128)S(1)}, f32[16,8,2304]{2,1,0:T(8,128)}, u32[]{:S(2)}) copy-start(f32[16,8,2304]{2,1,0:T(8,128)} %copy-done.14) | copy-start | bytes 3538948
  286.7 50.8 %copy-start.35 = (f32[256,2304]{1,0:T(8,128)S(1)}, f32[256,2304]{1,0:T(8,128)}, u32[]{:S(2)}) copy-start(f32[256,2304]{1,0:T(8,128)} %get-tuple-element.160) | copy-start | bytes 7077892
  346.5 5.0 collective-permute-start.1
  371.4 159.4 %reduce-scatter.15.cloned.1.call-start = ((), (), s32[]{:S(2)}) async-start(), calls=%async_computation.14 | async-start | bytes 5640192
  372.1 253.0 %reduce-scatter.9.cloned.1.call-start = ((), (), s32[]{:S(2)}) async-start(), calls=%async_computation.11 | async-start | bytes 11280384 | tf_op jit(solution)/shard_map/reduce_scatter | solution.py:416
  381.9 346.0 %reduce-scatter.11.cloned.1.call-start = ((), (), s32[]{:S(2)}) async-start(), calls=%async_computation.12 | async-start | bytes 15040512 | tf_op jit(solution)/shard_map/reduce_scatter | solution.py:536
  382.5 72.8 %copy-start.23 = (f32[256,1152]{1,0:T(8,128)S(1)}, f32[256,1152]{1,0:T(8,128)}, u32[]{:S(2)}) copy-start(f32[256,1152]{1,0:T(8,128)} %copy-done.22) | copy-start | bytes 3538948
  448.7 11.5 %all-to-all-start.4 = ((bf16[8,18,256]{2,1,0:T(8,128)(2,1)}), bf16[8,18,256]{2,1,0:T(8,128)(2,1)S(1)}, u32[]{:S(2)}, u32[]{:S(2)}) async-start(bf16[8,18,256]{2,1,0:T(8,128)(2,1)} %reshape.263), calls=%async_computation.4 | async-start | bytes 196608 | tf_op jit(solution)/shard_map/all_to_all | solution.py:418
  532.6 94.5 %all-to-all-start.6 = ((bf16[8,18,1152]{2,1,0:T(8,128)(2,1)}), bf16[8,18,1152]{2,1,0:T(8,128)(2,1)S(1)}, u32[]{:S(2)}, u32[]{:S(2)}) async-start(bf16[8,18,1152]{2,1,0:T(8,128)(2,1)} %reshape.265), calls=%async_computation.7 | async-start | bytes 884736 | tf_op jit(solution)/shard_map/all_to_all | solution.py:418
  627.1 17.3 %all-to-all-start.5 = ((bf16[8,36,1152]{2,1,0:T(8,128)(2,1)}), bf16[8,36,1152]{2,1,0:T(8,128)(2,1)S(1)}, u32[]{:S(2)}, u32[]{:S(2)}) async-start(bf16[8,36,1152]{2,1,0:T(8,128)(2,1)} %reshape.264), calls=%async_computation.6 | async-start | bytes 1474560 | tf_op jit(solution)/shard_map/all_to_all | solution.py:418
  (65 other events, 300.0 us)
Sparse Core Ops, SparseCore 0:
  371.5 75.6 reduce-scatter.12
  450.7 80.0 reduce-scatter.14
  534.6 90.5 reduce-scatter.8
  628.5 99.3 reduce-scatter.10

commit v2 on v1

--- a/solution.py
+++ b/solution.py
@@ -13,16 +13,38 @@
 LOG2E = math.log2(math.e)
 
 
-def fill_maps(sel_ref, wide_ref, steps, column, states):
-    def fill(j, unused):
-        rows = sel_ref[pl.ds(pl.multiple_of(j * SEGS, SEGS), SEGS), :]
-        for n in range(states):
-            wide_ref[j * states + n] = jnp.broadcast_to(
-                rows[:, column + n : column + n + 1], (SEGS, LANES)
-            )
-        return unused
-
-    lax.fori_loop(0, steps, fill, 0)
+def spread_ones(states):
+    row = lax.broadcasted_iota(jnp.int32, (LANES, states * LANES), 0)
+    lane = lax.broadcasted_iota(jnp.int32, (LANES, states * LANES), 1)
+    return row, lane // LANES
+
+
+def fill_maps(sel_ref, wide_ref, column, states):
+    row, block = spread_ones(states)
+    ones = jnp.where(row == block + column, 1.0, 0.0).astype(jnp.bfloat16)
+    left, total = sel_ref[...], None
+    for unused in range(3):
+        part = left.astype(jnp.bfloat16)
+        left = left - part.astype(jnp.float32)
+        spread = jnp.dot(part, ones, preferred_element_type=jnp.float32)
+        total = spread if total is None else total + spread
+    wide_ref[...] = total
+
+
+def gather_maps(sum_ref, column, states):
+    row, block = spread_ones(states)
+    ones = jnp.where(row == block + column, 1.0, 0.0).astype(jnp.bfloat16)
+    left, total = sum_ref[...], None
+    for unused in range(3):
+        part = left.astype(jnp.bfloat16)
+        left = left - part.astype(jnp.float32)
+        summed = lax.dot_general(part, ones, (((1,), (1,)), ((), ())), preferred_element_type=jnp.float32)
+        total = summed if total is None else total + summed
+    return total
+
+
+def at(n):
+    return pl.ds(n * LANES, LANES)
 
 
 def segment_prefix(value, span, rate, later):
@@ -59,7 +81,7 @@
 def summary_kernel(later, column, step_ref, other_ref, sel_ref, log_ref, part_ref, span_ref, msg_ref, wide):
     rows, width = step_ref.shape
     steps, states = rows // SEGS, log_ref.shape[0]
-    fill_maps(sel_ref, wide, steps, column, states)
+    fill_maps(sel_ref, wide, column, states)
 
     def block(eb, unused):
         lanes = pl.ds(pl.multiple_of(eb * LANES, LANES), LANES)
@@ -76,7 +98,7 @@
             new = []
             for n in range(states):
                 decay = jnp.exp2(step * rate[n])
-                fresh = wide[j * states + n] * other
+                fresh = wide[here, at(n)] * other
                 if later:
                     new.append(decay * (memory[n] + fresh))
                 else:
@@ -84,7 +106,7 @@
             return span + step, tuple(new)
 
         zero = jnp.zeros((SEGS, LANES), jnp.float32)
-        span, memory = lax.fori_loop(0, steps, advance, (zero, (zero,) * states), unroll=2)
+        span, memory = lax.fori_loop(0, steps, advance, (zero, (zero,) * states), unroll=8)
         total = span_prefix(span, later)
         span_ref[:, lanes] = total
         end = 0 if later else SEGS - 1
@@ -109,8 +131,8 @@
 def forward_kernel(column, step_ref, conv_ref, sel_ref, log_ref, part_ref, span_ref, in_ref, y_ref, entry_ref, wide_in, wide_out):
     rows, width = step_ref.shape
     steps, states = rows // SEGS, log_ref.shape[0]
-    fill_maps(sel_ref, wide_in, steps, column, states)
-    fill_maps(sel_ref, wide_out, steps, column + states, states)
+    fill_maps(sel_ref, wide_in, column, states)
+    fill_maps(sel_ref, wide_out, column + states, states)
 
     def block(eb, unused):
         lanes = pl.ds(pl.multiple_of(eb * LANES, LANES), LANES)
@@ -127,15 +149,15 @@
             fresh = step * conv_ref[here, lanes]
             new, terms = [], []
             for n in range(states):
-                value = jnp.exp2(step * rate[n]) * memory[n] + wide_in[j * states + n] * fresh
+                value = jnp.exp2(step * rate[n]) * memory[n] + wide_in[here, at(n)] * fresh
                 new.append(value)
-                terms.append(wide_out[j * states + n] * value)
+                terms.append(wide_out[here, at(n)] * value)
             while len(terms) > 1:
                 terms = [a + b for a, b in zip(terms[::2], terms[1::2])]
             y_ref[here, lanes] = terms[0]
             return tuple(new)
 
-        lax.fori_loop(0, steps, advance, tuple(first), unroll=2)
+        lax.fori_loop(0, steps, advance, tuple(first), unroll=8)
         return unused
 
     lax.fori_loop(0, width // LANES, block, 0)
@@ -145,8 +167,8 @@
                     gstep_ref, gconv_ref, gmaps_ref, glog_ref, wide_in, wide_out, sum_in, sum_out, states_ref, decays_ref):
     rows, width = step_ref.shape
     steps, states = rows // SEGS, log_ref.shape[0]
-    fill_maps(sel_ref, wide_in, steps, column, states)
-    fill_maps(sel_ref, wide_out, steps, column + states, states)
+    fill_maps(sel_ref, wide_in, column, states)
+    fill_maps(sel_ref, wide_out, column + states, states)
     sum_in[...] = jnp.zeros_like(sum_in)
     sum_out[...] = jnp.zeros_like(sum_out)
 
@@ -161,7 +183,7 @@
             new = []
             for n in range(states):
                 decay = jnp.exp2(step * rate[n])
-                value = decay * memory[n] + wide_in[j * states + n] * fresh
+                value = decay * memory[n] + wide_in[here, at(n)] * fresh
                 decays_ref[j * states + n] = decay
                 states_ref[(j + 1) * states + n] = value
                 new.append(value)
@@ -171,7 +193,7 @@
         for n in range(states):
             first.append(entry_ref[n, :, lanes])
             states_ref[n] = first[n]
-        lax.fori_loop(0, steps, advance, tuple(first), unroll=2)
+        lax.fori_loop(0, steps, advance, tuple(first), unroll=8)
 
         def retreat(i, carry):
             j = steps - 1 - i
@@ -184,10 +206,10 @@
             new_mu, new_slow, by_in, by_rate = [], [], [], []
             for n in range(states):
                 k = j * states + n
-                lam = wide_out[k] * grad + mu[n]
-                sum_out[k] += grad * states_ref[k + states]
-                sum_in[k] += lam * fresh
-                by_in.append(lam * wide_in[k])
+                lam = wide_out[here, at(n)] * grad + mu[n]
+                sum_out[here, at(n)] += grad * states_ref[k + states]
+                sum_in[here, at(n)] += lam * fresh
+                by_in.append(lam * wide_in[here, at(n)])
                 turned = lam * decays_ref[k]
                 new_mu.append(turned)
                 kept = turned * states_ref[k]
@@ -205,23 +227,14 @@
             carried = jnp.broadcast_to(in_ref[n, pl.ds(eb, 1), :], (SEGS, LANES))
             last.append(entering(part_ref[n, :, lanes], span_ref[:, lanes], rate[n], carried, True))
         zero = jnp.zeros((SEGS, LANES), jnp.float32)
-        unused_mu, slow = lax.fori_loop(0, steps, retreat, (tuple(last), (zero,) * states))
+        unused_mu, slow = lax.fori_loop(0, steps, retreat, (tuple(last), (zero,) * states), unroll=2)
         for n in range(states):
             glog_ref[n : n + 1, lanes] = (1.0 / LOG2E) * jnp.sum(slow[n] * rate[n], axis=0, keepdims=True)
         return unused
 
     lax.fori_loop(0, width // LANES, block, 0)
 
-    def collect(j, unused):
-        spot = lax.broadcasted_iota(jnp.int32, (SEGS, LANES), 1)
-        row = jnp.zeros((SEGS, LANES), jnp.float32)
-        for n in range(states):
-            row = jnp.where(spot == column + n, jnp.sum(sum_in[j * states + n], axis=1, keepdims=True), row)
-            row = jnp.where(spot == column + states + n, jnp.sum(sum_out[j * states + n], axis=1, keepdims=True), row)
-        gmaps_ref[pl.ds(pl.multiple_of(j * SEGS, SEGS), SEGS), :] = row
-        return unused
-
-    lax.fori_loop(0, steps, collect, 0)
+    gmaps_ref[...] = gather_maps(sum_in, column, states) + gather_maps(sum_out, column + states, states)
 
 
 def exchange_kernel(later, size, msg_ref, log_ref, in_ref, taken, made, send_first, recv_first, send_second, recv_second):
@@ -287,7 +300,7 @@
         out_shape=(shaped(states, SEGS, width), shaped(SEGS, width), shaped(states, 48, LANES)),
         in_specs=[WHOLE] * 4,
         out_specs=(WHOLE,) * 3,
-        scratch_shapes=[pltpu.VMEM((steps * states, SEGS, LANES), jnp.float32)],
+        scratch_shapes=[pltpu.VMEM((rows, states * LANES), jnp.float32)],
         compiler_params=roomy(24),
         name="summary_later" if later else "summary_earlier",
     )(step, other, selection, decay_log)
@@ -313,7 +326,7 @@
 def scan_forward(step, conv, selection, decay_log, part, span, entry, column):
     rows, width = step.shape
     states, steps = decay_log.shape[0], rows // SEGS
-    wide = pltpu.VMEM((steps * states, SEGS, LANES), jnp.float32)
+    wide = pltpu.VMEM((rows, states * LANES), jnp.float32)
     return pl.pallas_call(
         functools.partial(forward_kernel, column),
         out_shape=(shaped(rows, width), shaped(states, SEGS, width)),
@@ -328,14 +341,14 @@
 def scan_backward(step, conv, grad, selection, decay_log, first, part, span, entry, column):
     rows, width = step.shape
     states, steps = decay_log.shape[0], rows // SEGS
-    wide = pltpu.VMEM((steps * states, SEGS, LANES), jnp.float32)
+    wide = pltpu.VMEM((rows, states * LANES), jnp.float32)
     longer = pltpu.VMEM(((steps + 1) * states, SEGS, LANES), jnp.float32)
     return pl.pallas_call(
         functools.partial(backward_kernel, column),
         out_shape=(shaped(rows, width), shaped(rows, width), shaped(rows, LANES), shaped(states, width)),
         in_specs=[WHOLE] * 9,
         out_specs=(WHOLE,) * 4,
-        scratch_shapes=[wide] * 4 + [longer, wide],
+        scratch_shapes=[wide] * 4 + [longer, pltpu.VMEM((steps * states, SEGS, LANES), jnp.float32)],
         compiler_params=roomy(44),
         name="scan_backward",
     )(step, conv, grad, selection, decay_log, first, part, span, entry)
@@ -378,45 +391,316 @@
     return jnp.einsum("tk,td->kd", left, right, preferred_element_type=jnp.float32)
 
 
-def expert_sums_kernel(hidden_ref, received_ref, active_ref, grad_ref, out_ref):
+CHUNK = 1024
+GELU_OUT = math.sqrt(2.0 / math.pi)
+GELU_IN = 0.044715
+
+
+def transposed_dot(left, right):
+    return lax.dot_general(left, right, (((1,), (1,)), ((), ())), preferred_element_type=jnp.float32)
+
+
+def column_dot(left, right):
+    return lax.dot_general(left, right, (((0,), (0,)), ((), ())), preferred_element_type=jnp.float32)
+
+
+def three_parts(value):
+    parts, left = [], value
+    for unused in range(3):
+        part = left.astype(jnp.bfloat16)
+        left = left - part.astype(jnp.float32)
+        parts.append(part)
+    return parts
+
+
+def expert_pull_kernel(up_ref, second_ref, pull_ref):
+    pull_ref[...] = transposed_dot(up_ref[...], second_ref[...]).astype(jnp.bfloat16)
+
+
+def expert_pull(upstream, second):
+    rows, width = upstream.shape
+    hidden = second.shape[0]
+    return pl.pallas_call(
+        expert_pull_kernel,
+        grid=(hidden // CHUNK,),
+        out_shape=shaped(rows, hidden, dtype=jnp.bfloat16),
+        in_specs=[pl.BlockSpec((rows, width), lambda i: (0, 0)), pl.BlockSpec((CHUNK, width), lambda i: (i, 0))],
+        out_specs=pl.BlockSpec((rows, CHUNK), lambda i: (0, i)),
+        compiler_params=roomy(24),
+        cost_estimate=pl.CostEstimate(flops=2 * rows * hidden * width, bytes_accessed=2 * (width + rows) * hidden, transcendentals=0),
+        name="expert_pull",
+    )(upstream, second)
+
+
+def expert_kernel(got_ref, up_ref, pull_ref, first_ref, second_ref, active_ref, grad_ref, value_ref, sent_ref, value, sent):
+    step, last = pl.program_id(0), pl.num_programs(0) - 1
+    width = up_ref.shape[1]
+    first = first_ref[...]
+    pre = jnp.dot(got_ref[:, :width], first, preferred_element_type=jnp.float32)
+    square = pre * pre
+    bent = jnp.tanh(pre * (GELU_OUT + GELU_OUT * GELU_IN * square))
+    share = 0.5 + 0.5 * bent
+    active = (pre * share).astype(jnp.bfloat16)
+    slope = share + pre * (0.5 - 0.5 * bent * bent) * (GELU_OUT + 3.0 * GELU_OUT * GELU_IN * square)
+    grad = (slope * pull_ref[...].astype(jnp.float32)).astype(jnp.bfloat16)
+    active_ref[...] = active
+    grad_ref[...] = grad
+    more_value = jnp.dot(active, second_ref[...], preferred_element_type=jnp.float32)
+    more_sent = transposed_dot(grad, first)
+
+    @pl.when(step == 0)
+    def begin():
+        value[...] = more_value
+        sent[...] = more_sent
+
+    @pl.when(step > 0)
+    def go_on():
+        value[...] += more_value
+        sent[...] += more_sent
+
+    @pl.when(step == last)
+    def finish():
+        low = value[...].astype(jnp.bfloat16)
+        value_ref[...] = low
+        sent_ref[:, :width] = sent[...].astype(jnp.bfloat16)
+        along = jnp.sum(low.astype(jnp.float32) * up_ref[...].astype(jnp.float32), axis=1, keepdims=True)
+        place = lax.broadcasted_iota(jnp.int32, (sent_ref.shape[0], LANES), 1)
+        tail = jnp.zeros(place.shape, jnp.float32)
+        for k, part in enumerate(three_parts(along)):
+            tail = jnp.where(place == k, part.astype(jnp.float32), tail)
+        sent_ref[:, width:] = tail.astype(jnp.bfloat16)
+
+
+def expert_layer(received, upstream, pull, first, second):
+    rows, width = upstream.shape
+    hidden = second.shape[0]
+    wide = received.shape[1]
+
+    def fixed(cols):
+        return pl.BlockSpec((rows, cols), lambda i: (0, 0))
+
+    chunk = pl.BlockSpec((rows, CHUNK), lambda i: (0, i))
+    return pl.pallas_call(
+        expert_kernel,
+        grid=(hidden // CHUNK,),
+        out_shape=(
+            shaped(rows, hidden, dtype=jnp.bfloat16),
+            shaped(rows, hidden, dtype=jnp.bfloat16),
+            shaped(rows, width, dtype=jnp.bfloat16),
+            shaped(rows, wide, dtype=jnp.bfloat16),
+        ),
+        in_specs=[
+            fixed(wide),
+            fixed(width),
+            chunk,
+            pl.BlockSpec((width, CHUNK), lambda i: (0, i)),
+            pl.BlockSpec((CHUNK, width), lambda i: (i, 0)),
+        ],
+        out_specs=(chunk, chunk, fixed(width), fixed(wide)),
+        scratch_shapes=[pltpu.VMEM((rows, width), jnp.float32)] * 2,
+        compiler_params=roomy(48),
+        cost_estimate=pl.CostEstimate(flops=6 * rows * hidden * width, bytes_accessed=4 * hidden * (width + rows), transcendentals=rows * hidden),
+        name="expert_layer",
+    )(received, upstream, pull, first, second)
+
+
+def expert_sums_kernel(hidden_ref, received_ref, active_ref, up_ref, out_ref, scaled_received, scaled_up):
     pair = out_ref.shape[0]
     half = out_ref.shape[2]
-
-    def emit(left_ref, right_ref, which):
-        total = lax.dot_general(
-            left_ref[...], right_ref[...], (((0,), (0,)), ((), ())), preferred_element_type=jnp.float32
-        ).astype(jnp.bfloat16)
+    width = up_ref.shape[1]
+
+    @pl.when(pl.program_id(0) == 0)
+    def scale():
+        parts = received_ref[:, width:].astype(jnp.float32)
+        gate = parts[:, 0:1] + parts[:, 1:2] + parts[:, 2:3]
+        scaled_received[...] = (received_ref[:, :width].astype(jnp.float32) * gate).astype(jnp.bfloat16)
+        scaled_up[...] = (up_ref[...].astype(jnp.float32) * gate).astype(jnp.bfloat16)
+
+    for which, (left_ref, right_ref) in enumerate(((hidden_ref, scaled_received), (active_ref, scaled_up))):
+        total = column_dot(left_ref[...], right_ref[...]).astype(jnp.bfloat16)
         for i in range(pair):
             out_ref[i, which] = total[i * half : (i + 1) * half]
 
-    emit(hidden_ref, received_ref, 0)
-    emit(active_ref, grad_ref, 1)
-
-
-def expert_sums(grad_hidden, received, activated, grad_received, owners):
+
+def expert_sums(grad_hidden, received, activated, upstream, owners):
     rows, hidden = grad_hidden.shape
-    width = received.shape[1]
+    width = upstream.shape[1]
     pair = 2
-    cols = pair * hidden // owners
-    chunk = pl.BlockSpec((rows, cols), lambda i: (0, i))
-    fixed = pl.BlockSpec((rows, width), lambda i: (0, 0))
+    chunk = pl.BlockSpec((rows, pair * hidden // owners), lambda i: (0, i))
+
+    def fixed(cols):
+        return pl.BlockSpec((rows, cols), lambda i: (0, 0))
+
     return pl.pallas_call(
         expert_sums_kernel,
         grid=(owners // pair,),
         out_shape=shaped(owners, 2, hidden // owners, width, dtype=jnp.bfloat16),
-        in_specs=[chunk, fixed, chunk, fixed],
+        in_specs=[chunk, fixed(received.shape[1]), chunk, fixed(width)],
         out_specs=pl.BlockSpec((pair, 2, hidden // owners, width), lambda i: (i, 0, 0, 0)),
+        scratch_shapes=[pltpu.VMEM((rows, width), jnp.bfloat16)] * 2,
         compiler_params=roomy(32),
+        cost_estimate=pl.CostEstimate(flops=4 * rows * hidden * width, bytes_accessed=4 * hidden * (width + rows), transcendentals=0),
         name="expert_sums",
-    )(grad_hidden, received, activated, grad_received)
-
-
-def total_over(block, seqs, experts):
-    rows, width = block.shape
-    mine = lax.psum_scatter(block.astype(jnp.bfloat16), "seq", scatter_dimension=0, tiled=True)
-    parts = mine.reshape(experts, rows // (seqs * experts), width)
-    parts = lax.all_to_all(parts, "expert", split_axis=0, concat_axis=0, tiled=True)
-    return jnp.sum(parts.astype(jnp.float32), axis=0)
+    )(grad_hidden, received, activated, upstream)
+
+
+ORDERS = ("xyz", "yzx", "zxy")
+PIECE = 16
+
+
+def shares_kernel(in_cols, token_ref, out_cols, middle_ref, small_ref, sum_ref, in_ref, out_ref, made, taken, half_a, half_b, half_c, one_a, one_b, one_c, sends, arrivals):
+    seq, expert = lax.axis_index("seq"), lax.axis_index("expert")
+    core = lax.rem(expert, 2)
+    place = {"y": lax.div(seq, 4), "z": lax.rem(seq, 4), "x": lax.div(expert, 2)}
+    third = token_ref.shape[1] // len(ORDERS)
+    streams = [(L, q) for L in range(len(ORDERS)) for q in range(4)]
+
+    def flip(i):
+        return i + 1 - 2 * lax.rem(i, 2)
+
+    def device(**moved):
+        at = dict(place, **moved)
+        return {"seq": at["y"] * 4 + at["z"], "expert": at["x"] * 2 + at.get("core", core)}
+
+    partners = [device(core=1 - core)]
+    for axis in "xyz":
+        partners += [device(**{axis: flip(place[axis])}), device(**{axis: 3 - place[axis]})]
+    barrier = pltpu.get_barrier_semaphore()
+    for partner in partners:
+        pl.semaphore_signal(barrier, inc=1, device_id=partner, device_id_type=pl.DeviceIdType.MESH)
+    pl.semaphore_wait(barrier, len(partners))
+
+    def send(source, target, partner, stream, number):
+        k = streams.index(stream)
+        copy = pltpu.make_async_remote_copy(
+            src_ref=source, dst_ref=target, send_sem=sends.at[k, number], recv_sem=arrivals.at[k, number],
+            device_id=partner, device_id_type=pl.DeviceIdType.MESH,
+        )
+        copy.start()
+        return copy
+
+    def add(target, source, unit):
+        def step(i, unused):
+            target[i] = target[i] + source[i]
+            return unused
+
+        lax.fori_loop(0, unit, step, 0, unroll=min(unit, 8))
+
+    for source, target in ((in_cols, in_ref), (out_cols, out_ref)):
+
+        def turn_over(k, unused, source=source, target=target):
+            spot = pl.ds(pl.multiple_of(k * LANES, LANES), LANES)
+            target[spot, :] = source[:, spot].T
+            return unused
+
+        lax.fori_loop(0, source.shape[1] // LANES, turn_over, 0)
+
+    pending = {}
+    for L, order in enumerate(ORDERS):
+        lanes = pl.ds(L * third, third)
+        for q in (6, 7):
+            made[L, q] = jnp.zeros_like(made[L, q])
+
+        def block(s, unused):
+            y, z = lax.div(s, 4), lax.rem(s, 4)
+            by_in = jnp.dot(
+                in_ref[pl.ds(pl.multiple_of(s * 288, 16), 288), :], token_ref[:, lanes], preferred_element_type=jnp.float32
+            ).astype(jnp.bfloat16)
+            here = pl.ds(pl.multiple_of(s * 144, 16), 144)
+            by_out = jnp.dot(out_ref[here, :], middle_ref[:, lanes], preferred_element_type=jnp.float32)
+            left, right = small_ref[here, :LANES], small_ref[here, LANES:]
+            for x in range(4):
+                at = {"x": x, "y": y, "z": z}
+                slot = (at[order[0]] * 4 + at[order[1]]) * 4 + at[order[2]]
+                rows = by_in[72 * x : 72 * x + 72]
+                more = by_out[36 * x : 36 * x + 36].astype(jnp.bfloat16)
+                for q in range(4):
+                    made[L, q, slot] = rows[16 * q : 16 * q + 16]
+                made[L, 4, slot, 0:8] = rows[64:]
+                made[L, 4, slot, 8:16] = more[:8]
+                made[L, 5, slot] = more[8:24]
+                made[L, 6, slot, 0:12] = more[24:]
+                last = jnp.concatenate([left[36 * x : 36 * x + 36], right[36 * x : 36 * x + 36]], axis=0)
+                for part in range(third // LANES):
+                    k = 8 * (L * (third // LANES) + part)
+                    made[L, 7, slot, 0:8, part * LANES : (part + 1) * LANES] = last[k : k + 8].astype(jnp.bfloat16)
+            return unused
+
+        lax.fori_loop(0, 16, block, 0, unroll=2)
+        for q in range(4):
+            pending[L, q] = [
+                send(made.at[L, 4 * (1 - core) + q], taken.at[L, q], device(core=1 - core), (L, q), 0)
+            ]
+
+    halves, ones = (half_a, half_b, half_c), (one_a, one_b, one_c)
+    holding = {}
+    for L, q in streams:
+        for copy in pending[L, q]:
+            copy.wait()
+        add(taken.at[L, q], made.at[L, 4 * core + q], 64)
+        holding[L, q] = taken.at[L, q]
+        pending[L, q] = start_halves(L, q, 0, holding[L, q], halves, place, flip, device, send)
+    for turn in range(3):
+        unit = 16 >> (2 * turn)
+        for L, q in streams:
+            axis = ORDERS[L][turn]
+            i = place[axis]
+            for copy in pending[L, q]:
+                copy.wait()
+            other = 3 - i if q < 2 else flip(i)
+            got = halves[turn].at[L, q]
+            add(got.at[0], holding[L, q].at[pl.ds(i * unit, unit)], unit)
+            add(got.at[1], holding[L, q].at[pl.ds(other * unit, unit)], unit)
+            partner = device(**{axis: other})
+            pending[L, q] = [send(got.at[1], ones[turn].at[L, q], partner, (L, q), 3 + 3 * turn)]
+        for L, q in streams:
+            for copy in pending[L, q]:
+                copy.wait()
+            got = ones[turn].at[L, q]
+            if turn < 2:
+                add(got, halves[turn].at[L, q, 0], unit)
+                holding[L, q] = got
+                pending[L, q] = start_halves(L, q, turn + 1, got, halves, place, flip, device, send)
+            else:
+                whole = got[0].astype(jnp.float32) + halves[turn][L, q, 0, 0].astype(jnp.float32)
+                sum_ref[4 * core + q, :, L * third : (L + 1) * third] = whole
+    here = sum_ref.at[pl.ds(4 * core, 4)]
+    send(here, here, device(core=1 - core), (0, 0), 10).wait()
+
+
+def start_halves(L, q, turn, source, halves, place, flip, device, send):
+    axis = ORDERS[L][turn]
+    unit = 16 >> (2 * turn)
+    i = place[axis]
+    partner = flip(i) if q < 2 else 3 - i
+    second = 3 - partner if q < 2 else flip(partner)
+    target = halves[turn].at[L, q]
+    return [
+        send(source.at[pl.ds(partner * unit, unit)], target.at[0], device(**{axis: partner}), (L, q), 1 + 3 * turn),
+        send(source.at[pl.ds(second * unit, unit)], target.at[1], device(**{axis: partner}), (L, q), 2 + 3 * turn),
+    ]
+
+
+def shares(in_cols, tokens, out_cols, middle, small):
+    width = tokens.shape[1]
+    third = width // len(ORDERS)
+
+    def slots(*lead):
+        return pltpu.VMEM((len(ORDERS),) + lead + (PIECE, third), jnp.bfloat16)
+
+    return pl.pallas_call(
+        shares_kernel,
+        out_shape=shaped(8, PIECE, width),
+        in_specs=[WHOLE] * 5,
+        out_specs=WHOLE,
+        scratch_shapes=[pltpu.VMEM(cols.shape[::-1], jnp.bfloat16) for cols in (in_cols, out_cols)]
+        + [slots(8, 64), slots(4, 64)]
+        + [slots(4, 2, 16 >> (2 * turn)) for turn in range(3)]
+        + [slots(4, 16 >> (2 * turn)) for turn in range(3)]
+        + [pltpu.SemaphoreType.DMA((12, 11))] * 2,
+        compiler_params=roomy(60, collective_id=2, has_side_effects=True),
+        name="shares",
+    )(in_cols, tokens, out_cols, middle, small)
 
 
 def local(
@@ -454,6 +738,27 @@
     onward = [(i, i + 1) for i in range(seqs - 1)]
     backward = [(i + 1, i) for i in range(seqs - 1)]
 
+    picks = (routes[:, None] == jnp.arange(expert_count, dtype=jnp.int32)[None, :]).astype(bf16)
+    earlier = jnp.arange(row_count)[:, None] > jnp.arange(row_count)[None, :]
+    ahead = product(earlier.astype(bf16), picks)
+    chosen = picks.astype(f32)
+    slot_index = routes * capacity + jnp.sum(ahead * chosen, axis=1).astype(jnp.int32)
+    seats = jnp.arange(expert_count * capacity, dtype=jnp.int32)
+    placing = (seats[:, None] == slot_index[None, :]).astype(bf16)
+
+    def seated(rows):
+        return product(placing, rows).astype(bf16)
+
+    def swapped(rows):
+        parts = rows.reshape(expert_count, capacity, -1)
+        parts = lax.all_to_all(parts, "expert", split_axis=0, concat_axis=0, tiled=True)
+        return parts.reshape(expert_count * capacity, -1)
+
+    def unseated(rows):
+        return jnp.einsum("st,sd->td", placing, rows, preferred_element_type=f32)
+
+    upstream_there = swapped(seated(segmented(cotangent[0])))
+
     first_scale = rms_scale(stream)
     normed_in = (stream * first_scale * first_gain).astype(bf16)
     projected = product(normed_in, in_weight)
@@ -477,6 +782,7 @@
     log_rows = jnp.pad(decay_log.reshape(states, inner // LANES, LANES), ((0, 0), (0, 24 - inner // LANES), (0, 0)))
     part, span, message = summarize(step_size, conv_out, selection, decay_log, False, rank)
     entry = exchange(message, log_rows, False)
+    entry, upstream_there = lax.optimization_barrier((entry, upstream_there))
     scanned, first = scan_forward(step_size, conv_out, selection, decay_log, part, span, entry, rank)
 
     mixer_out = scanned + skip_gain * conv_out
@@ -485,58 +791,38 @@
     second_scale = rms_scale(middle)
     normed_mid = (middle * second_scale * second_gain).astype(bf16)
     router_probs = jax.nn.softmax(product(normed_mid, router_weight), axis=-1)
-    picks = (routes[:, None] == jnp.arange(expert_count, dtype=jnp.int32)[None, :]).astype(jnp.int32)
-    chosen = picks.astype(f32)
     gate_value = jnp.sum(router_probs * chosen, axis=1)
-    slot_rank = jnp.sum((jnp.cumsum(picks, axis=0) - 1) * picks, axis=1)
-    slot_index = routes * capacity + slot_rank
-
-    def dispatch(rows):
-        blank = jnp.zeros((expert_count * capacity, model_width), bf16)
-        placed = blank.at[slot_index].set(rows).reshape(expert_count, capacity, model_width)
-        return lax.all_to_all(placed, "expert", split_axis=0, concat_axis=0, tiled=True).reshape(-1, model_width)
-
-    def combine(rows):
-        home = lax.all_to_all(
-            rows.reshape(expert_count, capacity, model_width), "expert", split_axis=0, concat_axis=0, tiled=True
-        )
-        return home.reshape(-1, model_width)[slot_index].astype(f32)
-
-    first_matrix, second_matrix = expert_first[0], expert_second[0]
-    received = dispatch(normed_mid)
-    grad_value = (gate_value[:, None] * upstream).astype(bf16)
-    grad_received = dispatch(grad_value)
-    hidden_pre = product(received, first_matrix)
-    activated = jax.nn.gelu(hidden_pre).astype(bf16)
-    result = product(activated, second_matrix).astype(bf16)
-    grad_act = across(grad_received, second_matrix)
-    grad_hidden = jax.vjp(jax.nn.gelu, hidden_pre)[1](grad_act)[0].astype(bf16)
-    grad_sent = across(grad_hidden, first_matrix).astype(bf16)
-    expert_value = combine(result)
-    grad_mid_expert = combine(grad_sent)
-    expert_grads = expert_sums(grad_hidden, received, activated, grad_received, seqs)
-
-    mixed = middle + gate_value[:, None] * expert_value
-    grad_gate = jnp.sum(upstream * expert_value, axis=1)
+
+    gate_parts = jnp.stack(three_parts(gate_value), axis=1)
+    gate_parts = jnp.pad(gate_parts, ((0, 0), (0, LANES - gate_parts.shape[1])))
+    leaving = seated(jnp.concatenate([normed_mid, gate_parts], axis=1))
+    leaving, upstream_there = lax.optimization_barrier((leaving, upstream_there))
+    received = swapped(leaving)
+    pull = expert_pull(upstream_there, expert_second[0])
+    activated, grad_hidden, value_there, grad_there = expert_layer(
+        received, upstream_there, pull, expert_first[0], expert_second[0]
+    )
+    grad_home = unseated(swapped(grad_there))
+    expert_grads = expert_sums(grad_hidden, received, activated, upstream_there, seqs)
+    expert_grads, value_there = lax.optimization_barrier((expert_grads, value_there))
+    value_home = swapped(value_there)
+
+    grad_gate = jnp.sum(grad_home[:, model_width:], axis=1)
     grad_logits = (grad_gate[:, None] * gate_value[:, None] * (chosen - router_probs)).astype(bf16)
     grad_router = summed_rows(normed_mid, grad_logits)
-    grad_mid = across(grad_logits, router_weight) + grad_mid_expert
+    grad_mid = across(grad_logits, router_weight) + gate_value[:, None] * grad_home[:, :model_width]
     grad_middle_norm, grad_second_gain = rms_back(middle, second_scale, second_gain, grad_mid)
     grad_middle = upstream + grad_middle_norm
     middle_low = grad_middle.astype(bf16)
-    grad_out_weight = summed_rows(gated, middle_low)
     grad_gated = across(middle_low, out_weight)
     grad_mixer = grad_gated * jax.nn.silu(gate_input)
     grad_gate_input = grad_gated * mixer_out * silu_slope(gate_input)
     grad_skip = jnp.sum(grad_mixer * conv_out, axis=0)
 
-    expert_grads, out_low, grad_mixer = lax.optimization_barrier(
-        (expert_grads, grad_out_weight.astype(bf16), grad_mixer)
-    )
+    expert_grads, grad_mixer = lax.optimization_barrier((expert_grads, grad_mixer))
     expert_share = lax.psum_scatter(
         expert_grads.reshape(-1, model_width), "seq", scatter_dimension=0, tiled=True
     ).reshape(2, -1, model_width)
-    out_share = total_over(out_low, seqs, experts)
 
     part, span, message = summarize(step_size, grad_mixer, selection, decay_log, True, rank + states)
     entry = exchange(message, log_rows, True)
@@ -544,6 +830,8 @@
         step_size, conv_out, grad_mixer, selection, decay_log, first, part, span, entry, rank
     )
 
+    grad_step, value_home = lax.optimization_barrier((grad_step, value_home))
+    mixed = middle + gate_value[:, None] * unseated(value_home)
     grad_step_raw = grad_step * jax.nn.sigmoid(step_raw)
     grad_step_bias = jnp.sum(grad_step_raw, axis=0)
     step_raw_low = grad_step_raw.astype(bf16)
@@ -566,7 +854,6 @@
         shift = (taps - 1 - k) * SEGS
         grad_conv_input = grad_conv_input + conv_weight[k][None, :] * trailing[shift : shift + row_count]
     grad_projected = jnp.concatenate([grad_conv_input, grad_gate_input], axis=1).astype(bf16)
-    grad_in_weight = summed_rows(grad_projected, normed_in)
     grad_normed = across(grad_projected, in_weight)
     grad_stream_norm, grad_first_gain = rms_back(stream, first_scale, first_gain, grad_normed)
     grad_tokens = grad_middle + grad_stream_norm
@@ -587,8 +874,14 @@
     )
     small = jnp.concatenate(columns, axis=1)
     small = jnp.pad(small, ((0, 0), (0, -small.shape[1] % LANES)))
-    in_share = total_over(grad_in_weight, seqs, experts)
-    small_share = total_over(small, seqs, experts)
+    in_cols, expert_share = lax.optimization_barrier((grad_projected, expert_share))
+    sums = shares(in_cols, normed_in, gated, middle_low, small).reshape(-1, model_width)
+    core = lax.axis_index("expert") % 2
+    in_share = lax.dynamic_slice_in_dim(sums, 2 * each * core, 2 * each)
+    out_share = lax.dynamic_slice_in_dim(sums, 4 * each + each * core, each)
+    small_sum = sums[112:120].reshape(8, -1, LANES).transpose(1, 0, 2).reshape(-1, 2 * each, LANES)
+    small_sum = small_sum.transpose(1, 0, 2).reshape(2 * each, -1)
+    small_share = lax.dynamic_slice_in_dim(small_sum, each * core, each)
     starts, pieces = 0, []
     for column in columns:
         pieces.append(small_share[:, starts : starts + column.shape[1]])

time: 747 us -> 439 us (0.59)
  waiting for transfers between devices: 333 us -> 7.14 us
  Pallas kernels: 143 us -> 235 us
  matrix products: 95.6 us -> 46.1 us
  starting transfers between devices: 56.9 us -> 28.6 us
  local copies, waits for them, and re-layouts: 51.3 us -> 72.4 us
  other arithmetic: 42.9 us -> 29.6 us
    reduce_scatter x2 -> x0, waiting for transfers between devices: 147 us -> none  [total_over(): lax.psum_scatter(block.astype(jnp.bfloat16), 'seq', scatter_dimension=0,...]
    pallas_call x0 -> x3, Pallas kernels: none -> 105 us  [the longest x1 77.9 us: shares(): pl.pallas_call(shares_kernel, out_shape=shaped(8, PIECE, width), in_specs...]
    reduce_scatter x1, waiting for transfers between devices: 82.8 us -> 0.01 us  [local(): lax.psum_scatter(expert_grads.reshape(-1, model_width), 'seq', scatter_di...]
    unnamed x5 -> x1, waiting for transfers between devices: 71.7 us -> 0.02 us
    all_to_all x7 -> x4, starting transfers between devices: 50.6 us -> 22.7 us  [swapped(): lax.all_to_all(parts, 'expert', split_axis=0, concat_axis=0, tiled=True)]
    dot_general x7 -> x5, matrix products: 44.6 us -> 19.3 us  [across(): jnp.einsum('tk,dk->td', left, right, preferred_element_type=jnp.float32)]
    all_to_all x7 -> x4, waiting for transfers between devices: 30 us -> 7.11 us  [swapped(): lax.all_to_all(parts, 'expert', split_axis=0, concat_axis=0, tiled=True)]
    dot_general x7 -> x8, matrix products: 35.6 us -> 19.6 us  [product(): return jnp.dot(left, right, preferred_element_type=jnp.float32)]
  transfers between devices with their start and end apart: 13 -> 7, of which waited for: 10 -> 1; matrix products, arithmetic and copies ran while one was open for 9% -> 17% of each run, Pallas kernels for 2% -> 28%
where the time goes in v2:
time: 439 us; the launch traced here: 434 us
  Pallas kernels  235 us (54%)
  local copies, waits for them, and re-layouts  72.4 us (16%)
  matrix products  46.1 us (11%)
  other arithmetic  29.6 us (7%)
  starting transfers between devices  28.6 us (7%)
  between operations  15.3 us (3%)
  waiting for transfers between devices  7.14 us (2%)
    pallas_call x1, Pallas kernels, shares(): pl.pallas_call(shares_kernel, out_shape=shaped(8, PIECE, width), in_specs...  77.9 us
    pallas_call x1, Pallas kernels, scan_backward(): pl.pallas_call(functools.partial(backward_kernel, column), out_shape=(sha...  44.5 us
    pallas_call x2, Pallas kernels, exchange(): pl.pallas_call(functools.partial(exchange_kernel, later, states), out_sha...  39.8 us
    unnamed x133, local copies, waits for them, and re-layouts  34.7 us
    all_to_all x4, starting transfers between devices, swapped(): lax.all_to_all(parts, 'expert', split_axis=0, concat_axis=0, tiled=True)  22.7 us
    pallas_call x1, Pallas kernels, expert_layer(): pl.pallas_call(expert_kernel, grid=(hidden // CHUNK,), out_shape=(shaped(...  21.1 us
    pallas_call x2, Pallas kernels, summarize(): pl.pallas_call(functools.partial(summary_kernel, later, column), out_shap...  20.3 us
    dot_general x8, matrix products, product(): return jnp.dot(left, right, preferred_element_type=jnp.float32)  19.6 us
  transfers between devices with their start and end apart: 7, of which 1 were waited for; matrix products, arithmetic and copies ran while one was open for 17% of the time, Pallas kernels for 28%

profile of v2, /device:TPU:1, one launch (start us, length us, event | category | flops | bytes accessed | tf_op | source)
XLA Modules:
  0.0 434.4 jit_solution(3502312130298930524)
XLA Ops:
  10.7 6.2 %fusion.75 = f32[256,4608]{1,0:T(8,128)S(1)} fusion(bf16[256,1152]{1,0:T(8,128)(2,1)S(1)} %fusion.20.token_ref, bf16[1152,4608]{1,0:T(8,128)(2,1)} %param.21), kind=kOutput, calls=%fused_computation.159 | convolution fusion | flops 2717908992 | bytes 15925248 | tf_op jit(solution)/shard_map/dot_general | solution.py:383
  19.2 4.4 %collective-permute-start = (f32[3,2304]{1,0:T(4,128)S(1)}, f32[3,2304]{1,0:T(4,128)S(1)}, u32[]{:S(2)}, u32[]{:S(2)}) collective-permute-start(f32[3,2304]{1,0:T(4,128)S(1)} %bitcast.157), channel_id=1, source_target_pairs={{0,8},{8,16},{16,24},{24,32},{32,40},{40,48},{48,56},{56,64},{64,7... | collective-permute-start | bytes 82952 | tf_op jit(solution)/shard_map/ppermute | solution.py:769
  26.8 5.5 %all-to-all-start = ((bf16[8,64,1152]{2,1,0:T(8,128)(2,1)}), bf16[8,64,1152]{2,1,0:T(8,128)(2,1)}, u32[]{:S(2)}, u32[]{:S(2)}) async-start(bf16[8,64,1152]{2,1,0:T(8,128)(2,1)} %bitcast.12), calls=%async_computation | async-start | bytes 2359296 | tf_op jit(solution)/shard_map/all_to_all | solution.py:754
  35.9 5.9 %fusion.17 = (f32[256,2304]{1,0:T(8,128)S(1)}, f32[256,2304]{1,0:T(8,128)}) fusion(f32[256,2304]{1,0:T(8,128)} %slice.159, f32[2304]{0:T(1024)S(1)} %get-tuple-element.171, f32[24,2304]{1,0:T(8,128)S(1)} %maximum_bitcast_fusion, f32[2304]{0:T(1024)S(1)} %get-tuple-element.172, f32[2304]{0:T(1024)S(1)} %get-tuple-element.170, ...), kind=kLoop, calls=%fused_computation.47 | loop fusion | flops 8847360 | bytes 7345152 | tf_op jit(solution)/shard_map/jit(silu)/mul | solution.py:775
  45.5 10.4 %summary_earlier.1 = (f32[16,8,2304]{2,1,0:T(8,128)S(1)}, f32[8,2304]{1,0:T(8,128)S(1)}, f32[16,48,128]{2,1,0:T(8,128)S(1)}) custom-call(f32[256,2304]{1,0:T(8,128)S(1)} %get-tuple-element.185.step_ref, f32[256,2304]{1,0:T(8,128)S(1)} %get-tuple-element.177.other_ref.conv_ref, f32[256,128]{1,0:T(8,128)S(1)} %copy.143.sel_ref, f32[16,2304]{1,0:T(8,128)S(1)} %copy-done.9), custom_call_target="tpu_custom_call" | custom-call | tf_op jit(solution)/shard_map/summary_earlier/pallas_call | solution.py:298
  56.9 18.3 %exchange_earlier.1.in_ref = f32[16,24,128]{2,1,0:T(8,128)S(1)} custom-call(f32[16,48,128]{2,1,0:T(8,128)S(1)} %get-tuple-element.46.msg_ref, f32[16,24,128]{2,1,0:T(8,128)S(1)} %pad.21.log_ref), custom_call_target="tpu_custom_call" | custom-call | tf_op jit(solution)/shard_map/exchange_earlier/pallas_call | solution.py:311
  78.1 13.0 %scan_forward.1 = (f32[256,2304]{1,0:T(8,128)S(1)}, f32[16,8,2304]{2,1,0:T(8,128)S(1)}) custom-call(f32[256,2304]{1,0:T(8,128)S(1)} %copy-done.4, f32[256,2304]{1,0:T(8,128)S(1)} %get-tuple-element.177.other_ref.conv_ref, f32[256,128]{1,0:T(8,128)S(1)} %copy.143.sel_ref, f32[16,2304]{1,0:T(8,128)S(1)} %copy-done.9, f32[16,8,2304]{2,1,0:T(8,128)S(1)} %copy-done.18, ...), custom_call_target="tpu_custom_call" | custom-call | tf_op jit(solution)/shard_map/scan_forward/pallas_call | solution.py:330
  94.9 5.2 %multiply_reduce_fusion.7 = (f32[256]{0:T(256)S(1)}, f32[256,1152]{1,0:T(8,128)S(1)}) fusion(bf16[256,2304]{1,0:T(8,128)(2,1)S(1)} %multiply_convert_fusion.1.out_cols, bf16[2304,1152]{1,0:T(8,128)(2,1)} %param.29, f32[8,32,1152]{2,1,0:T(8,128)S(1)} %copy-done.30), kind=kOutput, calls=%fused_computation.68 | convolution fusion | flops 1359838976 | bytes 8848384 | tf_op jit(solution)/shard_map/dot_general | solution.py:383
  105.3 6.7 %all-to-all-start.1 = ((bf16[8,64,1280]{2,1,0:T(8,128)(2,1)}), bf16[8,64,1280]{2,1,0:T(8,128)(2,1)}, u32[]{:S(2)}, u32[]{:S(2)}) async-start(bf16[8,64,1280]{2,1,0:T(8,128)(2,1)} %bitcast.141), calls=%async_computation.1 | async-start | bytes 2621440 | tf_op jit(solution)/shard_map/all_to_all | solution.py:754
  115.0 6.1 %expert_pull.1.pull_ref = bf16[512,3072]{1,0:T(8,128)(2,1)S(1)} custom-call(bf16[512,1152]{1,0:T(8,128)(2,1)} %bitcast.13.up_ref, bf16[3072,1152]{1,0:T(8,128)(2,1)S(1)} %bitcast.132), custom_call_target="tpu_custom_call" | custom-call | flops 3623878656 | bytes 10223616 | tf_op jit(solution)/shard_map/expert_pull/pallas_call | solution.py:423
  122.8 7.1 %all-to-all-done.1 = bf16[8,64,1280]{2,1,0:T(8,128)(2,1)} async-done(((bf16[8,64,1280]{2,1,0:T(8,128)(2,1)}), bf16[8,64,1280]{2,1,0:T(8,128)(2,1)}, u32[]{:S(2)}, u32[]{:S(2)}) %all-to-all-start.1) | async-done | bytes 1310752 | tf_op jit(solution)/shard_map/all_to_all | solution.py:754
  130.0 21.1 %expert_layer.1 = (bf16[512,3072]{1,0:T(8,128)(2,1)}, bf16[512,3072]{1,0:T(8,128)(2,1)}, bf16[512,1152]{1,0:T(8,128)(2,1)S(1)}, bf16[512,1280]{1,0:T(8,128)(2,1)S(1)}) custom-call(bf16[512,1280]{1,0:T(8,128)(2,1)} %bitcast.16.got_ref.received_ref, bf16[512,1152]{1,0:T(8,128)(2,1)} %bitcast.13.up_ref, bf16[512,3072]{1,0:T(8,128)(2,1)} %copy-done.22, ...), custom_call_target="tpu_custom_call" | custom-call | flops 10871635968 | bytes 20447232 | tf_op jit(solution)/shard_map/expert_layer/pallas_call | solution.py:483
  153.1 5.0 %all-to-all-start.2 = ((bf16[8,64,1280]{2,1,0:T(8,128)(2,1)}), bf16[8,64,1280]{2,1,0:T(8,128)(2,1)}, u32[]{:S(2)}, u32[]{:S(2)}) async-start(bf16[8,64,1280]{2,1,0:T(8,128)(2,1)} %bitcast.129), calls=%async_computation.2 | async-start | bytes 2621440 | tf_op jit(solution)/shard_map/all_to_all | solution.py:754
  161.9 12.6 %expert_sums.1 = bf16[16,2,192,1152]{3,2,1,0:T(8,128)(2,1)S(1)} custom-call(bf16[512,3072]{1,0:T(8,128)(2,1)S(1)} %copy-done.24, bf16[512,1280]{1,0:T(8,128)(2,1)} %bitcast.16.got_ref.received_ref, bf16[512,3072]{1,0:T(8,128)(2,1)S(1)} %copy-done.23, bf16[512,1152]{1,0:T(8,128)(2,1)} %bitcast.13.up_ref), custom_call_target="tpu_custom_call" | custom-call | flops 7247757312 | bytes 20447232 | tf_op jit(solution)/shard_map/expert_sums/pallas_call | solution.py:534
  174.6 5.0 %copy-done.6 = bf16[16,2,192,1152]{3,2,1,0:T(8,128)(2,1)} copy-done((bf16[16,2,192,1152]{3,2,1,0:T(8,128)(2,1)}, bf16[16,2,192,1152]{3,2,1,0:T(8,128)(2,1)S(1)}, u32[]{:S(2)}) %copy-start.6) | copy-done | bytes 14155800
  184.5 7.6 %multiply_reduce_fusion = (f32[2304]{0:T(1024)S(1)}, f32[256,2304]{1,0:T(8,128)}, bf16[256,2304]{1,0:T(8,128)(2,1)}) fusion(f32[256,2304]{1,0:T(8,128)S(1)} %get-tuple-element.177.other_ref.conv_ref, f32[256,4608]{1,0:T(8,128)} %copy-done.28, f32[256,2304]{1,0:T(8,128)S(1)} %copy-done.12, f32[2304]{0:T(1024)S(1)} %copy-done.59, ...), kind=kOutput, calls=%fused_computation.35 | convolution fusion | flops 1368389376 | bytes 16533504 | tf_op jit(solution)/shard_map/tk,dk->td/dot_general | solution.py:387
  192.2 5.5 %all-to-all-start.3 = ((bf16[8,64,1152]{2,1,0:T(8,128)(2,1)}), bf16[8,64,1152]{2,1,0:T(8,128)(2,1)}, u32[]{:S(2)}, u32[]{:S(2)}) async-start(bf16[8,64,1152]{2,1,0:T(8,128)(2,1)} %bitcast.130), calls=%async_computation.3 | async-start | bytes 2359296 | tf_op jit(solution)/shard_map/all_to_all | solution.py:754
  199.4 10.0 %summary_later.1 = (f32[16,8,2304]{2,1,0:T(8,128)S(1)}, f32[8,2304]{1,0:T(8,128)S(1)}, f32[16,48,128]{2,1,0:T(8,128)S(1)}) custom-call(f32[256,2304]{1,0:T(8,128)S(1)} %copy-done.5, f32[256,2304]{1,0:T(8,128)S(1)} %copy-done.7, f32[256,128]{1,0:T(8,128)S(1)} %copy.143.sel_ref, f32[16,2304]{1,0:T(8,128)S(1)} %copy-done.9), custom_call_target="tpu_custom_call" | custom-call | tf_op jit(solution)/shard_map/summary_later/pallas_call | solution.py:298
  209.3 21.5 %exchange_later.1.in_ref = f32[16,24,128]{2,1,0:T(8,128)S(1)} custom-call(f32[16,48,128]{2,1,0:T(8,128)S(1)} %get-tuple-element.61.msg_ref, f32[16,24,128]{2,1,0:T(8,128)S(1)} %pad.21.log_ref), custom_call_target="tpu_custom_call" | custom-call | tf_op jit(solution)/shard_map/exchange_later/pallas_call | solution.py:311
  230.8 44.5 %scan_backward.1 = (f32[256,2304]{1,0:T(8,128)S(1)}, f32[256,2304]{1,0:T(8,128)S(1)}, f32[256,128]{1,0:T(8,128)S(1)}, f32[16,2304]{1,0:T(8,128)S(1)}) custom-call(f32[256,2304]{1,0:T(8,128)S(1)} %copy-done.5, f32[256,2304]{1,0:T(8,128)} %copy-done.1, f32[256,2304]{1,0:T(8,128)} %get-tuple-element.57.other_ref.grad_ref, f32[256,128]{1,0:T(8,128)S(1)} %copy.143.sel_ref, ...), custom_call_target="tpu_custom_call" | custom-call | tf_op jit(solution)/shard_map/scan_backward/pallas_call | solution.py:346
  298.2 8.1 %fusion.71 = (f32[2304]{0:T(1024)S(1)}, f32[2304]{0:T(1024)S(1)}, f32[2304]{0:T(1024)S(1)}, f32[2304]{0:T(1024)S(1)}, f32[2304]{0:T(1024)S(1)}, /*index=5*/bf16[256,2304]{1,0:T(8,128)(2,1)S(1)}) fusion(f32[256,2304]{1,0:T(8,128)} %copy-done.42, f32[256,4608]{1,0:T(8,128)} %copy-done.28, f32[256,2304]{1,0:T(8,128)} %slice.159, f32[24,2304]{1,0:T(8,128)S(1)} %copy-done.47, ...), kind=kLoop, calls=%fused_computation.156 | loop fusion | flops 13554432 | bytes 8782848 | tf_op jit(solution)/shard_map/reduce_sum | solution.py:844
  306.4 8.2 %fusion.26 = (f32[1152]{0:T(1024)S(1)}, f32[256]{0:T(256)S(1)}, f32[256,1152]{1,0:T(8,128)S(1)}) fusion(f32[8,32,1152]{2,1,0:T(8,128)S(1)} %copy-done.31, f32[256]{0:T(256)S(1)} %rsqrt.26, f32[1152]{0:T(1024)S(1)} %copy-done.57, bf16[1152,4608]{1,0:T(8,128)(2,1)} %param.21, bf16[256,2304]{1,0:T(8,128)(2,1)S(1)} %copy-done.48, ...), kind=kOutput, calls=%fused_computation.63 | convolution fusion | flops 2724395776 | bytes 15346688 | tf_op jit(solution)/shard_map/tk,dk->td/dot_general | solution.py:387
  326.6 8.4 %concatenate.47 = f32[2304,209]{1,0:T(8,128)S(1)} concatenate(f32[2304,104]{1,0:T(8,128)} %fusion.39, f32[2304,72]{1,0:T(8,128)} %fusion.34, f32[2304,16]{1,0:T(8,128)} %bitcast.136, f32[2304,1]{1,0:T(8,128)} %stack.23, f32[2304,1]{1,0:T(8,128)} %stack.24, f32[2304,1]{1,0:T(8,128)} %stack.25, f32[2304,1]{1,0:T(8,128)} %stack.26, f32[2304,1]{1,0:T(8,128)} %broadcast_in_dim.25, ...), dimensions={1} | concatenate | bytes 3852288 | tf_op jit(solution)/shard_map/concatenate | solution.py:875
  339.1 77.9 %shares.1 = f32[8,16,1152]{2,1,0:T(8,128)} custom-call(bf16[256,4608]{1,0:T(8,128)(2,1)} %pad_maximum_fusion.2.in_cols, bf16[256,1152]{1,0:T(8,128)(2,1)} %copy-done.44, bf16[256,2304]{1,0:T(8,128)(2,1)} %copy-done.41, bf16[256,1152]{1,0:T(8,128)(2,1)} %copy-done.45, f32[2304,256]{1,0:T(8,128)} %pad.24.small_ref), custom_call_target="tpu_custom_call" | custom-call | tf_op jit(solution)/shard_map/shares/pallas_call | solution.py:691
  (234 shorter events, 94.9 us)
Async XLA Ops:
  7.2 35.3 %copy-start = (bf16[72,2304]{1,0:T(8,128)(2,1)S(1)}, bf16[72,2304]{1,0:T(8,128)(2,1)}, u32[]{:S(2)}) copy-start(bf16[72,2304]{1,0:T(8,128)(2,1)} %param.25) | copy-start | bytes 995332
  9.7 7.3 %copy-start.29 = (f32[8,32,1152]{2,1,0:T(8,128)}, f32[8,32,1152]{2,1,0:T(8,128)S(1)}, u32[]{:S(2)}) copy-start(f32[8,32,1152]{2,1,0:T(8,128)S(1)} %convert.36) | copy-start | bytes 3538948
  10.7 13.4 %copy-start.60 = (s32[1,256,1]{1,2,0:T(1,128)S(1)}, s32[1,256,1]{1,2,0:T(1,128)}, u32[]{:S(2)}) copy-start(s32[1,256,1]{1,2,0:T(1,128)} %param.18) | copy-start | bytes 3076
  10.7 14.5 %copy-start.36 = (bf16[1,256,1152]{2,1,0:T(8,128)(2,1)S(1)}, bf16[1,256,1152]{2,1,0:T(8,128)(2,1)}, u32[]{:S(2)}) copy-start(bf16[1,256,1152]{2,1,0:T(8,128)(2,1)} %param.19) | copy-start | bytes 1769476
  19.1 13.2 %copy-start.56 = (f32[4,2304]{1,0:T(4,128)S(1)}, f32[4,2304]{1,0:T(4,128)}, u32[]{:S(2)}) copy-start(f32[4,2304]{1,0:T(4,128)} %param.22) | copy-start | bytes 110596
  19.2 16.6 %collective-permute-start = (f32[3,2304]{1,0:T(4,128)S(1)}, f32[3,2304]{1,0:T(4,128)S(1)}, u32[]{:S(2)}, u32[]{:S(2)}) collective-permute-start(f32[3,2304]{1,0:T(4,128)S(1)} %bitcast.157), channel_id=1, source_target_pairs={{0,8},{8,16},{16,24},{24,32},{32,40},{40,48},{48,56},{56,64},{64,7... | collective-permute-start | bytes 82952 | tf_op jit(solution)/shard_map/ppermute | solution.py:769
  26.8 48.3 %all-to-all-start = ((bf16[8,64,1152]{2,1,0:T(8,128)(2,1)}), bf16[8,64,1152]{2,1,0:T(8,128)(2,1)}, u32[]{:S(2)}, u32[]{:S(2)}) async-start(bf16[8,64,1152]{2,1,0:T(8,128)(2,1)} %bitcast.12), calls=%async_computation | async-start | bytes 2359296 | tf_op jit(solution)/shard_map/all_to_all | solution.py:754
  41.8 142.0 %copy-start.1 = (f32[256,2304]{1,0:T(8,128)}, f32[256,2304]{1,0:T(8,128)S(1)}, u32[]{:S(2)}) copy-start(f32[256,2304]{1,0:T(8,128)S(1)} %get-tuple-element.177.other_ref.conv_ref) | copy-start | bytes 7077892
  45.5 10.4 %copy-start.3 = (f32[256,2304]{1,0:T(8,128)}, f32[256,2304]{1,0:T(8,128)S(1)}, u32[]{:S(2)}) copy-start(f32[256,2304]{1,0:T(8,128)S(1)} %get-tuple-element.185.step_ref) | copy-start | bytes 7077892
  78.1 13.0 %copy-start.59 = (f32[2304]{0:T(1024)S(1)}, f32[2304]{0:T(1024)}, u32[]{:S(2)}) copy-start(f32[2304]{0:T(1024)} %param.28) | copy-start | bytes 27652
  94.9 7.2 %copy-start.55 = (bf16[1152,8]{0,1:T(8,128)(2,1)S(1)}, bf16[1152,8]{0,1:T(8,128)(2,1)}, u32[]{:S(2)}) copy-start(bf16[1152,8]{0,1:T(8,128)(2,1)} %param.31) | copy-start | bytes 55300
  105.3 24.6 %all-to-all-start.1 = ((bf16[8,64,1280]{2,1,0:T(8,128)(2,1)}), bf16[8,64,1280]{2,1,0:T(8,128)(2,1)}, u32[]{:S(2)}, u32[]{:S(2)}) async-start(bf16[8,64,1280]{2,1,0:T(8,128)(2,1)} %bitcast.141), calls=%async_computation.1 | async-start | bytes 2621440 | tf_op jit(solution)/shard_map/all_to_all | solution.py:754
  153.1 26.4 %all-to-all-start.2 = ((bf16[8,64,1280]{2,1,0:T(8,128)(2,1)}), bf16[8,64,1280]{2,1,0:T(8,128)(2,1)}, u32[]{:S(2)}, u32[]{:S(2)}) async-start(bf16[8,64,1280]{2,1,0:T(8,128)(2,1)} %bitcast.129), calls=%async_computation.2 | async-start | bytes 2621440 | tf_op jit(solution)/shard_map/all_to_all | solution.py:754
  158.2 181.0 %reduce-scatter.2.cloned.1.call-start = ((), (), s32[]{:S(2)}) async-start(), calls=%async_computation.5 | async-start | bytes 15040512 | tf_op jit(solution)/shard_map/reduce_scatter | solution.py:823
  184.5 7.6 %copy-start.45 = (bf16[256,1152]{1,0:T(8,128)(2,1)}, bf16[256,1152]{1,0:T(8,128)(2,1)S(1)}, u32[]{:S(2)}) copy-start(bf16[256,1152]{1,0:T(8,128)(2,1)S(1)} %fusion.69.middle_ref) | copy-start | bytes 1769476
  192.2 86.1 %all-to-all-start.3 = ((bf16[8,64,1152]{2,1,0:T(8,128)(2,1)}), bf16[8,64,1152]{2,1,0:T(8,128)(2,1)}, u32[]{:S(2)}, u32[]{:S(2)}) async-start(bf16[8,64,1152]{2,1,0:T(8,128)(2,1)} %bitcast.130), calls=%async_computation.3 | async-start | bytes 2359296 | tf_op jit(solution)/shard_map/all_to_all | solution.py:754
  199.4 31.5 %copy-start.16 = (f32[16,8,2304]{2,1,0:T(8,128)S(1)}, f32[16,8,2304]{2,1,0:T(8,128)}, u32[]{:S(2)}) copy-start(f32[16,8,2304]{2,1,0:T(8,128)} %copy-done.15) | copy-start | bytes 3538948
  285.4 12.7 %collective-permute-start.1 = (f32[3,2304]{1,0:T(4,128)S(1)}, f32[3,2304]{1,0:T(4,128)S(1)}, u32[]{:S(2)}, u32[]{:S(2)}) collective-permute-start(f32[3,2304]{1,0:T(4,128)S(1)} %bitcast.156), channel_id=1, source_target_pairs={{8,0},{16,8},{24,16},{32,24},{40,32},{48,40},{56,48},{64,56},{72,6... | collective-permute-start | bytes 82952 | tf_op jit(solution)/shard_map/ppermute | solution.py:849
  298.2 8.1 %copy-start.31 = (f32[8,32,1152]{2,1,0:T(8,128)S(1)}, f32[8,32,1152]{2,1,0:T(8,128)}, u32[]{:S(2)}) copy-start(f32[8,32,1152]{2,1,0:T(8,128)} %copy-done.29) | copy-start | bytes 3538948
  298.2 8.1 %copy-start.48 = (bf16[256,2304]{1,0:T(8,128)(2,1)S(1)}, bf16[256,2304]{1,0:T(8,128)(2,1)}, u32[]{:S(2)}) copy-start(bf16[256,2304]{1,0:T(8,128)(2,1)} %get-tuple-element.179) | copy-start | bytes 3538948
  306.3 8.3 %copy-start.39 = (bf16[256,2304]{1,0:T(8,128)(2,1)}, bf16[256,2304]{1,0:T(8,128)(2,1)S(1)}, u32[]{:S(2)}) copy-start(bf16[256,2304]{1,0:T(8,128)(2,1)S(1)} %get-tuple-element.180) | copy-start | bytes 3538948
  306.3 8.3 %copy-start.33 = (f32[256,1152]{1,0:T(8,128)S(1)}, f32[256,1152]{1,0:T(8,128)}, u32[]{:S(2)}) copy-start(f32[256,1152]{1,0:T(8,128)} %copy-done.32) | copy-start | bytes 3538948
  306.4 8.3 %copy-start.38 = (bf16[1,256,1152]{2,1,0:T(8,128)(2,1)S(1)}, bf16[1,256,1152]{2,1,0:T(8,128)(2,1)}, u32[]{:S(2)}) copy-start(bf16[1,256,1152]{2,1,0:T(8,128)(2,1)} %param.19) | copy-start | bytes 1769476
  339.1 85.5 %copy-start.50 = (bf16[384,1152]{1,0:T(8,128)(2,1)S(1)}, bf16[384,1152]{1,0:T(8,128)(2,1)}, u32[]{:S(2)}) copy-start(bf16[384,1152]{1,0:T(8,128)(2,1)} %reduce-scatter.2.cloned.1.call-done) | copy-start | bytes 2654212
  (45 other events, 133.1 us)
Sparse Core Ops, SparseCore 0:
  192.3 103.6 reduce-scatter.1

commit v3 on v2

v3 whole, which is shorter than its diff:
```python
import functools
import math

import jax
import jax.numpy as jnp
from jax import lax
from jax.experimental import pallas as pl
from jax.experimental.pallas import tpu as pltpu
from jax.sharding import PartitionSpec as P

LANES = 128
SEGS = 8
LOG2E = math.log2(math.e)
PARTS = 3
GRID = 4


def spread_ones(states):
    row = lax.broadcasted_iota(jnp.int32, (LANES, states * LANES), 0)
    lane = lax.broadcasted_iota(jnp.int32, (LANES, states * LANES), 1)
    return row, lane // LANES


def fill_maps(sel_ref, wide_ref, column):
    steps, states = wide_ref.shape[:2]
    row, block = spread_ones(states)
    ones = jnp.where(row == block + column, 1.0, 0.0).astype(jnp.bfloat16)
    left, total = sel_ref[...], None
    for unused in range(3):
        part = left.astype(jnp.bfloat16)
        left = left - part.astype(jnp.float32)
        spread = jnp.dot(part, ones, preferred_element_type=jnp.float32)
        total = spread if total is None else total + spread
    for n in range(states):
        wide_ref[:, n] = total[:, n * LANES : (n + 1) * LANES].reshape(steps, SEGS, LANES)


def gather_maps(sum_ref, column):
    steps, states = sum_ref.shape[:2]
    row, block = spread_ones(states)
    ones = jnp.where(row == block + column, 1.0, 0.0).astype(jnp.bfloat16)
    left = jnp.concatenate([sum_ref[:, n].reshape(steps * SEGS, LANES) for n in range(states)], axis=1)
    total = None
    for unused in range(3):
        part = left.astype(jnp.bfloat16)
        left = left - part.astype(jnp.float32)
        summed = transposed_dot(part, ones)
        total = summed if total is None else total + summed
    return total


def lanes_of(block):
    return pl.ds(pl.multiple_of(block * LANES, LANES), LANES)


def rows_of(j):
    return pl.ds(pl.multiple_of(j * SEGS, SEGS), SEGS)


def rates_of(log_ref, lanes):
    states = log_ref.shape[0]
    rate = -LOG2E * jnp.exp(log_ref[:, lanes])
    return jnp.stack([jnp.broadcast_to(rate[n : n + 1], (SEGS, LANES)) for n in range(states)])


def neighbour(value, hop, later, fill):
    axis = value.ndim - 2
    place = lax.broadcasted_iota(jnp.int32, value.shape, axis)
    if later:
        return jnp.where(place < SEGS - hop, pltpu.roll(value, SEGS - hop, axis), fill)
    return jnp.where(place >= hop, pltpu.roll(value, hop, axis), fill)


def summarize(later, part, step_ref, other_ref, wide, log_ref, part_ref, span_ref, message):
    steps, states = wide.shape[:2]
    blocks = step_ref.shape[1] // LANES // PARTS

    def block(i, unused):
        lanes = lanes_of(part * blocks + i)
        rate = rates_of(log_ref, lanes)

        def advance(turn, carry):
            span, memory = carry
            j = steps - 1 - turn if later else turn
            step = step_ref[rows_of(j), lanes]
            other = other_ref[rows_of(j), lanes]
            decay = jnp.exp2(step * rate)
            if later:
                memory = decay * (memory + wide[j] * other)
            else:
                memory = decay * memory + wide[j] * (step * other)
            return span + step, memory

        zero = jnp.zeros((SEGS, LANES), jnp.float32)
        span, memory = lax.fori_loop(0, steps, advance, (zero, jnp.zeros(rate.shape, jnp.float32)), unroll=8)
        hop = 1
        while hop < SEGS:
            memory = memory + jnp.exp2(rate * span) * neighbour(memory, hop, later, 0.0)
            span = span + neighbour(span, hop, later, 0.0)
            hop *= 2
        span_ref[:, lanes] = span
        part_ref[:, :, lanes] = memory
        end = 0 if later else SEGS - 1
        for n in range(states):
            message[n // GRID, n % GRID, pl.ds(i, 1), :] = memory[n, end : end + 1]
        for q in range(GRID):
            message[q, GRID, pl.ds(i, 1), :] = span[end : end + 1]
        return unused

    lax.fori_loop(0, blocks, block, 0)


def entering(later, part_ref, span_ref, rate, lanes, carried):
    ends = part_ref[:, :, lanes] + jnp.exp2(rate * span_ref[:, lanes]) * carried
    return neighbour(ends, 1, later, carried)


def carried_at(in_ref, part, i):
    states = GRID * GRID
    return jnp.stack(
        [jnp.broadcast_to(in_ref[n // GRID, n % GRID, pl.ds(i, 1), :], (SEGS, LANES)) for n in range(states)]
    )


def scan_part(part, step_ref, conv_ref, wide_in, wide_out, log_ref, part_ref, span_ref, in_ref, y_ref, entry_ref):
    steps = wide_in.shape[0]
    blocks = step_ref.shape[1] // LANES // PARTS

    def block(i, unused):
        lanes = lanes_of(part * blocks + i)
        rate = rates_of(log_ref, lanes)
        first = entering(False, part_ref, span_ref, rate, lanes, carried_at(in_ref, part, i))
        entry_ref[:, :, lanes] = first

        def advance(j, memory):
            step = step_ref[rows_of(j), lanes]
            memory = jnp.exp2(step * rate) * memory + wide_in[j] * (step * conv_ref[rows_of(j), lanes])
            y_ref[rows_of(j), lanes] = jnp.sum(wide_out[j] * memory, axis=0)
            return memory

        lax.fori_loop(0, steps, advance, first, unroll=8)
        return unused

    lax.fori_loop(0, blocks, block, 0)


def retreat_part(
    part, step_ref, conv_ref, grad_ref, raw_ref, wide_in, wide_out, log_ref, pull_ref, entry_ref, part_ref, span_ref, in_ref,
    low_ref, gconv_ref, glog_ref, gbias_ref, sum_in, sum_out, states_ref, decays_ref, raw_sum, raw_rows,
):
    steps = wide_in.shape[0]
    blocks = step_ref.shape[1] // LANES // PARTS

    def block(i, unused):
        lanes = lanes_of(part * blocks + i)
        rate = rates_of(log_ref, lanes)

        def advance(j, memory):
            step = step_ref[rows_of(j), lanes]
            decay = jnp.exp2(step * rate)
            memory = decay * memory + wide_in[j] * (step * conv_ref[rows_of(j), lanes])
            decays_ref[j] = decay
            states_ref[j + 1] = memory
            return memory

        first = entry_ref[:, :, lanes]
        states_ref[0] = first
        lax.fori_loop(0, steps, advance, first, unroll=8)

        def retreat(turn, carry):
            j = steps - 1 - turn
            mu, slow = carry
            step = step_ref[rows_of(j), lanes]
            conv = conv_ref[rows_of(j), lanes]
            grad = grad_ref[rows_of(j), lanes]
            lam = wide_out[j] * grad + mu
            sum_out[j] += grad * states_ref[j + 1]
            sum_in[j] += lam * (step * conv)
            by_in = jnp.sum(lam * wide_in[j], axis=0)
            mu = lam * decays_ref[j]
            kept = mu * states_ref[j]
            by_rate = jnp.sum(kept * rate, axis=0)
            grad_step = by_in * conv + (1.0 / LOG2E) * by_rate
            raw_rows[rows_of(j), :] = grad_step * jax.nn.sigmoid(raw_ref[rows_of(j), lanes])
            gconv_ref[rows_of(j), lanes] = by_in * step
            return mu, slow + kept * step

        last = entering(True, part_ref, span_ref, rate, lanes, carried_at(in_ref, part, i))
        unused_mu, slow = lax.fori_loop(0, steps, retreat, (last, jnp.zeros(rate.shape, jnp.float32)), unroll=4)
        glog_ref[:, lanes] = (1.0 / LOG2E) * jnp.sum(slow * rate, axis=1)
        raw_steps = raw_rows[...]
        gbias_ref[:, lanes] = jnp.sum(raw_steps, axis=0, keepdims=True)
        low = raw_steps.astype(jnp.bfloat16)
        low_ref[:, lanes] = low
        raw_sum[...] += transposed_dot(low, pull_ref[:, lanes])
        return unused

    lax.fori_loop(0, blocks, block, 0)


class Relay:
    def __init__(self, later, log_rows, message, got, row, rows_got, above, made, in_ref, sends, arrivals):
        self.later, self.log_rows, self.message, self.got = later, log_rows, message, got
        self.row, self.rows_got, self.above, self.made, self.in_ref = row, rows_got, above, made, in_ref
        self.sends, self.arrivals = sends, arrivals
        seq = lax.axis_index("seq")
        self.y, self.z = lax.div(seq, GRID), lax.rem(seq, GRID)
        self.flying = {}
        barrier = pltpu.get_barrier_semaphore()
        for k in range(1, GRID):
            for peer in (self.across(k), self.along(k)):
                pl.semaphore_signal(barrier, inc=1, device_id=peer, device_id_type=pl.DeviceIdType.MESH)

    def across(self, k):
        return {"seq": self.y * GRID + lax.rem(self.z + k, GRID)}

    def along(self, k):
        return {"seq": lax.rem(self.y + k, GRID) * GRID + self.z}

    def meet(self):
        pl.semaphore_wait(pltpu.get_barrier_semaphore(), 2 * (GRID - 1))

    def send(self, part, phase, k, source, target, peer):
        copy = pltpu.make_async_remote_copy(
            src_ref=source, dst_ref=target, send_sem=self.sends.at[part, phase, k], recv_sem=self.arrivals.at[part, phase, k],
            device_id=peer, device_id_type=pl.DeviceIdType.MESH,
        )
        copy.start()
        self.flying.setdefault((part, phase), []).append(copy)

    def land(self, part, phase):
        for copy in self.flying[part, phase]:
            copy.wait()

    def order(self):
        return range(GRID - 1, -1, -1) if self.later else range(GRID)

    def rate(self, part):
        return -LOG2E * jnp.exp(self.log_rows[part, self.z])

    def first(self, part):
        for k in range(1, GRID):
            peer = lax.rem(self.z + k, GRID)
            self.send(part, 0, k, self.message.at[part, peer], self.got.at[part, k], self.across(k))
        self.got[part, 0] = self.message[part, self.z]

    def second(self, part):
        self.land(part, 0)
        rate = self.rate(part)
        state, span = jnp.zeros(rate.shape, jnp.float32), jnp.zeros(rate.shape[1:], jnp.float32)
        for z in self.order():
            block = self.got[part, lax.rem(self.z - z + GRID, GRID)]
            state = jnp.exp2(rate * block[GRID]) * state + block[:GRID]
            span = span + block[GRID]
        self.row[part, :GRID] = state
        self.row[part, GRID] = span
        for k in range(1, GRID):
            self.send(part, 1, k, self.row.at[part], self.rows_got.at[part, k], self.along(k))
        self.rows_got[part, 0] = self.row[part]

    def third(self, part):
        self.land(part, 1)
        rate = self.rate(part)
        state = jnp.zeros(rate.shape, jnp.float32)
        for y in self.order():
            self.above[part, y] = state
            block = self.rows_got[part, lax.rem(self.y - y + GRID, GRID)]
            state = jnp.exp2(rate * block[GRID]) * state + block[:GRID]
        state = self.above[part, self.y]
        for z in self.order():
            self.made[part, z] = state
            block = self.got[part, lax.rem(self.z - z + GRID, GRID)]
            state = jnp.exp2(rate * block[GRID]) * state + block[:GRID]
        for k in range(1, GRID):
            peer = lax.rem(self.z + k, GRID)
            self.send(part, 2, k, self.made.at[part, peer], self.in_ref.at[part, self.z], self.across(k))
        self.in_ref[part, self.z] = self.made[part, self.z]

    def done(self, part):
        self.land(part, 2)


def staged(relay, summary, extra, scan):
    summary(0)
    relay.meet()
    relay.first(0)
    summary(1)
    relay.first(1)
    relay.second(0)
    summary(2)
    relay.first(2)
    relay.third(0)
    relay.second(1)
    extra()
    relay.second(2)
    relay.third(1)
    relay.done(0)
    scan(0)
    relay.third(2)
    relay.done(1)
    scan(1)
    relay.done(2)
    scan(2)


def forward_kernel(
    column, step_ref, conv_ref, sel_ref, log_ref, log_rows, y_ref, entry_ref, part_ref, span_ref, wide_in, wide_out, in_ref, *relayed
):
    states = log_ref.shape[0]
    relay = Relay(False, log_rows, *relayed[:6], in_ref, *relayed[6:])
    message = relayed[0]
    fill_maps(sel_ref, wide_in, column)

    def summary(part):
        summarize(False, part, step_ref, conv_ref, wide_in, log_ref, part_ref, span_ref, message.at[part])

    def scan(part):
        scan_part(part, step_ref, conv_ref, wide_in, wide_out, log_ref, part_ref, span_ref, in_ref.at[part], y_ref, entry_ref)

    staged(relay, summary, lambda: fill_maps(sel_ref, wide_out, column + states), scan)


def backward_kernel(
    column, step_ref, conv_ref, grad_ref, raw_ref, sel_ref, log_ref, log_rows, pull_ref, entry_ref,
    low_ref, gconv_ref, gsel_ref, glog_ref, gbias_ref,
    part_ref, span_ref, wide_in, wide_out, sum_in, sum_out, states_ref, decays_ref, raw_sum, raw_rows, in_ref, *relayed
):
    states = log_ref.shape[0]
    relay = Relay(True, log_rows, *relayed[:6], in_ref, *relayed[6:])
    message = relayed[0]
    fill_maps(sel_ref, wide_out, column + states)

    def summary(part):
        summarize(True, part, step_ref, grad_ref, wide_out, log_ref, part_ref, span_ref, message.at[part])

    def prepare():
        fill_maps(sel_ref, wide_in, column)
        sum_in[...] = jnp.zeros_like(sum_in)
        sum_out[...] = jnp.zeros_like(sum_out)
        raw_sum[...] = jnp.zeros_like(raw_sum)

    def scan(part):
        retreat_part(
            part, step_ref, conv_ref, grad_ref, raw_ref, wide_in, wide_out, log_ref, pull_ref, entry_ref, part_ref, span_ref,
            in_ref.at[part], low_ref, gconv_ref, glog_ref, gbias_ref, sum_in, sum_out, states_ref, decays_ref, raw_sum, raw_rows,
        )

    staged(relay, summary, prepare, scan)
    maps = gather_maps(sum_in, column) + gather_maps(sum_out, column + states)
    gsel_ref[...] = (raw_sum[...] + maps).astype(jnp.bfloat16)


WHOLE = pl.BlockSpec(memory_space=pltpu.VMEM)


def shaped(*dims, dtype=jnp.float32):
    return jax.ShapeDtypeStruct(dims, dtype)


def roomy(mebibytes, **more):
    return pltpu.CompilerParams(vmem_limit_bytes=mebibytes << 20, **more)


def wide_scratch(rows, states, extra=0):
    return pltpu.VMEM((rows // SEGS + extra, states, SEGS, LANES), jnp.float32)


def chain_scratch(states, width):
    return [pltpu.VMEM((states, SEGS, width), jnp.float32), pltpu.VMEM((SEGS, width), jnp.float32)]


def relay_scratch():
    def kept(*dims):
        return pltpu.VMEM((PARTS,) + dims + (SEGS, LANES), jnp.float32)

    return [
        kept(GRID, GRID),
        kept(GRID, GRID + 1),
        kept(GRID, GRID + 1),
        kept(GRID + 1),
        kept(GRID, GRID + 1),
        kept(GRID, GRID),
        kept(GRID, GRID),
        pltpu.SemaphoreType.DMA((PARTS, 3, GRID)),
        pltpu.SemaphoreType.DMA((PARTS, 3, GRID)),
    ]


def scan_forward(step, conv, selection, decay_log, log_rows, column):
    rows, width = step.shape
    states = decay_log.shape[0]
    return pl.pallas_call(
        functools.partial(forward_kernel, column),
        out_shape=(shaped(rows, width), shaped(states, SEGS, width)),
        in_specs=[WHOLE] * 5,
        out_specs=(WHOLE,) * 2,
        scratch_shapes=chain_scratch(states, width) + [wide_scratch(rows, states)] * 2 + relay_scratch(),
        compiler_params=roomy(32, collective_id=0, has_side_effects=True),
        name="scan_forward",
    )(step, conv, selection, decay_log, log_rows)


def scan_backward(step, conv, grad, raw, selection, decay_log, log_rows, pull, first, column):
    rows, width = step.shape
    states = decay_log.shape[0]
    narrow = pltpu.VMEM((rows, LANES), jnp.float32)
    return pl.pallas_call(
        functools.partial(backward_kernel, column),
        out_shape=(
            shaped(rows, width, dtype=jnp.bfloat16),
            shaped(rows, width),
            shaped(rows, LANES, dtype=jnp.bfloat16),
            shaped(states, width),
            shaped(1, width),
        ),
        in_specs=[WHOLE] * 9,
        out_specs=(WHOLE,) * 5,
        scratch_shapes=chain_scratch(states, width)
        + [wide_scratch(rows, states)] * 4
        + [wide_scratch(rows, states, 1), wide_scratch(rows, states)]
        + [narrow] * 2
        + relay_scratch(),
        compiler_params=roomy(46, collective_id=1, has_side_effects=True),
        name="scan_backward",
    )(step, conv, grad, raw, selection, decay_log, log_rows, pull, first)


def segmented(block):
    rows = block.shape[0]
    return block.reshape(SEGS, rows // SEGS, -1).transpose(1, 0, 2).reshape(rows, -1)


def in_order(block):
    rows = block.shape[0]
    return block.reshape(rows // SEGS, SEGS, -1).transpose(1, 0, 2).reshape(rows, -1)


def rms_scale(stream):
    return lax.rsqrt(jnp.mean(stream * stream, axis=-1, keepdims=True) + 1e-05)


def rms_back(stream, scale, gain, grad):
    grown = grad * gain
    along = jnp.mean(stream * grown, axis=-1, keepdims=True)
    return scale * grown - stream * (scale * scale * scale * along), jnp.sum(grad * stream * scale, axis=0)


def silu_slope(value):
    gate = jax.nn.sigmoid(value)
    return gate * (1.0 + value * (1.0 - gate))


def product(left, right):
    return jnp.dot(left, right, preferred_element_type=jnp.float32)


def across(left, right):
    return jnp.einsum("tk,dk->td", left, right, preferred_element_type=jnp.float32)


def summed_rows(left, right):
    return jnp.einsum("tk,td->kd", left, right, preferred_element_type=jnp.float32)


CHUNK = 1024
GELU_OUT = math.sqrt(2.0 / math.pi)
GELU_IN = 0.044715


def transposed_dot(left, right):
    return lax.dot_general(left, right, (((1,), (1,)), ((), ())), preferred_element_type=jnp.float32)


def column_dot(left, right):
    return lax.dot_general(left, right, (((0,), (0,)), ((), ())), preferred_element_type=jnp.float32)


def three_parts(value):
    parts, left = [], value
    for unused in range(3):
        part = left.astype(jnp.bfloat16)
        left = left - part.astype(jnp.float32)
        parts.append(part)
    return parts


def expert_pull_kernel(up_ref, second_ref, pull_ref):
    pull_ref[...] = transposed_dot(up_ref[...], second_ref[...]).astype(jnp.bfloat16)


def expert_pull(upstream, second):
    rows, width = upstream.shape
    hidden = second.shape[0]
    return pl.pallas_call(
        expert_pull_kernel,
        grid=(hidden // CHUNK,),
        out_shape=shaped(rows, hidden, dtype=jnp.bfloat16),
        in_specs=[pl.BlockSpec((rows, width), lambda i: (0, 0)), pl.BlockSpec((CHUNK, width), lambda i: (i, 0))],
        out_specs=pl.BlockSpec((rows, CHUNK), lambda i: (0, i)),
        compiler_params=roomy(60),
        cost_estimate=pl.CostEstimate(flops=2 * rows * hidden * width, bytes_accessed=2 * (width + rows) * hidden, transcendentals=0),
        name="expert_pull",
    )(upstream, second)


def expert_kernel(got_ref, up_ref, pull_ref, first_ref, second_ref, active_ref, grad_ref, value_ref, sent_ref, value, sent):
    step, last = pl.program_id(0), pl.num_programs(0) - 1
    width = up_ref.shape[1]
    first = first_ref[...]
    pre = jnp.dot(got_ref[:, :width], first, preferred_element_type=jnp.float32)
    square = pre * pre
    bent = jnp.tanh(pre * (GELU_OUT + GELU_OUT * GELU_IN * square))
    share = 0.5 + 0.5 * bent
    active = (pre * share).astype(jnp.bfloat16)
    slope = share + pre * (0.5 - 0.5 * bent * bent) * (GELU_OUT + 3.0 * GELU_OUT * GELU_IN * square)
    grad = (slope * pull_ref[...].astype(jnp.float32)).astype(jnp.bfloat16)
    active_ref[...] = active
    grad_ref[...] = grad
    more_value = jnp.dot(active, second_ref[...], preferred_element_type=jnp.float32)
    more_sent = transposed_dot(grad, first)

    @pl.when(step == 0)
    def begin():
        value[...] = more_value
        sent[...] = more_sent

    @pl.when(step > 0)
    def go_on():
        value[...] += more_value
        sent[...] += more_sent

    @pl.when(step == last)
    def finish():
        low = value[...].astype(jnp.bfloat16)
        value_ref[...] = low
        sent_ref[:, :width] = sent[...].astype(jnp.bfloat16)
        along = jnp.sum(low.astype(jnp.float32) * up_ref[...].astype(jnp.float32), axis=1, keepdims=True)
        place = lax.broadcasted_iota(jnp.int32, (sent_ref.shape[0], LANES), 1)
        tail = jnp.zeros(place.shape, jnp.float32)
        for k, part in enumerate(three_parts(along)):
            tail = jnp.where(place == k, part.astype(jnp.float32), tail)
        sent_ref[:, width:] = tail.astype(jnp.bfloat16)


def expert_layer(received, upstream, pull, first, second):
    rows, width = upstream.shape
    hidden = second.shape[0]
    wide = received.shape[1]

    def fixed(cols):
        return pl.BlockSpec((rows, cols), lambda i: (0, 0))

    chunk = pl.BlockSpec((rows, CHUNK), lambda i: (0, i))
    return pl.pallas_call(
        expert_kernel,
        grid=(hidden // CHUNK,),
        out_shape=(
            shaped(rows, hidden, dtype=jnp.bfloat16),
            shaped(rows, hidden, dtype=jnp.bfloat16),
            shaped(rows, width, dtype=jnp.bfloat16),
            shaped(rows, wide, dtype=jnp.bfloat16),
        ),
        in_specs=[
            fixed(wide),
            fixed(width),
            chunk,
            pl.BlockSpec((width, CHUNK), lambda i: (0, i)),
            pl.BlockSpec((CHUNK, width), lambda i: (i, 0)),
        ],
        out_specs=(chunk, chunk, fixed(width), fixed(wide)),
        scratch_shapes=[pltpu.VMEM((rows, width), jnp.float32)] * 2,
        compiler_params=roomy(60),
        cost_estimate=pl.CostEstimate(flops=6 * rows * hidden * width, bytes_accessed=4 * hidden * (width + rows), transcendentals=rows * hidden),
        name="expert_layer",
    )(received, upstream, pull, first, second)


def expert_sums_kernel(hidden_ref, received_ref, active_ref, up_ref, out_ref, scaled_received, scaled_up):
    pair = out_ref.shape[0]
    half = out_ref.shape[2]
    width = up_ref.shape[1]

    @pl.when(pl.program_id(0) == 0)
    def scale():
        parts = received_ref[:, width:].astype(jnp.float32)
        gate = parts[:, 0:1] + parts[:, 1:2] + parts[:, 2:3]
        scaled_received[...] = (received_ref[:, :width].astype(jnp.float32) * gate).astype(jnp.bfloat16)
        scaled_up[...] = (up_ref[...].astype(jnp.float32) * gate).astype(jnp.bfloat16)

    for which, (left_ref, right_ref) in enumerate(((hidden_ref, scaled_received), (active_ref, scaled_up))):
        total = column_dot(left_ref[...], right_ref[...]).astype(jnp.bfloat16)
        for i in range(pair):
            out_ref[i, which] = total[i * half : (i + 1) * half]


def expert_sums(grad_hidden, received, activated, upstream, owners):
    rows, hidden = grad_hidden.shape
    width = upstream.shape[1]
    pair = 2
    chunk = pl.BlockSpec((rows, pair * hidden // owners), lambda i: (0, i))

    def fixed(cols):
        return pl.BlockSpec((rows, cols), lambda i: (0, 0))

    return pl.pallas_call(
        expert_sums_kernel,
        grid=(owners // pair,),
        out_shape=shaped(owners, 2, hidden // owners, width, dtype=jnp.bfloat16),
        in_specs=[chunk, fixed(received.shape[1]), chunk, fixed(width)],
        out_specs=pl.BlockSpec((pair, 2, hidden // owners, width), lambda i: (i, 0, 0, 0)),
        scratch_shapes=[pltpu.VMEM((rows, width), jnp.bfloat16)] * 2,
        compiler_params=roomy(60),
        cost_estimate=pl.CostEstimate(flops=4 * rows * hidden * width, bytes_accessed=4 * hidden * (width + rows), transcendentals=0),
        name="expert_sums",
    )(grad_hidden, received, activated, upstream)


SELECTED = 104
BAND = 384


def conv_back_kernel(
    taps, gsel_ref, sel_ref, low_ref, gconv_ref, mixer_ref, conv_ref, pre_ref, padded_ref, weight_ref, skip_ref, glog_ref, gbias_ref,
    gpre_ref, left_ref, right_ref, rows_ref,
):
    rows = gconv_ref.shape[0]
    states = glog_ref.shape[0]
    gsel = gsel_ref[...]
    rank = SELECTED - 2 * states
    place = lax.broadcasted_iota(jnp.int32, sel_ref.shape, 1)
    step_low = jnp.where(place < rank, sel_ref[...], 0.0).astype(jnp.bfloat16)
    tall = lax.broadcasted_iota(jnp.int32, (rows_ref.shape[0], LANES), 0)
    wide = lax.broadcasted_iota(jnp.int32, (rows_ref.shape[0], LANES), 1)
    spots = jnp.where(wide == tall + SELECTED, 1.0, 0.0).astype(jnp.bfloat16)
    rows_ref[...] = jnp.zeros_like(rows_ref)
    rows_ref[:states, :] = glog_ref[...]
    for b in range(BAND // LANES):
        lanes = pl.ds(b * LANES, LANES)
        mixer = mixer_ref[:, lanes]
        conv = conv_ref[:, lanes]
        pre = pre_ref[:, lanes]
        grad = transposed_dot(gsel, weight_ref[pl.ds(b * LANES, LANES), :]) + gconv_ref[:, lanes] + skip_ref[:, lanes] * mixer
        grad = grad * silu_slope(pre)
        gpre_ref[:, lanes] = grad
        for k in range(taps):
            rows_ref[states + k : states + k + 1, lanes] = jnp.sum(grad * padded_ref[k * SEGS : k * SEGS + rows, lanes], axis=0, keepdims=True)
        rows_ref[states + taps : states + taps + 1, lanes] = jnp.sum(grad, axis=0, keepdims=True)
        rows_ref[states + taps + 1 : states + taps + 2, lanes] = gbias_ref[:, lanes]
        rows_ref[states + taps + 2 : states + taps + 3, lanes] = jnp.sum(mixer * conv, axis=0, keepdims=True)
        total = column_dot(conv.astype(jnp.bfloat16), gsel)
        for part in three_parts(rows_ref[:, lanes]):
            total = total + column_dot(part, spots)
        left_ref[pl.ds(b * LANES, LANES), :] = total
        right_ref[pl.ds(b * LANES, LANES), :] = column_dot(low_ref[:, lanes], step_low)


def conv_back(gsel, selection, low, grad_conv, grad_mixer, conv, preact, padded, weight, skip, grad_log, grad_bias, taps):
    rows, width = grad_conv.shape

    def band(height):
        return pl.BlockSpec((height, BAND), lambda i: (0, i))

    whole = pl.BlockSpec((rows, LANES), lambda i: (0, 0))
    down = pl.BlockSpec((BAND, LANES), lambda i: (i, 0))
    return pl.pallas_call(
        functools.partial(conv_back_kernel, taps),
        grid=(width // BAND,),
        out_shape=(shaped(rows, width), shaped(width, LANES), shaped(width, LANES)),
        in_specs=[whole, whole]
        + [band(rows)] * 5
        + [band(padded.shape[0]), down, band(1), band(grad_log.shape[0]), band(1)],
        out_specs=(band(rows), down, down),
        scratch_shapes=[pltpu.VMEM((24, BAND), jnp.float32)],
        compiler_params=roomy(60),
        name="conv_back",
    )(gsel, selection, low, grad_conv, grad_mixer, conv, preact, padded, weight, skip, grad_log, grad_bias)


CUT = 768


def token_back_kernel(taps, gpre_ref, next_ref, tap_ref, gate_ref, weight_ref, stream_ref, gain_ref, middle_ref, gconv_ref, token_ref, ggain_ref, total):
    step, last = pl.program_id(0), pl.num_programs(0) - 1
    half = pl.num_programs(0) // 2
    rows = gpre_ref.shape[0]

    def more(piece):
        summed = transposed_dot(piece, weight_ref[...])

        @pl.when(step == 0)
        def begin():
            total[...] = summed

        @pl.when(step > 0)
        def go_on():
            total[...] += summed

    @pl.when(step < half)
    def conv_part():
        place = lax.broadcasted_iota(jnp.int32, (SEGS, CUT), 0)
        grown = None
        for k in range(taps):
            late = taps - 1 - k
            shifted = gpre_ref[late * SEGS :, :]
            if late:
                wrapped = [
                    jnp.where(place == SEGS - 1, next_ref[j : j + 1, :], pltpu.roll(gpre_ref[j * SEGS : (j + 1) * SEGS, :], SEGS - 1, 0))
                    for j in range(late)
                ]
                shifted = jnp.concatenate([shifted] + wrapped, axis=0)
            term = tap_ref[k : k + 1, :] * shifted
            grown = term if grown is None else grown + term
        piece = grown.astype(jnp.bfloat16)
        gconv_ref[...] = piece
        more(piece)

    @pl.when(step >= half)
    def gate_part():
        more(gate_ref[...])

    @pl.when(step == last)
    def finish():
        stream = stream_ref[...].astype(jnp.float32)
        scale = rms_scale(stream)
        back, gain = rms_back(stream, scale, gain_ref[...], total[...])
        token_ref[...] = middle_ref[...] + back
        ggain_ref[...] = gain[None, :]


def token_back(grad_preact, following, taps, grad_gate, in_weight, stream, gain, grad_middle):
    rows, width = grad_preact.shape
    model = stream.shape[1]
    half = width // CUT

    def early(height):
        return pl.BlockSpec((height, CUT), lambda i: (0, jnp.minimum(i, half - 1)))

    fixed = pl.BlockSpec((rows, model), lambda i: (0, 0))
    row = pl.BlockSpec((1, model), lambda i: (0, 0))
    return pl.pallas_call(
        functools.partial(token_back_kernel, taps.shape[0]),
        grid=(2 * half,),
        out_shape=(shaped(rows, width, dtype=jnp.bfloat16), shaped(rows, model), shaped(1, model)),
        in_specs=[
            early(rows),
            early(following.shape[0]),
            early(taps.shape[0]),
            pl.BlockSpec((rows, CUT), lambda i: (0, jnp.maximum(i - half, 0))),
            pl.BlockSpec((model, CUT), lambda i: (0, i)),
            fixed,
            row,
            fixed,
        ],
        out_specs=(early(rows), fixed, row),
        scratch_shapes=[pltpu.VMEM((rows, model), jnp.float32)],
        compiler_params=roomy(60),
        name="token_back",
    )(grad_preact, following, taps, grad_gate, in_weight, stream, gain[None, :], grad_middle)


ORDERS = ("xyz", "yzx", "zxy")
PIECE = 16


def shares_kernel(
    conv_cols, gate_cols, token_ref, out_cols, middle_ref, left_ref, right_ref, narrow_ref, sum_ref, in_ref, out_ref, made, taken,
    half_a, half_b, half_c, one_a, one_b, one_c, sends, arrivals):
    seq, expert = lax.axis_index("seq"), lax.axis_index("expert")
    core = lax.rem(expert, 2)
    place = {"y": lax.div(seq, 4), "z": lax.rem(seq, 4), "x": lax.div(expert, 2)}
    third = token_ref.shape[1] // len(ORDERS)
    streams = [(L, q) for L in range(len(ORDERS)) for q in range(4)]

    def flip(i):
        return i + 1 - 2 * lax.rem(i, 2)

    def device(**moved):
        at = dict(place, **moved)
        return {"seq": at["y"] * 4 + at["z"], "expert": at["x"] * 2 + at.get("core", core)}

    partners = [device(core=1 - core)]
    for axis in "xyz":
        partners += [device(**{axis: flip(place[axis])}), device(**{axis: 3 - place[axis]})]
    barrier = pltpu.get_barrier_semaphore()
    for partner in partners:
        pl.semaphore_signal(barrier, inc=1, device_id=partner, device_id_type=pl.DeviceIdType.MESH)
    pl.semaphore_wait(barrier, len(partners))

    def send(source, target, partner, stream, number):
        k = streams.index(stream)
        copy = pltpu.make_async_remote_copy(
            src_ref=source, dst_ref=target, send_sem=sends.at[k, number], recv_sem=arrivals.at[k, number],
            device_id=partner, device_id_type=pl.DeviceIdType.MESH,
        )
        copy.start()
        return copy

    def add(target, source, unit):
        def step(i, unused):
            target[i] = target[i] + source[i]
            return unused

        lax.fori_loop(0, unit, step, 0, unroll=min(unit, 8))

    inner = out_cols.shape[1]
    for source, target, base in ((conv_cols, in_ref, 0), (gate_cols, in_ref, inner), (out_cols, out_ref, 0)):

        def turn_over(k, unused, source=source, target=target, base=base):
            spot = pl.ds(pl.multiple_of(k * LANES, LANES), LANES)
            target[pl.ds(pl.multiple_of(base + k * LANES, LANES), LANES), :] = source[:, spot].T
            return unused

        lax.fori_loop(0, source.shape[1] // LANES, turn_over, 0)

    pending = {}
    for L, order in enumerate(ORDERS):
        lanes = pl.ds(L * third, third)
        narrow = narrow_ref[:, lanes].astype(jnp.bfloat16)

        def block(s, unused):
            y, z = lax.div(s, 4), lax.rem(s, 4)
            by_in = jnp.dot(
                in_ref[pl.ds(pl.multiple_of(s * 288, 16), 288), :], token_ref[:, lanes], preferred_element_type=jnp.float32
            ).astype(jnp.bfloat16)
            here = pl.ds(pl.multiple_of(s * 144, 16), 144)
            by_out = jnp.dot(out_ref[here, :], middle_ref[:, lanes], preferred_element_type=jnp.float32)
            left, right = left_ref[here, :], right_ref[here, :]
            for x in range(4):
                at = {"x": x, "y": y, "z": z}
                slot = (at[order[0]] * 4 + at[order[1]]) * 4 + at[order[2]]
                rows = by_in[72 * x : 72 * x + 72]
                more = by_out[36 * x : 36 * x + 36].astype(jnp.bfloat16)
                for q in range(4):
                    made[L, q, slot] = rows[16 * q : 16 * q + 16]
                made[L, 4, slot, 0:8] = rows[64:]
                made[L, 4, slot, 8:16] = more[:8]
                made[L, 5, slot] = more[8:24]
                made[L, 6, slot, 0:12] = more[24:]
                made[L, 6, slot, 12:16] = narrow[8:12]
                made[L, 7, slot, 8:16] = narrow[0:8]
                last = jnp.concatenate([left[36 * x : 36 * x + 36], right[36 * x : 36 * x + 36]], axis=0)
                for part in range(third // LANES):
                    k = 8 * (L * (third // LANES) + part)
                    made[L, 7, slot, 0:8, part * LANES : (part + 1) * LANES] = last[k : k + 8].astype(jnp.bfloat16)
            return unused

        lax.fori_loop(0, 16, block, 0, unroll=2)
        for q in range(4):
            pending[L, q] = [
                send(made.at[L, 4 * (1 - core) + q], taken.at[L, q], device(core=1 - core), (L, q), 0)
            ]

    halves, ones = (half_a, half_b, half_c), (one_a, one_b, one_c)
    holding = {}
    for L, q in streams:
        for copy in pending[L, q]:
            copy.wait()
        add(taken.at[L, q], made.at[L, 4 * core + q], 64)
        holding[L, q] = taken.at[L, q]
        pending[L, q] = start_halves(L, q, 0, holding[L, q], halves, place, flip, device, send)
    for turn in range(3):
        unit = 16 >> (2 * turn)
        for L, q in streams:
            axis = ORDERS[L][turn]
            i = place[axis]
            for copy in pending[L, q]:
                copy.wait()
            other = 3 - i if q < 2 else flip(i)
            got = halves[turn].at[L, q]
            add(got.at[0], holding[L, q].at[pl.ds(i * unit, unit)], unit)
            add(got.at[1], holding[L, q].at[pl.ds(other * unit, unit)], unit)
            partner = device(**{axis: other})
            pending[L, q] = [send(got.at[1], ones[turn].at[L, q], partner, (L, q), 3 + 3 * turn)]
        for L, q in streams:
            for copy in pending[L, q]:
                copy.wait()
            got = ones[turn].at[L, q]
            if turn < 2:
                add(got, halves[turn].at[L, q, 0], unit)
                holding[L, q] = got
                pending[L, q] = start_halves(L, q, turn + 1, got, halves, place, flip, device, send)
            else:
                whole = got[0].astype(jnp.float32) + halves[turn][L, q, 0, 0].astype(jnp.float32)
                sum_ref[4 * core + q, :, L * third : (L + 1) * third] = whole
    here = sum_ref.at[pl.ds(4 * core, 4)]
    send(here, here, device(core=1 - core), (0, 0), 10).wait()


def start_halves(L, q, turn, source, halves, place, flip, device, send):
    axis = ORDERS[L][turn]
    unit = 16 >> (2 * turn)
    i = place[axis]
    partner = flip(i) if q < 2 else 3 - i
    second = 3 - partner if q < 2 else flip(partner)
    target = halves[turn].at[L, q]
    return [
        send(source.at[pl.ds(partner * unit, unit)], target.at[0], device(**{axis: partner}), (L, q), 1 + 3 * turn),
        send(source.at[pl.ds(second * unit, unit)], target.at[1], device(**{axis: partner}), (L, q), 2 + 3 * turn),
    ]


def shares(conv_cols, gate_cols, tokens, out_cols, middle, left, right, narrow):
    width = tokens.shape[1]
    rows, inner = out_cols.shape
    third = width // len(ORDERS)

    def slots(*lead):
        return pltpu.VMEM((len(ORDERS),) + lead + (PIECE, third), jnp.bfloat16)

    return pl.pallas_call(
        shares_kernel,
        out_shape=shaped(8, PIECE, width),
        in_specs=[WHOLE] * 8,
        out_specs=WHOLE,
        scratch_shapes=[pltpu.VMEM((2 * inner, rows), jnp.bfloat16), pltpu.VMEM((inner, rows), jnp.bfloat16)]
        + [slots(8, 64), slots(4, 64)]
        + [slots(4, 2, 16 >> (2 * turn)) for turn in range(3)]
        + [slots(4, 16 >> (2 * turn)) for turn in range(3)]
        + [pltpu.SemaphoreType.DMA((12, 11))] * 2,
        compiler_params=roomy(60, collective_id=2, has_side_effects=True),
        name="shares",
    )(conv_cols, gate_cols, tokens, out_cols, middle, left, right, narrow)


def local(
    tokens,
    expert_index,
    cotangent,
    first_gain,
    in_weight,
    conv_weight,
    conv_bias,
    select_weight,
    step_weight,
    step_bias,
    decay_log,
    skip_gain,
    out_weight,
    second_gain,
    router_weight,
    expert_first,
    expert_second,
):
    bf16, f32 = jnp.bfloat16, jnp.float32
    stream = segmented(tokens[0]).astype(f32)
    routes = segmented(expert_index[0])[:, 0]
    upstream = segmented(cotangent[0]).astype(f32)
    row_count, model_width = stream.shape
    inner = conv_bias.shape[0]
    rank = step_weight.shape[0]
    states = decay_log.shape[0]
    taps = conv_weight.shape[0]
    expert_count = router_weight.shape[1]
    capacity = 2 * row_count // expert_count
    seqs, experts = lax.axis_size("seq"), lax.axis_size("expert")
    reach = (taps - 1) * SEGS
    onward = [(i, i + 1) for i in range(seqs - 1)]
    backward = [(i + 1, i) for i in range(seqs - 1)]

    picks = (routes[:, None] == jnp.arange(expert_count, dtype=jnp.int32)[None, :]).astype(bf16)
    earlier = jnp.arange(row_count)[:, None] > jnp.arange(row_count)[None, :]
    ahead = product(earlier.astype(bf16), picks)
    chosen = picks.astype(f32)
    slot_index = routes * capacity + jnp.sum(ahead * chosen, axis=1).astype(jnp.int32)
    seats = jnp.arange(expert_count * capacity, dtype=jnp.int32)
    placing = (seats[:, None] == slot_index[None, :]).astype(bf16)

    def seated(rows):
        return product(placing, rows).astype(bf16)

    def swapped(rows):
        parts = rows.reshape(expert_count, capacity, -1)
        parts = lax.all_to_all(parts, "expert", split_axis=0, concat_axis=0, tiled=True)
        return parts.reshape(expert_count * capacity, -1)

    def unseated(rows):
        return jnp.einsum("st,sd->td", placing, rows, preferred_element_type=f32)

    upstream_there = swapped(seated(segmented(cotangent[0])))

    first_scale = rms_scale(stream)
    normed_in = (stream * first_scale * first_gain).astype(bf16)
    projected = product(normed_in, in_weight)
    conv_input = projected[:, :inner]
    gate_input = projected[:, inner:]

    ends = conv_input[row_count - reach :].reshape(taps - 1, SEGS, inner)
    arrived = lax.ppermute(ends[:, SEGS - 1], "seq", onward)
    front = jnp.concatenate([arrived[:, None], ends[:, : SEGS - 1]], axis=1).reshape(reach, inner)
    padded = jnp.concatenate([front, conv_input], axis=0)
    preact = conv_bias[None, :]
    for k in range(taps):
        preact = preact + conv_weight[k][None, :] * padded[k * SEGS : k * SEGS + row_count]
    conv_out = jax.nn.silu(preact)
    conv_low = conv_out.astype(bf16)
    select_wide = jnp.pad(select_weight, ((0, 0), (0, LANES - select_weight.shape[1])))
    selection = product(conv_low, select_wide)
    step_low = selection[:, :rank].astype(bf16)
    step_raw = product(step_low, step_weight) + step_bias
    step_size = jax.nn.softplus(step_raw)

    blocks = inner // LANES // PARTS
    log_rows = decay_log.reshape(GRID, GRID, PARTS, blocks, LANES).transpose(2, 0, 1, 3, 4)
    log_rows = jnp.pad(log_rows, ((0, 0), (0, 0), (0, 0), (0, SEGS - blocks), (0, 0)))
    step_size, upstream_there = lax.optimization_barrier((step_size, upstream_there))
    scanned, first = scan_forward(step_size, conv_out, selection, decay_log, log_rows, rank)

    mixer_out = scanned + skip_gain * conv_out
    gated = (mixer_out * jax.nn.silu(gate_input)).astype(bf16)
    middle = stream + product(gated, out_weight)
    second_scale = rms_scale(middle)
    normed_mid = (middle * second_scale * second_gain).astype(bf16)
    router_probs = jax.nn.softmax(product(normed_mid, router_weight), axis=-1)
    gate_value = jnp.sum(router_probs * chosen, axis=1)

    gate_parts = jnp.stack(three_parts(gate_value), axis=1)
    gate_parts = jnp.pad(gate_parts, ((0, 0), (0, LANES - gate_parts.shape[1])))
    leaving = seated(jnp.concatenate([normed_mid, gate_parts], axis=1))
    leaving, upstream_there = lax.optimization_barrier((leaving, upstream_there))
    received = swapped(leaving)
    pull = expert_pull(upstream_there, expert_second[0])
    activated, grad_hidden, value_there, grad_there = expert_layer(
        received, upstream_there, pull, expert_first[0], expert_second[0]
    )
    grad_home = unseated(swapped(grad_there))
    expert_grads = expert_sums(grad_hidden, received, activated, upstream_there, seqs)
    expert_grads, value_there = lax.optimization_barrier((expert_grads, value_there))
    value_home = swapped(value_there)

    grad_gate = jnp.sum(grad_home[:, model_width:], axis=1)
    grad_logits = (grad_gate[:, None] * gate_value[:, None] * (chosen - router_probs)).astype(bf16)
    grad_router = summed_rows(grad_logits, normed_mid)
    grad_mid = across(grad_logits, router_weight) + gate_value[:, None] * grad_home[:, :model_width]
    grad_middle_norm, grad_second_gain = rms_back(middle, second_scale, second_gain, grad_mid)
    grad_middle = upstream + grad_middle_norm
    middle_low = grad_middle.astype(bf16)
    grad_gated = across(middle_low, out_weight)
    grad_mixer = grad_gated * jax.nn.silu(gate_input)
    grad_gate_input = grad_gated * mixer_out * silu_slope(gate_input)

    expert_grads, grad_mixer = lax.optimization_barrier((expert_grads, grad_mixer))
    expert_share = lax.psum_scatter(
        expert_grads.reshape(-1, model_width), "seq", scatter_dimension=0, tiled=True
    ).reshape(2, -1, model_width)

    step_pull = jnp.pad(step_weight, ((0, LANES - rank), (0, 0)))
    step_raw_low, grad_conv_scan, grad_selection, grad_decay_log, grad_step_bias = scan_backward(
        step_size, conv_out, grad_mixer, step_raw, selection, decay_log, log_rows, step_pull, first, rank
    )
    grad_selection, value_home = lax.optimization_barrier((grad_selection, value_home))
    mixed = middle + gate_value[:, None] * unseated(value_home)
    grad_preact, left, right = conv_back(
        grad_selection,
        selection,
        step_raw_low,
        grad_conv_scan,
        grad_mixer,
        conv_out,
        preact,
        padded,
        select_wide,
        skip_gain[None, :],
        grad_decay_log,
        grad_step_bias,
        taps,
    )
    heads = grad_preact[:reach].reshape(taps - 1, SEGS, inner)
    following = lax.ppermute(heads[:, 0], "seq", backward)
    grad_conv_input, grad_tokens, grad_first_gain = token_back(
        grad_preact, following, conv_weight, grad_gate_input.astype(bf16), in_weight, stream, first_gain, grad_middle
    )

    devices = seqs * experts
    each, fewer = inner // devices, model_width // devices
    narrow = jnp.concatenate([grad_first_gain, grad_second_gain[None, :], grad_router, jnp.zeros((6, model_width), f32)])
    grad_conv_input, expert_share = lax.optimization_barrier((grad_conv_input, expert_share))
    sums = shares(grad_conv_input, grad_gate_input.astype(bf16), normed_in, gated, middle_low, left, right, narrow)
    sums = sums.reshape(-1, model_width)
    core = lax.axis_index("expert") % 2
    in_share = lax.dynamic_slice_in_dim(sums, 2 * each * core, 2 * each)
    out_share = lax.dynamic_slice_in_dim(sums, 4 * each + each * core, each)
    small = sums[112:120].reshape(8, -1, LANES).transpose(1, 0, 2).reshape(2, 2 * each, LANES)
    small = lax.dynamic_slice_in_dim(small, each * core, each, axis=1)
    rows_sum = small[0, :, rank + 2 * states :]
    owner = lax.axis_index("seq") * experts + lax.axis_index("expert")
    narrow_sum = jnp.concatenate([sums[120:128], sums[108:110]])
    narrow_sum = lax.dynamic_slice_in_dim(narrow_sum, owner * fewer, fewer, axis=1)
    return (
        in_order(mixed.astype(bf16))[None],
        in_order(grad_tokens)[None],
        narrow_sum[0],
        in_share.T,
        rows_sum[:, states : states + taps].T,
        rows_sum[:, states + taps],
        small[0, :, : rank + 2 * states],
        small[1, :, :rank].T,
        rows_sum[:, states + taps + 1],
        rows_sum[:, :states].T,
        rows_sum[:, states + taps + 2],
        out_share,
        narrow_sum[1],
        narrow_sum[2:].T,
        expert_share[0].T.astype(f32)[None],
        expert_share[1].astype(f32)[None],
    )


def solution(mesh):
    return jax.shard_map(
        local,
        mesh=mesh,
        in_specs=(
            P("expert", "seq", None),
            P("expert", "seq", None),
            P("expert", "seq", None),
            P(),
            P(),
            P(),
            P(),
            P(),
            P(),
            P(),
            P(),
            P(),
            P(),
            P(),
            P(),
            P("expert", None, None),
            P("expert", None, None),
        ),
        out_specs=(
            P("expert", "seq", None),
            P("expert", "seq", None),
            P(("seq", "expert")),
            P(None, ("seq", "expert")),
            P(None, ("seq", "expert")),
            P(("seq", "expert")),
            P(("seq", "expert"), None),
            P(None, ("seq", "expert")),
            P(("seq", "expert")),
            P(None, ("seq", "expert")),
            P(("seq", "expert")),
            P(("seq", "expert"), None),
            P(("seq", "expert")),
            P(("seq", "expert"), None),
            P("expert", None, "seq"),
            P("expert", "seq", None),
        ),
        check_vma=False,
    )
```

time: 439 us -> 385 us (0.88)
  local copies, waits for them, and re-layouts: 72.4 us -> 36.8 us
  matrix products: 46.1 us -> 34 us
  other arithmetic: 29.6 us -> 20.4 us
  waiting for transfers between devices: 7.14 us -> 14.1 us
  Pallas kernels: 235 us -> 230 us
    pallas_call x4 -> x2, Pallas kernels: 60.1 us -> 22.8 us  [the longest x1 11.8 us: token_back(): pl.pallas_call(functools.partial(token_back_kernel, taps.shape[0]), grid=...]
    unnamed x133 -> x110, local copies, waits for them, and re-layouts: 34.7 us -> 13.5 us
    pallas_call x1, Pallas kernels: 13 us -> 26.6 us  [scan_forward(): pl.pallas_call(functools.partial(forward_kernel, column), out_shape=(shap...]
    pallas_call x1, Pallas kernels: 44.5 us -> 57.6 us  [scan_backward(): pl.pallas_call(functools.partial(backward_kernel, column), out_shape=(sha...]
    dot_general x5 -> x2, matrix products: 19.3 us -> 7.92 us  [across(): jnp.einsum('tk,dk->td', left, right, preferred_element_type=jnp.float32)]
    reduce_sum x2 -> x0, other arithmetic: 11.2 us -> none  [the longest x1 8.07 us: local(): grad_conv_bias = jnp.sum(grad_preact, axis=0)]
    concatenate x7 -> x1, local copies, waits for them, and re-layouts: 9.52 us -> 0.08 us  [local(): jnp.concatenate([grad_first_gain, grad_second_gain[None, :], grad_router,...]
    another operation x4 -> x0, local copies, waits for them, and re-layouts: 5.64 us -> none  [local(): jnp.stack([jnp.sum(grad_preact * padded[k * SEGS:k * SEGS + row_count], a...]
  transfers between devices with their start and end apart: 7 -> 7, of which waited for: 1 -> 3; matrix products, arithmetic and copies ran while one was open for 17% -> 10% of each run, Pallas kernels for 28% -> 27%
where the time goes in v3:
time: 385 us; the launch traced here: 380 us
  Pallas kernels  230 us (60%)
  local copies, waits for them, and re-layouts  36.8 us (10%)
  matrix products  34 us (9%)
  starting transfers between devices  29.8 us (8%)
  other arithmetic  20.4 us (5%)
  between operations  15.1 us (4%)
  waiting for transfers between devices  14.1 us (4%)
    pallas_call x1, Pallas kernels, shares(): pl.pallas_call(shares_kernel, out_shape=shaped(8, PIECE, width), in_specs...  77.7 us
    pallas_call x1, Pallas kernels, scan_backward(): pl.pallas_call(functools.partial(backward_kernel, column), out_shape=(sha...  57.6 us
    pallas_call x1, Pallas kernels, scan_forward(): pl.pallas_call(functools.partial(forward_kernel, column), out_shape=(shap...  26.6 us
    all_to_all x4, starting transfers between devices, swapped(): lax.all_to_all(parts, 'expert', split_axis=0, concat_axis=0, tiled=True)  23.9 us
    dot_general x8, matrix products, product(): return jnp.dot(left, right, preferred_element_type=jnp.float32)  22 us
    pallas_call x1, Pallas kernels, expert_layer(): pl.pallas_call(expert_kernel, grid=(hidden // CHUNK,), out_shape=(shaped(...  21.9 us
    pallas_call x1, Pallas kernels, expert_sums(): pl.pallas_call(expert_sums_kernel, grid=(owners // pair,), out_shape=shap...  15.2 us
    unnamed x110, local copies, waits for them, and re-layouts  13.5 us
  transfers between devices with their start and end apart: 7, of which 3 were waited for; matrix products, arithmetic and copies ran while one was open for 10% of the time, Pallas kernels for 27%

profile of v3, /device:TPU:1, one launch (start us, length us, event | category | flops | bytes accessed | tf_op | source)
XLA Modules:
  0.0 380.1 jit_solution(2443614280045476338)
XLA Ops:
  10.7 6.2 %fusion.53 = f32[256,4608]{1,0:T(8,128)S(1)} fusion(bf16[256,1152]{1,0:T(8,128)(2,1)S(1)} %multiply_convert_fusion.3.token_ref, bf16[1152,4608]{1,0:T(8,128)(2,1)} %weight_ref.1), kind=kOutput, calls=%fused_computation.123 | convolution fusion | flops 2717908992 | bytes 15925248 | tf_op jit(solution)/shard_map/dot_general | solution.py:454
  19.1 4.4 %collective-permute-start = (f32[3,2304]{1,0:T(4,128)S(1)}, f32[3,2304]{1,0:T(4,128)S(1)}, u32[]{:S(2)}, u32[]{:S(2)}) collective-permute-start(f32[3,2304]{1,0:T(4,128)S(1)} %bitcast.127), channel_id=1, source_target_pairs={{0,8},{8,16},{16,24},{24,32},{32,40},{40,48},{48,56},{56,64},{64,7... | collective-permute-start | bytes 82952 | tf_op jit(solution)/shard_map/ppermute | solution.py:988
  26.8 5.8 %all-to-all-start = ((bf16[8,64,1152]{2,1,0:T(8,128)(2,1)}), bf16[8,64,1152]{2,1,0:T(8,128)(2,1)}, u32[]{:S(2)}, u32[]{:S(2)}) async-start(bf16[8,64,1152]{2,1,0:T(8,128)(2,1)} %bitcast.12), calls=%async_computation | async-start | bytes 2359296 | tf_op jit(solution)/shard_map/all_to_all | solution.py:973
  32.8 3.3 slice.137
  36.7 5.6 %divide_multiply_fusion = (f32[256,2304]{1,0:T(8,128)S(1)}, f32[256,2304]{1,0:T(8,128)}) fusion(f32[256,2304]{1,0:T(8,128)} %slice.137, f32[2304]{0:T(1024)S(1)} %get-tuple-element.143, f32[2304]{0:T(1024)S(1)} %get-tuple-element.141, f32[2304]{0:T(1024)S(1)} %get-tuple-element.142, f32[24,2304]{1,0:T(8,128)S(1)} %maximum_bitcast_fusion, ...), kind=kLoop, calls=%fused_computation.32 | loop fusion | flops 8847360 | bytes 7345152 | tf_op jit(solution)/shard_map/jit(silu)/mul | solution.py:994
  44.8 4.8 %compare_select_fusion = (f32[256,2304]{1,0:T(8,128)}, f32[256,2304]{1,0:T(8,128)}) fusion(f32[2304]{0:T(1024)S(1)} %copy-done.51, bf16[72,2304]{1,0:T(8,128)(2,1)} %param.25, f32[256,128]{0,1:T(8,128)} %fusion.15), kind=kOutput, calls=%fused_computation | convolution fusion | flops 89063424 | bytes 5096448 | tf_op jit(solution)/shard_map/dot_general | solution.py:454
  51.3 26.6 %scan_forward.1 = (f32[256,2304]{1,0:T(8,128)S(1)}, f32[16,8,2304]{2,1,0:T(8,128)S(1)}) custom-call(f32[256,2304]{1,0:T(8,128)S(1)} %copy-done.2, f32[256,2304]{1,0:T(8,128)S(1)} %get-tuple-element.149.conv_ref, f32[256,128]{1,0:T(8,128)S(1)} %copy.83.sel_ref, f32[16,2304]{1,0:T(8,128)S(1)} %copy-done.7, f32[3,4,4,8,128]{4,3,2,1,0:T(8,128)S(1)} %pad.17.log_rows), custom_call_target="tpu_custom_call" | custom-call | tf_op jit(solution)/shard_map/scan_forward/pallas_call | solution.py:392
  78.0 3.7 multiply_convert_fusion.1.out_cols
  81.8 5.2 %multiply_reduce_fusion.2 = (f32[256]{0:T(256)S(1)}, f32[256,1152]{1,0:T(8,128)S(1)}) fusion(bf16[256,2304]{1,0:T(8,128)(2,1)S(1)} %multiply_convert_fusion.1.out_cols, bf16[2304,1152]{1,0:T(8,128)(2,1)} %param.29, f32[8,32,1152]{2,1,0:T(8,128)S(1)} %copy-done.24), kind=kOutput, calls=%fused_computation.41 | convolution fusion | flops 1359838976 | bytes 8848384 | tf_op jit(solution)/shard_map/dot_general | solution.py:454
  92.8 7.7 %all-to-all-start.1 = ((bf16[8,64,1280]{2,1,0:T(8,128)(2,1)}), bf16[8,64,1280]{2,1,0:T(8,128)(2,1)}, u32[]{:S(2)}, u32[]{:S(2)}) async-start(bf16[8,64,1280]{2,1,0:T(8,128)(2,1)} %bitcast.119), calls=%async_computation.1 | async-start | bytes 2621440 | tf_op jit(solution)/shard_map/all_to_all | solution.py:973
  100.6 8.2 %expert_pull.1.pull_ref = bf16[512,3072]{1,0:T(8,128)(2,1)} custom-call(bf16[512,1152]{1,0:T(8,128)(2,1)} %bitcast.13.up_ref, bf16[3072,1152]{1,0:T(8,128)(2,1)} %bitcast.133), custom_call_target="tpu_custom_call" | custom-call | flops 3623878656 | bytes 10223616 | tf_op jit(solution)/shard_map/expert_pull/pallas_call | solution.py:494
  108.7 9.8 %all-to-all-done.1 = bf16[8,64,1280]{2,1,0:T(8,128)(2,1)} async-done(((bf16[8,64,1280]{2,1,0:T(8,128)(2,1)}), bf16[8,64,1280]{2,1,0:T(8,128)(2,1)}, u32[]{:S(2)}, u32[]{:S(2)}) %all-to-all-start.1) | async-done | bytes 1310752 | tf_op jit(solution)/shard_map/all_to_all | solution.py:973
  118.5 21.9 %expert_layer.1 = (bf16[512,3072]{1,0:T(8,128)(2,1)}, bf16[512,3072]{1,0:T(8,128)(2,1)}, bf16[512,1152]{1,0:T(8,128)(2,1)}, bf16[512,1280]{1,0:T(8,128)(2,1)}) custom-call(bf16[512,1280]{1,0:T(8,128)(2,1)} %bitcast.17.got_ref.received_ref, bf16[512,1152]{1,0:T(8,128)(2,1)} %bitcast.13.up_ref, bf16[512,3072]{1,0:T(8,128)(2,1)} %expert_pull.1.pull_ref, ...), custom_call_target="tpu_custom_call" | custom-call | flops 10871635968 | bytes 20447232 | tf_op jit(solution)/shard_map/expert_layer/pallas_call | solution.py:554
  140.4 5.0 %all-to-all-start.2 = ((bf16[8,64,1280]{2,1,0:T(8,128)(2,1)}), bf16[8,64,1280]{2,1,0:T(8,128)(2,1)}, u32[]{:S(2)}, u32[]{:S(2)}) async-start(bf16[8,64,1280]{2,1,0:T(8,128)(2,1)} %bitcast.118), calls=%async_computation.2 | async-start | bytes 2621440 | tf_op jit(solution)/shard_map/all_to_all | solution.py:973
  145.4 15.2 %expert_sums.1 = bf16[16,2,192,1152]{3,2,1,0:T(8,128)(2,1)} custom-call(bf16[512,3072]{1,0:T(8,128)(2,1)} %get-tuple-element.50.hidden_ref, bf16[512,1280]{1,0:T(8,128)(2,1)} %bitcast.17.got_ref.received_ref, bf16[512,3072]{1,0:T(8,128)(2,1)} %get-tuple-element.51.active_ref, bf16[512,1152]{1,0:T(8,128)(2,1)} %bitcast.13.up_ref), custom_call_target="tpu_custom_call" | custom-call | flops 7247757312 | bytes 20447232 | tf_op jit(solution)/shard_map/expert_sums/pallas_call | solution.py:605
  160.6 2.8 all-to-all-done.2
  168.6 7.2 %multiply_convert_fusion = (bf16[256,2304]{1,0:T(8,128)(2,1)}, f32[256,2304]{1,0:T(8,128)}) fusion(f32[256,4608]{1,0:T(8,128)} %copy-done.21, f32[256,2304]{1,0:T(8,128)S(1)} %copy-done.4, f32[256,2304]{1,0:T(8,128)S(1)} %get-tuple-element.149.conv_ref, f32[2304]{0:T(1024)S(1)} %copy-done.35, bf16[256,1152]{1,0:T(8,128)(2,1)S(1)} %get-tuple-element.147.middle_ref, ...), kind=kOutput, calls=%fused_computation.27 | convolution fusion | flops 1367212032 | bytes 16524288 | tf_op jit(solution)/shard_map/tk,dk->td/dot_general | solution.py:458
  175.8 5.3 %all-to-all-start.3 = ((bf16[8,64,1152]{2,1,0:T(8,128)(2,1)}), bf16[8,64,1152]{2,1,0:T(8,128)(2,1)}, u32[]{:S(2)}, u32[]{:S(2)}) async-start(bf16[8,64,1152]{2,1,0:T(8,128)(2,1)} %bitcast.23), calls=%async_computation.3 | async-start | bytes 2359296 | tf_op jit(solution)/shard_map/all_to_all | solution.py:973
  188.1 2.7 pad_maximum_fusion.padded_ref
  190.8 57.6 %scan_backward.1 = (bf16[256,2304]{1,0:T(8,128)(2,1)S(1)}, f32[256,2304]{1,0:T(8,128)S(1)}, bf16[256,128]{1,0:T(8,128)(2,1)S(1)}, f32[16,2304]{1,0:T(8,128)S(1)}, f32[1,2304]{1,0:T(1,128)S(1)}) custom-call(f32[256,2304]{1,0:T(8,128)} %get-tuple-element.45.step_ref, f32[256,2304]{1,0:T(8,128)} %copy-done.1, f32[256,2304]{1,0:T(8,128)} %get-tuple-element.55.grad_ref.mixer_ref, ...), custom_call_target="tpu_custom_call" | custom-call | tf_op jit(solution)/shard_map/scan_backward/pallas_call | solution.py:407
  252.6 11.0 %conv_back.1 = (f32[256,2304]{1,0:T(8,128)}, f32[2304,128]{1,0:T(8,128)}, f32[2304,128]{1,0:T(8,128)}) custom-call(bf16[256,128]{1,0:T(8,128)(2,1)} %copy-done.12, f32[256,128]{1,0:T(8,128)} %copy-done.6, bf16[256,2304]{1,0:T(8,128)(2,1)} %copy-done.10, f32[256,2304]{1,0:T(8,128)} %copy-done.5, f32[256,2304]{1,0:T(8,128)} %get-tuple-element.55.grad_ref.mixer_ref, ...), custom_call_target="tpu_custom_call" | custom-call | tf_op jit(solution)/shard_map/conv_back/pallas_call | solution.py:665
  271.3 11.8 %token_back.1 = (bf16[256,2304]{1,0:T(8,128)(2,1)}, f32[256,1152]{1,0:T(8,128)}, f32[1,1152]{1,0:T(1,128)}) custom-call(f32[256,2304]{1,0:T(8,128)} %get-tuple-element.65.gpre_ref, f32[3,2304]{1,0:T(4,128)} %copy-done.36, f32[4,2304]{1,0:T(4,128)} %tap_ref.1, bf16[256,2304]{1,0:T(8,128)(2,1)} %get-tuple-element.151.gate_ref.gate_cols, ...), custom_call_target="tpu_custom_call" | custom-call | tf_op jit(solution)/shard_map/token_back/pallas_call | solution.py:740
  283.1 2.5 copy.89
  286.3 77.7 %shares.1 = f32[8,16,1152]{2,1,0:T(8,128)} custom-call(bf16[256,2304]{1,0:T(8,128)(2,1)} %get-tuple-element.69.conv_cols, bf16[256,2304]{1,0:T(8,128)(2,1)} %get-tuple-element.151.gate_ref.gate_cols, bf16[256,1152]{1,0:T(8,128)(2,1)} %copy-done.25, bf16[256,2304]{1,0:T(8,128)(2,1)} %copy-done.22, bf16[256,1152]{1,0:T(8,128)(2,1)} %copy-done.26, ...), custom_call_target="tpu_custom_call" | custom-call | tf_op jit(solution)/shard_map/shares/pallas_call | solution.py:910
  (187 shorter events, 53.0 us)
Async XLA Ops:
  7.2 81.0 %copy-start = (bf16[1152,8]{0,1:T(8,128)(2,1)S(1)}, bf16[1152,8]{0,1:T(8,128)(2,1)}, u32[]{:S(2)}) copy-start(bf16[1152,8]{0,1:T(8,128)(2,1)} %param.31) | copy-start | bytes 55300
  9.6 7.3 %copy-start.23 = (f32[8,32,1152]{2,1,0:T(8,128)}, f32[8,32,1152]{2,1,0:T(8,128)S(1)}, u32[]{:S(2)}) copy-start(f32[8,32,1152]{2,1,0:T(8,128)S(1)} %convert.14) | copy-start | bytes 3538948
  10.6 13.4 %copy-start.50 = (s32[1,256,1]{1,2,0:T(1,128)S(1)}, s32[1,256,1]{1,2,0:T(1,128)}, u32[]{:S(2)}) copy-start(s32[1,256,1]{1,2,0:T(1,128)} %param.18) | copy-start | bytes 3076
  10.6 14.5 %copy-start.27 = (bf16[1,256,1152]{2,1,0:T(8,128)(2,1)S(1)}, bf16[1,256,1152]{2,1,0:T(8,128)(2,1)}, u32[]{:S(2)}) copy-start(bf16[1,256,1152]{2,1,0:T(8,128)(2,1)} %param.19) | copy-start | bytes 1769476
  19.0 13.6 %copy-start.33 = (f32[4,2304]{1,0:T(4,128)S(1)}, f32[4,2304]{1,0:T(4,128)}, u32[]{:S(2)}) copy-start(f32[4,2304]{1,0:T(4,128)} %tap_ref.1) | copy-start | bytes 110596
  19.1 17.3 %collective-permute-start = (f32[3,2304]{1,0:T(4,128)S(1)}, f32[3,2304]{1,0:T(4,128)S(1)}, u32[]{:S(2)}, u32[]{:S(2)}) collective-permute-start(f32[3,2304]{1,0:T(4,128)S(1)} %bitcast.127), channel_id=1, source_target_pairs={{0,8},{8,16},{16,24},{24,32},{32,40},{40,48},{48,56},{56,64},{64,7... | collective-permute-start | bytes 82952 | tf_op jit(solution)/shard_map/ppermute | solution.py:988
  24.9 63.6 %copy-start.38 = (s32[256]{0:T(256)}, s32[256]{0:T(256)S(1)}, u32[]{:S(2)}) copy-start(s32[256]{0:T(256)S(1)} %squeeze_reshape.3) | copy-start | bytes 3076
  25.2 10.9 %copy-start.40 = (s32[256]{0:T(256)}, s32[256]{0:T(256)S(1)}, u32[]{:S(2)}) copy-start(s32[256]{0:T(256)S(1)} %convert_add_fusion) | copy-start | bytes 3076
  26.8 22.8 %all-to-all-start = ((bf16[8,64,1152]{2,1,0:T(8,128)(2,1)}), bf16[8,64,1152]{2,1,0:T(8,128)(2,1)}, u32[]{:S(2)}, u32[]{:S(2)}) async-start(bf16[8,64,1152]{2,1,0:T(8,128)(2,1)} %bitcast.12), calls=%async_computation | async-start | bytes 2359296 | tf_op jit(solution)/shard_map/all_to_all | solution.py:973
  42.4 125.5 %copy-start.1 = (f32[256,2304]{1,0:T(8,128)}, f32[256,2304]{1,0:T(8,128)S(1)}, u32[]{:S(2)}) copy-start(f32[256,2304]{1,0:T(8,128)S(1)} %get-tuple-element.149.conv_ref) | copy-start | bytes 7077892
  44.8 145.9 %copy-start.6 = (f32[256,128]{1,0:T(8,128)}, f32[256,128]{1,0:T(8,128)S(1)}, u32[]{:S(2)}) copy-start(f32[256,128]{1,0:T(8,128)S(1)} %copy.83.sel_ref) | copy-start | bytes 393220
  51.3 26.7 %copy-start.35 = (f32[2304]{0:T(1024)S(1)}, f32[2304]{0:T(1024)}, u32[]{:S(2)}) copy-start(f32[2304]{0:T(1024)} %param.28) | copy-start | bytes 27652
  92.8 25.7 %all-to-all-start.1 = ((bf16[8,64,1280]{2,1,0:T(8,128)(2,1)}), bf16[8,64,1280]{2,1,0:T(8,128)(2,1)}, u32[]{:S(2)}, u32[]{:S(2)}) async-start(bf16[8,64,1280]{2,1,0:T(8,128)(2,1)} %bitcast.119), calls=%async_computation.1 | async-start | bytes 2621440 | tf_op jit(solution)/shard_map/all_to_all | solution.py:973
  140.4 23.1 %all-to-all-start.2 = ((bf16[8,64,1280]{2,1,0:T(8,128)(2,1)}), bf16[8,64,1280]{2,1,0:T(8,128)(2,1)}, u32[]{:S(2)}, u32[]{:S(2)}) async-start(bf16[8,64,1280]{2,1,0:T(8,128)(2,1)} %bitcast.118), calls=%async_computation.2 | async-start | bytes 2621440 | tf_op jit(solution)/shard_map/all_to_all | solution.py:973
  145.4 140.9 %reduce-scatter.2.cloned.1.call-start = ((), (), s32[]{:S(2)}) async-start(), calls=%async_computation.5 | async-start | bytes 15040512 | tf_op jit(solution)/shard_map/reduce_scatter | solution.py:1042
  145.4 18.0 %copy-start.41 = (s32[256]{0:T(256)S(1)}, s32[256]{0:T(256)}, u32[]{:S(2)}) copy-start(s32[256]{0:T(256)} %copy-done.40) | copy-start | bytes 3076
  167.9 7.9 %copy-start.26 = (bf16[256,1152]{1,0:T(8,128)(2,1)}, bf16[256,1152]{1,0:T(8,128)(2,1)S(1)}, u32[]{:S(2)}) copy-start(bf16[256,1152]{1,0:T(8,128)(2,1)S(1)} %get-tuple-element.147.middle_ref) | copy-start | bytes 1769476
  175.8 76.2 %all-to-all-start.3 = ((bf16[8,64,1152]{2,1,0:T(8,128)(2,1)}), bf16[8,64,1152]{2,1,0:T(8,128)(2,1)}, u32[]{:S(2)}, u32[]{:S(2)}) async-start(bf16[8,64,1152]{2,1,0:T(8,128)(2,1)} %bitcast.23), calls=%async_computation.3 | async-start | bytes 2359296 | tf_op jit(solution)/shard_map/all_to_all | solution.py:973
  181.1 6.9 %copy-start.14 = (f32[256,2304]{1,0:T(8,128)S(1)}, f32[256,2304]{1,0:T(8,128)}, u32[]{:S(2)}) copy-start(f32[256,2304]{1,0:T(8,128)} %slice.137) | copy-start | bytes 7077892
  252.6 13.5 %copy-start.19 = (bf16[256,1152]{1,0:T(8,128)(2,1)S(1)}, bf16[256,1152]{1,0:T(8,128)(2,1)}, u32[]{:S(2)}) copy-start(bf16[256,1152]{1,0:T(8,128)(2,1)} %copy-done.18) | copy-start | bytes 1769476
  252.6 13.7 %copy-start.17 = (f32[256,1152]{1,0:T(8,128)S(1)}, f32[256,1152]{1,0:T(8,128)}, u32[]{:S(2)}) copy-start(f32[256,1152]{1,0:T(8,128)} %copy-done.15) | copy-start | bytes 3538948
  264.6 6.1 %collective-permute-start.1 = (f32[3,2304]{1,0:T(4,128)S(1)}, f32[3,2304]{1,0:T(4,128)S(1)}, u32[]{:S(2)}, u32[]{:S(2)}) collective-permute-start(f32[3,2304]{1,0:T(4,128)S(1)} %bitcast.129), channel_id=1, source_target_pairs={{8,0},{16,8},{24,16},{32,24},{40,32},{48,40},{56,48},{64,56},{72,6... | collective-permute-start | bytes 82952 | tf_op jit(solution)/shard_map/ppermute | solution.py:1068
  286.3 82.1 %copy-start.31 = (bf16[384,1152]{1,0:T(8,128)(2,1)S(1)}, bf16[384,1152]{1,0:T(8,128)(2,1)}, u32[]{:S(2)}) copy-start(bf16[384,1152]{1,0:T(8,128)(2,1)} %reduce-scatter.2.cloned.1.call-done) | copy-start | bytes 2654212
  364.1 7.6 %copy-start.30 = (f32[8,16,1152]{2,1,0:T(8,128)S(1)}, f32[8,16,1152]{2,1,0:T(8,128)}, u32[]{:S(2)}) copy-start(f32[8,16,1152]{2,1,0:T(8,128)} %shares.1) | copy-start | bytes 1769476
  (35 other events, 97.9 us)
Sparse Core Ops, SparseCore 0:
  176.0 101.0 reduce-scatter.1
